TPU v7x, 32 devices: a whole 2x2x4 slice. The times are simulated.
32 devices in a mesh: fsdp: 4 (over x, core), ctx: 4 (over z), tp: 2 (over y).
Axes of the slice: x: 2, y: 2, z: 4, core: 2. Of those that a mesh axis runs over, the one named last changes fastest.
Arguments:
- images: bfloat16 [8, 2304, 768], P('fsdp', 'ctx'), may hold values from -6 to 6
- norm1_gain: bfloat16 [768], replicated, may hold values from 0.5 to 1.5
- norm1_bias: bfloat16 [768], replicated, may hold values from -1.25 to 1.25
- qkv_weight: bfloat16 [3, 768, 768], P(None, ('fsdp', 'ctx'), 'tp'), may hold values from -0.21875 to 0.21875
- qv_bias: bfloat16 [2, 768], P(None, 'tp'), may hold values from -1.25 to 1.25
- rel_pos_h: bfloat16 [95, 64], replicated, may hold values from -0.75 to 0.75
- rel_pos_w: bfloat16 [95, 64], replicated, may hold values from -0.75 to 0.75
- proj_weight: bfloat16 [768, 768], P(('fsdp', 'ctx'), 'tp'), may hold values from -2.5 to 2.5
- proj_bias: bfloat16 [768], replicated, may hold values from -1.25 to 1.25
- norm2_gain: bfloat16 [768], replicated, may hold values from 0.5 to 1.5
- norm2_bias: bfloat16 [768], replicated, may hold values from -1.25 to 1.25
- up_weight: bfloat16 [768, 3072], P(('fsdp', 'ctx'), 'tp'), may hold values from -0.21875 to 0.21875
- up_bias: bfloat16 [3072], P('tp'), may hold values from -1.75 to 1.75
- down_weight: bfloat16 [768, 3072], P(('fsdp', 'ctx'), 'tp'), may hold values from -0.109375 to 0.109375
- down_bias: bfloat16 [768], replicated, may hold values from -1.25 to 1.25
- out_cotangent: bfloat16 [8, 2304, 768], P('fsdp', 'ctx'), may hold values from -8 to 8
Outputs:
- block_out: bfloat16 [8, 2304, 768], P('fsdp', 'ctx')
- images_grad: bfloat16 [8, 2304, 768], P('fsdp', 'ctx')
- norm1_gain_grad: float32 [768], replicated
- norm1_bias_grad: float32 [768], replicated
- qkv_weight_grad: float32 [3, 768, 768], P(None, ('fsdp', 'ctx'), 'tp')
- qv_bias_grad: float32 [2, 768], P(None, 'tp')
- rel_pos_h_grad: float32 [95, 64], replicated
- rel_pos_w_grad: float32 [95, 64], replicated
- proj_weight_grad: float32 [768, 768], P(('fsdp', 'ctx'), 'tp')
- proj_bias_grad: float32 [768], replicated
- norm2_gain_grad: float32 [768], replicated
- norm2_bias_grad: float32 [768], replicated
- up_weight_grad: float32 [768, 3072], P(('fsdp', 'ctx'), 'tp')
- up_bias_grad: float32 [3072], P('tp')
- down_weight_grad: float32 [768, 3072], P(('fsdp', 'ctx'), 'tp')
- down_bias_grad: float32 [768], replicated
All inputs are finite; a program needn't handle non-finite values.
Results may differ from a plain program's by a relative error of at most 0.018.
Values may be sent and summed in bfloat16 or wider, within the bound.
No kernel may reach another device: no remote copies, remote signals or barrier semaphores. Data moves between devices by JAX's collectives and lax.ppermute only.
A program may use at most 256 MiB of HBM per device.

v0:
```python
from functools import partial

import jax
import jax.numpy as jnp
from jax import lax
from jax.sharding import PartitionSpec as P

G = 48
HD = 64


eps = 1e-06
highest = lax.Precision.HIGHEST


def layer_norm(values, gain_vec, shift_vec):
    centered = values - jnp.mean(values, axis=-1, keepdims=True)
    inverse = lax.rsqrt(jnp.mean(centered * centered, axis=-1, keepdims=True) + eps)
    standard = centered * inverse
    return (standard * gain_vec + shift_vec, standard, inverse)


def norm_back(upstream, standard, inverse, gain_vec):
    scaled = upstream * gain_vec
    mean_term = jnp.mean(scaled, axis=-1, keepdims=True)
    proj_term = jnp.mean(scaled * standard, axis=-1, keepdims=True)
    return inverse * (scaled - mean_term - standard * proj_term)


def exact_gelu(values):
    return jax.nn.gelu(values, approximate=False)


def table_rows(pos_table, first_row, num_rows):
    table_len = pos_table.shape[0]
    grid_side = (table_len + 1) // 2
    query_row = first_row + lax.broadcasted_iota(jnp.int32, (num_rows, grid_side, table_len), 0)
    key_row = lax.broadcasted_iota(jnp.int32, (num_rows, grid_side, table_len), 1)
    entry_idx = lax.broadcasted_iota(jnp.int32, (num_rows, grid_side, table_len), 2)
    chooser = (query_row - key_row + grid_side - 1 == entry_idx).astype(jnp.float32)
    chooser = chooser.reshape(num_rows * grid_side, table_len)
    picked = jnp.dot(chooser, pos_table, precision=highest)
    return (picked.reshape(num_rows, grid_side, -1), chooser)


def rel_terms(query_f, row_first, rel_h, rel_w):
    grid_rows = query_f.shape[0] // G
    head_count = query_f.shape[1]
    near_h, pick_h = table_rows(rel_h, row_first, grid_rows)
    near_w, pick_w = table_rows(rel_w, 0, G)
    shaped = query_f.reshape(grid_rows, G, head_count, query_f.shape[2])
    term_h = jnp.einsum("awhc,akc->awhk", shaped, near_h, precision=highest)
    term_w = jnp.einsum("awhc,wkc->awhk", shaped, near_w, precision=highest)
    return (
        term_h.reshape(-1, head_count, G),
        term_w.reshape(-1, head_count, G),
        near_h,
        near_w,
        pick_h,
        pick_w,
    )


def piece_scores(query, key_h, term_h, term_w, factor):
    num_keys = key_h.shape[0]
    products = jnp.einsum("rhc,nhc->rhn", query, key_h, preferred_element_type=jnp.float32)
    position = (term_h[..., :, None] + term_w[..., None, :]).reshape(
        term_h.shape[0], term_h.shape[1], num_keys
    )
    return products * factor + position


def attend_step(running, pieces, offset, query, term_h, term_w, factor):
    run_max, run_sum, accumulated = running
    key_piece, value_piece = pieces
    num_keys = key_piece.shape[0]
    head_count = query.shape[1]
    key_h = key_piece.reshape(num_keys, head_count, -1)
    value_h = value_piece.reshape(num_keys, head_count, -1)
    scores = piece_scores(query, key_h, term_h, term_w, factor)
    new_max = jnp.maximum(run_max, jnp.max(scores, axis=-1))
    weights_p = jnp.exp(scores - new_max[..., None])
    run_sum = jnp.sum(weights_p, axis=-1)
    accumulated = jnp.einsum(
        "rhn,nhc->rhc", weights_p.astype(jnp.bfloat16), value_h, preferred_element_type=jnp.float32
    )
    return (new_max, run_sum, accumulated)


def grad_step(running, pieces, offset, query, out_grad, log_total, row_dot, term_h, term_w, factor):
    key_piece, value_piece = pieces
    num_keys = key_piece.shape[0]
    num_rows, head_count, head_size = query.shape
    key_h = key_piece.reshape(num_keys, head_count, head_size)
    value_h = value_piece.reshape(num_keys, head_count, head_size)
    scores = piece_scores(query, key_h, term_h, term_w, factor)
    weights_p = jnp.exp(scores - log_total[..., None])
    prob_grad = jnp.einsum("rhc,nhc->rhn", out_grad, value_h, preferred_element_type=jnp.float32)
    score_grad = (weights_p * (prob_grad - row_dot[..., None])).astype(jnp.bfloat16)
    query_acc = jnp.einsum("rhn,nhc->rhc", score_grad, key_h, preferred_element_type=jnp.float32)
    key_grad = (
        jnp.einsum("rhn,rhc->nhc", score_grad, query, preferred_element_type=jnp.float32) * factor
    )
    value_grad = jnp.einsum(
        "rhn,rhc->nhc", weights_p.astype(jnp.bfloat16), out_grad, preferred_element_type=jnp.float32
    )
    joined = jnp.concatenate(
        [key_grad.reshape(num_keys, -1), value_grad.reshape(num_keys, -1)], axis=1
    )
    grid_grad = score_grad.reshape(num_rows, head_count, num_keys // G, G)
    part_h = jnp.sum(grid_grad, axis=-1, dtype=jnp.float32)
    grad_w = jnp.sum(grid_grad, axis=-2, dtype=jnp.float32)
    return (query_acc, joined, part_h, grad_w)


def tensor_total(partial_sum):
    return lax.psum(partial_sum.astype(jnp.bfloat16), "tp").astype(jnp.float32)


def contract_last(left_mat, right_mat):
    return lax.dot_general(
        left_mat, right_mat, (((1,), (1,)), ((), ())), preferred_element_type=jnp.float32
    )


def micro_step(weights_full, picture, cotangent, params):
    (
        gain_one,
        shift_one,
        qv_shift,
        rel_h,
        rel_w,
        proj_shift,
        gain_two,
        shift_two,
        up_shift,
        down_shift,
    ) = params
    qkv_full, proj_full, up_full, down_full = weights_full
    rows_dev = picture.shape[0]
    half_width = qkv_full.shape[2]
    head_count = half_width // HD
    grid_rows = rows_dev // G
    row_first = lax.axis_index("ctx") * grid_rows
    factor = HD ** (-0.5)
    source = picture.astype(jnp.float32)
    normed_f, standard_one, inverse_one = layer_norm(source, gain_one, shift_one)
    normed = normed_f.astype(jnp.bfloat16)
    projected = jnp.einsum("rd,jde->jre", normed, qkv_full, preferred_element_type=jnp.float32)
    query_flat = (projected[0] + qv_shift[0]).astype(jnp.bfloat16)
    key_flat = projected[1].astype(jnp.bfloat16)
    value_flat = (projected[2] + qv_shift[1]).astype(jnp.bfloat16)
    query = query_flat.reshape(rows_dev, head_count, HD)
    query_f = query.astype(jnp.float32)
    term_h, term_w, near_h, near_w, pick_h, pick_w = rel_terms(query_f, row_first, rel_h, rel_w)
    start_state = (
        jnp.full((rows_dev, head_count), -1e30, jnp.float32),
        jnp.zeros((rows_dev, head_count), jnp.float32),
        jnp.zeros((rows_dev, head_count, HD), jnp.float32),
    )
    forward_fn = partial(attend_step, query=query, term_h=term_h, term_w=term_w, factor=factor)
    run_max, run_sum, accumulated = forward_fn(
        start_state,
        (
            lax.all_gather(key_flat, "ctx", axis=0, tiled=True),
            lax.all_gather(value_flat, "ctx", axis=0, tiled=True),
        ),
        jnp.int32(0),
    )
    attended = accumulated / run_sum[..., None]
    log_total = run_max + jnp.log(run_sum)
    mixed = attended.reshape(rows_dev, half_width).astype(jnp.bfloat16)
    middle = source + tensor_total(contract_last(mixed, proj_full)) + proj_shift
    normed2_f, standard_two, inverse_two = layer_norm(middle, gain_two, shift_two)
    normed2 = normed2_f.astype(jnp.bfloat16)
    hidden = jnp.dot(normed2, up_full, preferred_element_type=jnp.float32) + up_shift
    active, gelu_back = jax.vjp(exact_gelu, hidden)
    active_low = active.astype(jnp.bfloat16)
    result = (middle + tensor_total(contract_last(active_low, down_full)) + down_shift).astype(
        jnp.bfloat16
    )
    top_f = cotangent.astype(jnp.float32)
    down_grad = jnp.einsum("rd,rf->df", cotangent, active_low, preferred_element_type=jnp.float32)
    down_shift_grad = jnp.sum(top_f, axis=0)
    active_grad = jnp.dot(cotangent, down_full, preferred_element_type=jnp.float32)
    hidden_grad = gelu_back(active_grad)[0].astype(jnp.bfloat16)
    up_grad = jnp.einsum("rd,rf->df", normed2, hidden_grad, preferred_element_type=jnp.float32)
    up_shift_grad = jnp.sum(hidden_grad, axis=0, dtype=jnp.float32)
    normed2_grad = lax.psum(contract_last(hidden_grad, up_full).astype(jnp.bfloat16), "tp").astype(
        jnp.float32
    )
    middle_grad = top_f + norm_back(normed2_grad, standard_two, inverse_two, gain_two)
    gain_two_grad = jnp.sum(normed2_grad * standard_two, axis=0)
    shift_two_grad = jnp.sum(normed2_grad, axis=0)
    branch_grad = middle_grad.astype(jnp.bfloat16)
    proj_grad = jnp.einsum("rd,re->de", branch_grad, mixed, preferred_element_type=jnp.float32)
    proj_shift_grad = jnp.sum(branch_grad, axis=0, dtype=jnp.float32)
    mixed_grad = (
        jnp.dot(branch_grad, proj_full, preferred_element_type=jnp.float32)
        .astype(jnp.bfloat16)
        .reshape(rows_dev, head_count, HD)
    )
    row_dot = jnp.sum(mixed_grad.astype(jnp.float32) * attended, axis=-1)
    ctx_count = lax.axis_size("ctx")
    start_back = (
        jnp.zeros((rows_dev, head_count, HD), jnp.float32),
        jnp.zeros((rows_dev * ctx_count, 2 * half_width), jnp.float32),
        jnp.zeros((rows_dev, head_count, G), jnp.float32),
        jnp.zeros((rows_dev, head_count, G), jnp.float32),
    )
    back_fn = partial(
        grad_step,
        query=query,
        out_grad=mixed_grad,
        log_total=log_total,
        row_dot=row_dot,
        term_h=term_h,
        term_w=term_w,
        factor=factor,
    )
    query_acc, key_value_acc, grad_h, grad_w = back_fn(
        start_back,
        (
            lax.all_gather(key_flat, "ctx", axis=0, tiled=True),
            lax.all_gather(value_flat, "ctx", axis=0, tiled=True),
        ),
        jnp.int32(0),
    )
    key_value_mine = lax.psum_scatter(
        key_value_acc.astype(jnp.bfloat16), "ctx", scatter_dimension=0, tiled=True
    ).astype(jnp.float32)
    grid_h = grad_h.reshape(grid_rows, G, head_count, G)
    grid_w = grad_w.reshape(grid_rows, G, head_count, G)
    shaped_q = query_f.reshape(grid_rows, G, head_count, HD)
    rel_query = jnp.einsum("awhk,akc->awhc", grid_h, near_h, precision=highest) + jnp.einsum(
        "awhk,wkc->awhc", grid_w, near_w, precision=highest
    )
    query_grad = (
        (query_acc * factor + rel_query.reshape(rows_dev, head_count, HD))
        .reshape(rows_dev, half_width)
        .astype(jnp.bfloat16)
    )
    key_grad = key_value_mine[:, :half_width].astype(jnp.bfloat16)
    value_grad = key_value_mine[:, half_width:].astype(jnp.bfloat16)
    table_h_part = jnp.dot(
        pick_h.T,
        jnp.einsum("awhk,awhc->akc", grid_h, shaped_q, precision=highest).reshape(-1, HD),
        precision=highest,
    )
    table_w_part = jnp.dot(
        pick_w.T,
        jnp.einsum("awhk,awhc->wkc", grid_w, shaped_q, precision=highest).reshape(-1, HD),
        precision=highest,
    )
    stacked = jnp.stack([query_grad, key_grad, value_grad])
    qkv_grad = jnp.einsum("rd,jre->jde", normed, stacked, preferred_element_type=jnp.float32)
    qv_shift_grad = jnp.stack(
        [
            jnp.sum(query_grad, axis=0, dtype=jnp.float32),
            jnp.sum(value_grad, axis=0, dtype=jnp.float32),
        ]
    )
    normed_part = jnp.einsum("jre,jde->rd", stacked, qkv_full, preferred_element_type=jnp.float32)
    normed_grad, table_h_grad, table_w_grad = (
        lax.psum(normed_part.astype(jnp.bfloat16), "tp").astype(jnp.float32),
        lax.psum(table_h_part.astype(jnp.bfloat16), "tp").astype(jnp.float32),
        lax.psum(table_w_part.astype(jnp.bfloat16), "tp").astype(jnp.float32),
    )
    input_grad = (middle_grad + norm_back(normed_grad, standard_one, inverse_one, gain_one)).astype(
        jnp.bfloat16
    )
    gain_one_grad = jnp.sum(normed_grad * standard_one, axis=0)
    shift_one_grad = jnp.sum(normed_grad, axis=0)
    big_grads = (qkv_grad, proj_grad, up_grad, down_grad)
    small_grads = (
        gain_one_grad,
        shift_one_grad,
        qv_shift_grad,
        table_h_grad,
        table_w_grad,
        proj_shift_grad,
        gain_two_grad,
        shift_two_grad,
        up_shift_grad,
        down_shift_grad,
    )
    return (result, input_grad, big_grads, small_grads)


def add_trees(first_tree, second_tree):
    return jax.tree.map(lambda first_v, second_v: first_v + second_v, first_tree, second_tree)


def zeros_like_tree(tree):
    return jax.tree.map(lambda member: jnp.zeros(member.shape, jnp.float32), tree)


def local(
    images,
    norm1_gain,
    norm1_bias,
    qkv_weight,
    qv_bias,
    rel_pos_h,
    rel_pos_w,
    proj_weight,
    proj_bias,
    norm2_gain,
    norm2_bias,
    up_weight,
    up_bias,
    down_weight,
    down_bias,
    out_cotangent,
):
    params = tuple(
        (
            member.astype(jnp.float32)
            for member in (
                norm1_gain,
                norm1_bias,
                qv_bias,
                rel_pos_h,
                rel_pos_w,
                proj_bias,
                norm2_gain,
                norm2_bias,
                up_bias,
                down_bias,
            )
        )
    )
    small_start = zeros_like_tree(params)

    def per_batch(totals, pair):
        weights_full = (
            lax.all_gather(qkv_weight, ("fsdp", "ctx"), axis=1, tiled=True),
            lax.all_gather(proj_weight, ("fsdp", "ctx"), axis=0, tiled=True),
            lax.all_gather(up_weight, ("fsdp", "ctx"), axis=0, tiled=True),
            lax.all_gather(down_weight, ("fsdp", "ctx"), axis=0, tiled=True),
        )
        result, input_grad, big_grads, small_grads = micro_step(
            weights_full, pair[0], pair[1], params
        )
        shards = (
            lax.psum_scatter(big_grads[0], ("fsdp", "ctx"), scatter_dimension=1, tiled=True),
            lax.psum_scatter(big_grads[1], ("fsdp", "ctx"), scatter_dimension=0, tiled=True),
            lax.psum_scatter(big_grads[2], ("fsdp", "ctx"), scatter_dimension=0, tiled=True),
            lax.psum_scatter(big_grads[3], ("fsdp", "ctx"), scatter_dimension=0, tiled=True),
        )
        return (add_trees(totals, (shards, small_grads)), (result, input_grad))

    shard_start = zeros_like_tree((qkv_weight, proj_weight, up_weight, down_weight))
    (shard_totals, small_totals), (outputs, input_grads) = lax.scan(
        per_batch, (shard_start, small_start), (images, out_cotangent)
    )
    small_final = lax.psum(small_totals, ("fsdp", "ctx"))
    return (
        outputs,
        input_grads,
        small_final[0],
        small_final[1],
        shard_totals[0],
        small_final[2],
        small_final[3],
        small_final[4],
        shard_totals[1],
        small_final[5],
        small_final[6],
        small_final[7],
        shard_totals[2],
        small_final[8],
        shard_totals[3],
        small_final[9],
    )


def solution(mesh):
    placed = (
        P("fsdp", "ctx", None),
        P(),
        P(),
        P(None, ("fsdp", "ctx"), "tp"),
        P(None, "tp"),
        P(),
        P(),
        P(("fsdp", "ctx"), "tp"),
        P(),
        P(),
        P(),
        P(("fsdp", "ctx"), "tp"),
        P("tp"),
        P(("fsdp", "ctx"), "tp"),
        P(),
        P("fsdp", "ctx", None),
    )
    return jax.shard_map(
        local,
        mesh=mesh,
        in_specs=placed,
        out_specs=(
            P("fsdp", "ctx", None),
            P("fsdp", "ctx", None),
            P(),
            P(),
            P(None, ("fsdp", "ctx"), "tp"),
            P(None, "tp"),
            P(),
            P(),
            P(("fsdp", "ctx"), "tp"),
            P(),
            P(),
            P(),
            P(("fsdp", "ctx"), "tp"),
            P("tp"),
            P(("fsdp", "ctx"), "tp"),
            P(),
        ),
        check_vma=False,
    )
```

profile of v0, /device:TPU:8, one launch (start us, length us, event | category | flops | bytes accessed | tf_op | source)
XLA Modules:
  0.0 1931.3 jit_solution(16435455338423944920)
XLA Ops:
  19.9 1793.9 %while.46 = (s32[]{:T(128)}, f32[3,48,384]{2,0,1:T(4,128)}, f32[48,384]{1,0:T(8,128)}, f32[48,1536]{1,0:T(8,128)}, f32[48,1536]{1,0:T(8,128)}, /*index=5*/f32[76...) while((s32[]{:T(128)}, f32[3,48,384]{2,0,1:T(4,128)}, ...), condition=%wide.region_34.35_spmd.clone, body=%wide.region_0.34_spmd.clone.sunk | while | flops 19802564608 | bytes 812366784 | solution.py:354
  27.8 39.4 %all_gather.72 = bf16[768,384]{1,0:T(8,128)(2,1)S(1)} all-gather(bf16[48,384]{1,0:T(8,128)(2,1)S(1)} %copy-done.27), channel_id=1, replica_groups=mesh['fsdp'=4,'ctx'=4,'tp'=2] {'fsdp','ctx'}, dimensions={0}, use_global_device_ids=true | all-gather | bytes 626688 | tf_op jit(solution)/shard_map/while/body/eval_jaxpr/all_gather | solution.py:338
  97.2 12.8 broadcast_add_fusion.2
  110.0 35.3 %copy.163 = f32[576,6,2304]{2,0,1:T(8,128)} copy(f32[576,6,2304]{0,2,1:T(8,128)} %bitcast.362) | data formatting | bytes 63700992 | tf_op jit(solution)/shard_map/while/body/eval_jaxpr/add | solution.py:67
  151.6 25.0 %fusion.255 = (f32[576,6]{0,1:T(8,128)S(1)}, f32[576,6,2304]{2,0,1:T(8,128)}) fusion(f32[576,6,2304]{2,0,1:T(8,128)} %copy.163, bf16[2304,6,64]{0,2,1:T(8,128)(2,1)} %bitcast.363, f32[576,6,64]{0,2,1:T(8,128)} %bitcast.367, f32[6,64]{1,0:T(8,128)S(1)} %add.929), kind=kOutput, calls=%fused_computation.184.clone.1 | convolution fusion | flops 1043542656 | bytes 66370560 | tf_op jit(solution)/shard_map/while/body/eval_jaxpr/rhc,nhc->rhn/dot_general | solution.py:66
  176.6 14.3 fusion.256
  194.8 14.1 fusion.258
  212.6 36.0 %all-reduce.18.cloned.1.call-done = bf16[576,768]{1,0:T(8,128)(2,1)} async-done(((bf16[576,768]{1,0:T(8,128)(2,1)}), bf16[576,768]{1,0:T(8,128)(2,1)}) %all-reduce.18.cloned.1.call-update) | async-done | bytes 884752 | tf_op jit(solution)/shard_map/while/body/eval_jaxpr/psum | solution.py:117
  250.8 41.7 %all-gather.10.cloned.1.call-done = bf16[768,1536]{1,0:T(8,128)(2,1)} async-done(((bf16[48,1536]{1,0:T(8,128)(2,1)}), bf16[768,1536]{1,0:T(8,128)(2,1)}) %all-gather.10.cloned.1.call-update) | async-done | bytes 2359312 | tf_op jit(solution)/shard_map/while/body/eval_jaxpr/all_gather | solution.py:339
  292.5 12.4 multiply_convert_fusion.2
  304.9 30.8 %all-gather.18.cloned.1.call-done = bf16[768,1536]{1,0:T(8,128)(2,1)} async-done(((bf16[48,1536]{1,0:T(8,128)(2,1)}), bf16[768,1536]{1,0:T(8,128)(2,1)}) %all-gather.18.cloned.1.call-update) | async-done | bytes 2359312 | tf_op jit(solution)/shard_map/while/body/eval_jaxpr/all_gather | solution.py:340
  335.7 6.6 convert_reduce_fusion.14
  346.7 35.3 %all-reduce.20.cloned.1.call-done = bf16[576,768]{1,0:T(8,128)(2,1)} async-done(((bf16[576,768]{1,0:T(8,128)(2,1)}), bf16[576,768]{1,0:T(8,128)(2,1)}) %all-reduce.20.cloned.1.call-update) | async-done | bytes 884752 | tf_op jit(solution)/shard_map/while/body/eval_jaxpr/psum | solution.py:189
  390.6 13.8 fusion.261
  409.5 19.7 %fusion.262 = bf16[576,6,2304]{2,0,1:T(8,128)(2,1)} fusion(f32[576,6,2304]{2,0,1:T(8,128)} %get-tuple-element.1290, bf16[2304,6,64]{0,2,1:T(8,128)(2,1)} %bitcast.366, bf16[576,6,64]{0,2,1:T(8,128)(2,1)S(1)} %bitcast.371, f32[576,6]{0,1:T(8,128)S(1)} %multiply_reduce_fusion.5, f32[576,6]{0,1:T(8,128)S(1)} %log_add_fusion.2), kind=kOutput, calls=%fused_computation.2.clone.1 | convolution fusion | flops 1051066368 | bytes 50015232 | tf_op jit(solution)/shard_map/while/body/eval_jaxpr/rhc,nhc->rhn/dot_general | solution.py:98
  429.2 9.9 fusion.263
  469.2 25.3 %copy.170 = f32[576,6,2304]{0,2,1:T(8,128)} copy(bf16[576,6,2304]{2,0,1:T(8,128)(2,1)} %fusion.262) | data formatting | bytes 47775744 | tf_op jit(solution)/shard_map/while/body/eval_jaxpr/convert_element_type | solution.py:111
  494.5 15.0 fusion.264
  532.1 12.5 convert_reduce_fusion.16
  568.2 8.5 all-reduce.9
  593.6 59.9 %reduce-scatter.9.cloned.1.call-done = f32[48,1536]{1,0:T(8,128)} async-done(((f32[768,1536]{1,0:T(8,128)}), f32[48,1536]{1,0:T(8,128)}) %reduce-scatter.9.cloned.1.call-update) | async-done | bytes 294928 | tf_op jit(solution)/shard_map/while/body/eval_jaxpr/reduce_scatter | solution.py:348
  655.2 77.3 %reduce-scatter.11.cloned.1.call-done = f32[48,1536]{1,0:T(8,128)} async-done(((f32[768,1536]{1,0:T(8,128)}), f32[48,1536]{1,0:T(8,128)}) %reduce-scatter.11.cloned.1.call-update) | async-done | bytes 294928 | tf_op jit(solution)/shard_map/while/body/eval_jaxpr/reduce_scatter | solution.py:349
  735.6 54.8 %all-reduce.24.cloned.1.call-done = (bf16[576,768]{1,0:T(8,128)(2,1)}, bf16[576,768]{1,0:T(8,128)(2,1)}) async-done(((bf16[576,768]{1,0:T(8,128)(2,1)}, bf16[576,768]{1,0:T(8,128)(2,1)}), (bf16[576,768]{1,0:T(8,128)(2,1)}, bf16[576,768]{1,0:T(8,128)(2,1)})) %all-reduce.24.cloned.1.call-update) | async-done | bytes 1769488 | tf_op jit(solution)/shard_map/while/body/eval_jaxpr/psum | solution.py:265
  794.1 117.3 %all-reduce.22.cloned.1.call-done = f32[3,768,384]{2,0,1:T(4,128)} async-done(((f32[3,768,384]{2,0,1:T(4,128)}), f32[3,768,384]{2,0,1:T(4,128)}) %all-reduce.22.cloned.1.call-update) | async-done | bytes 3538960 | tf_op jit(solution)/shard_map/while
  924.6 38.1 %all_gather.72 = bf16[768,384]{1,0:T(8,128)(2,1)S(1)} all-gather(bf16[48,384]{1,0:T(8,128)(2,1)S(1)} %copy-done.27), channel_id=1, replica_groups=mesh['fsdp'=4,'ctx'=4,'tp'=2] {'fsdp','ctx'}, dimensions={0}, use_global_device_ids=true | all-gather | bytes 626688 | tf_op jit(solution)/shard_map/while/body/eval_jaxpr/all_gather | solution.py:338
  992.7 12.8 broadcast_add_fusion.2
  1005.5 35.3 %copy.163 = f32[576,6,2304]{2,0,1:T(8,128)} copy(f32[576,6,2304]{0,2,1:T(8,128)} %bitcast.362) | data formatting | bytes 63700992 | tf_op jit(solution)/shard_map/while/body/eval_jaxpr/add | solution.py:67
  1046.9 24.9 %fusion.255 = (f32[576,6]{0,1:T(8,128)S(1)}, f32[576,6,2304]{2,0,1:T(8,128)}) fusion(f32[576,6,2304]{2,0,1:T(8,128)} %copy.163, bf16[2304,6,64]{0,2,1:T(8,128)(2,1)} %bitcast.363, f32[576,6,64]{0,2,1:T(8,128)} %bitcast.367, f32[6,64]{1,0:T(8,128)S(1)} %add.929), kind=kOutput, calls=%fused_computation.184.clone.1 | convolution fusion | flops 1043542656 | bytes 66370560 | tf_op jit(solution)/shard_map/while/body/eval_jaxpr/rhc,nhc->rhn/dot_general | solution.py:66
  1071.8 14.3 fusion.256
  1090.0 14.1 fusion.258
  1108.0 36.4 %all-reduce.18.cloned.1.call-done = bf16[576,768]{1,0:T(8,128)(2,1)} async-done(((bf16[576,768]{1,0:T(8,128)(2,1)}), bf16[576,768]{1,0:T(8,128)(2,1)}) %all-reduce.18.cloned.1.call-update) | async-done | bytes 884752 | tf_op jit(solution)/shard_map/while/body/eval_jaxpr/psum | solution.py:117
  1146.5 41.7 %all-gather.10.cloned.1.call-done = bf16[768,1536]{1,0:T(8,128)(2,1)} async-done(((bf16[48,1536]{1,0:T(8,128)(2,1)}), bf16[768,1536]{1,0:T(8,128)(2,1)}) %all-gather.10.cloned.1.call-update) | async-done | bytes 2359312 | tf_op jit(solution)/shard_map/while/body/eval_jaxpr/all_gather | solution.py:339
  1188.3 12.4 multiply_convert_fusion.2
  1200.7 30.9 %all-gather.18.cloned.1.call-done = bf16[768,1536]{1,0:T(8,128)(2,1)} async-done(((bf16[48,1536]{1,0:T(8,128)(2,1)}), bf16[768,1536]{1,0:T(8,128)(2,1)}) %all-gather.18.cloned.1.call-update) | async-done | bytes 2359312 | tf_op jit(solution)/shard_map/while/body/eval_jaxpr/all_gather | solution.py:340
  1231.7 6.6 convert_reduce_fusion.14
  1242.5 35.5 %all-reduce.20.cloned.1.call-done = bf16[576,768]{1,0:T(8,128)(2,1)} async-done(((bf16[576,768]{1,0:T(8,128)(2,1)}), bf16[576,768]{1,0:T(8,128)(2,1)}) %all-reduce.20.cloned.1.call-update) | async-done | bytes 884752 | tf_op jit(solution)/shard_map/while/body/eval_jaxpr/psum | solution.py:189
  1286.5 13.8 fusion.261
  1305.5 19.7 %fusion.262 = bf16[576,6,2304]{2,0,1:T(8,128)(2,1)} fusion(f32[576,6,2304]{2,0,1:T(8,128)} %get-tuple-element.1290, bf16[2304,6,64]{0,2,1:T(8,128)(2,1)} %bitcast.366, bf16[576,6,64]{0,2,1:T(8,128)(2,1)S(1)} %bitcast.371, f32[576,6]{0,1:T(8,128)S(1)} %multiply_reduce_fusion.5, f32[576,6]{0,1:T(8,128)S(1)} %log_add_fusion.2), kind=kOutput, calls=%fused_computation.2.clone.1 | convolution fusion | flops 1051066368 | bytes 50015232 | tf_op jit(solution)/shard_map/while/body/eval_jaxpr/rhc,nhc->rhn/dot_general | solution.py:98
  1325.2 9.9 fusion.263
  1365.1 25.3 %copy.170 = f32[576,6,2304]{0,2,1:T(8,128)} copy(bf16[576,6,2304]{2,0,1:T(8,128)(2,1)} %fusion.262) | data formatting | bytes 47775744 | tf_op jit(solution)/shard_map/while/body/eval_jaxpr/convert_element_type | solution.py:111
  1390.4 15.0 fusion.264
  1428.0 12.5 convert_reduce_fusion.16
  1464.1 8.5 all-reduce.9
  1489.6 59.9 %reduce-scatter.9.cloned.1.call-done = f32[48,1536]{1,0:T(8,128)} async-done(((f32[768,1536]{1,0:T(8,128)}), f32[48,1536]{1,0:T(8,128)}) %reduce-scatter.9.cloned.1.call-update) | async-done | bytes 294928 | tf_op jit(solution)/shard_map/while/body/eval_jaxpr/reduce_scatter | solution.py:348
  1551.4 77.1 %reduce-scatter.11.cloned.1.call-done = f32[48,1536]{1,0:T(8,128)} async-done(((f32[768,1536]{1,0:T(8,128)}), f32[48,1536]{1,0:T(8,128)}) %reduce-scatter.11.cloned.1.call-update) | async-done | bytes 294928 | tf_op jit(solution)/shard_map/while/body/eval_jaxpr/reduce_scatter | solution.py:349
  1631.6 54.8 %all-reduce.24.cloned.1.call-done = (bf16[576,768]{1,0:T(8,128)(2,1)}, bf16[576,768]{1,0:T(8,128)(2,1)}) async-done(((bf16[576,768]{1,0:T(8,128)(2,1)}, bf16[576,768]{1,0:T(8,128)(2,1)}), (bf16[576,768]{1,0:T(8,128)(2,1)}, bf16[576,768]{1,0:T(8,128)(2,1)})) %all-reduce.24.cloned.1.call-update) | async-done | bytes 1769488 | tf_op jit(solution)/shard_map/while/body/eval_jaxpr/psum | solution.py:265
  1690.8 116.4 %all-reduce.22.cloned.1.call-done = f32[3,768,384]{2,0,1:T(4,128)} async-done(((f32[3,768,384]{2,0,1:T(4,128)}), f32[3,768,384]{2,0,1:T(4,128)}) %all-reduce.22.cloned.1.call-update) | async-done | bytes 3538960 | tf_op jit(solution)/shard_map/while
  1816.1 94.9 %all-reduce.16.cloned.1.call-done = (f32[768]{0:T(1024)}, f32[768]{0:T(1024)}, f32[2,384]{1,0:T(2,128)}, f32[95,64]{0,1:T(8,128)}, f32[95,64]{0,1:T(8,128)}, /*i...) async-done(((f32[768]{0:T(1024)}, f32[768]{0:T(1024)}, f32[2,384]{1,0:T(2,128)}, f32[95,64]{0,1:T(8,128)}, f32[95,64]{0,1:T(8,128)}, ...) | async-done | bytes 76304 | tf_op jit(solution)/shard_map/psum | solution.py:357
  (411 shorter events, 383.2 us)
Async XLA Ops:
  19.9 47.3 %all-gather.12.cloned.1.call-start = ((), (), s32[]{:S(2)}) async-start(), calls=%async_computation.6 | async-start | bytes 1880064 | tf_op jit(solution)/shard_map/while/body/eval_jaxpr/all_gather | solution.py:337
  20.6 127.2 %all-gather.14.cloned.1.call-start = ((), (), s32[]{:S(2)}) async-start(), calls=%async_computation.7 | async-start | bytes 2211840 | tf_op jit(solution)/shard_map/while/body/eval_jaxpr/all_gather | solution.py:224
  24.6 64.3 %copy-start.13 = (f32[12,48,64,1]{2,1,3,0:T(8,128)}, f32[12,48,64,1]{2,1,3,0:T(8,128)S(1)}, u32[]{:S(2)}) copy-start(f32[12,48,64,1]{2,1,3,0:T(8,128)S(1)} %convolution_bitcast_fusion.16) | copy-start | bytes 442372 | tf_op jit(solution)/shard_map/while
  27.3 39.9 %copy-start.23 = (f32[576]{0:T(1024)}, f32[576]{0:T(1024)S(1)}, u32[]{:S(2)}) copy-start(f32[576]{0:T(1024)S(1)} %broadcast_multiply_fusion.11) | copy-start | bytes 6916 | tf_op jit(solution)/shard_map/while
  27.7 39.4 %copy-start.25 = (f32[576]{0:T(1024)}, f32[576]{0:T(1024)S(1)}, u32[]{:S(2)}) copy-start(f32[576]{0:T(1024)S(1)} %add_rsqrt_fusion.4) | copy-start | bytes 6916 | tf_op jit(solution)/shard_map/while
  67.2 141.7 %copy-start.6 = (bf16[768,384]{1,0:T(8,128)(2,1)}, bf16[768,384]{1,0:T(8,128)(2,1)S(1)}, u32[]{:S(2)}) copy-start(bf16[768,384]{1,0:T(8,128)(2,1)S(1)} %all_gather.72) | copy-start | bytes 1769476 | tf_op jit(solution)/shard_map/while
  76.0 115.0 %all-gather.16.cloned.1.call-start = ((), (), s32[]{:S(2)}) async-start(), calls=%async_computation.8 | async-start | bytes 2211840 | tf_op jit(solution)/shard_map/while/body/eval_jaxpr/all_gather | solution.py:225
  110.0 35.3 %copy-start.30 = (f32[384]{0:T(512)S(1)}, f32[384]{0:T(512)}, u32[]{:S(2)}) copy-start(f32[384]{0:T(512)} %get-tuple-element.1292) | copy-start | bytes 4612 | tf_op jit(solution)/shard_map/while
  147.3 101.3 %all-reduce.18.cloned.1.call-start = ((), (), s32[]{:S(2)}) async-start(), calls=%async_computation.9 | async-start | bytes 1769472 | tf_op jit(solution)/shard_map/while/body/eval_jaxpr/psum | solution.py:117
  211.4 81.1 %all-gather.10.cloned.1.call-start = ((), (), s32[]{:S(2)}) async-start(), calls=%async_computation.5 | async-start | bytes 2506752 | tf_op jit(solution)/shard_map/while/body/eval_jaxpr/all_gather | solution.py:339
  212.0 123.8 %all-gather.18.cloned.1.call-start = ((), (), s32[]{:S(2)}) async-start(), calls=%async_computation.10 | async-start | bytes 2506752 | tf_op jit(solution)/shard_map/while/body/eval_jaxpr/all_gather | solution.py:340
  212.6 169.5 %all-reduce.20.cloned.1.call-start = ((), (), s32[]{:S(2)}) async-start(), calls=%async_computation.11 | async-start | bytes 1769472 | tf_op jit(solution)/shard_map/while/body/eval_jaxpr/psum | solution.py:189
  248.6 43.9 %copy-start.32 = (f32[1536]{0:T(1024)S(1)}, f32[1536]{0:T(1024)}, u32[]{:S(2)}) copy-start(f32[1536]{0:T(1024)} %get-tuple-element.1445) | copy-start | bytes 18436 | tf_op jit(solution)/shard_map/while
  248.6 43.9 %copy-start.33 = (f32[768]{0:T(1024)S(1)}, f32[768]{0:T(1024)}, u32[]{:S(2)}) copy-start(f32[768]{0:T(1024)} %get-tuple-element.1443) | copy-start | bytes 9220 | tf_op jit(solution)/shard_map/while
  346.1 205.7 %reduce-scatter.5.cloned.1.call-start = ((), (), s32[]{:S(2)}) async-start(), calls=%async_computation.12 | async-start | bytes 4423680 | tf_op jit(solution)/shard_map/while/body/eval_jaxpr/reduce_scatter | solution.py:229
  447.2 133.5 %reduce-scatter.7.cloned.1.call-start = ((), (), s32[]{:S(2)}) async-start(), calls=%async_computation.14 | async-start | bytes 1253376 | tf_op jit(solution)/shard_map/while/body/eval_jaxpr/reduce_scatter | solution.py:347
  450.1 203.4 %reduce-scatter.9.cloned.1.call-start = ((), (), s32[]{:S(2)}) async-start(), calls=%async_computation.15 | async-start | bytes 5013504 | tf_op jit(solution)/shard_map/while/body/eval_jaxpr/reduce_scatter | solution.py:348
  456.5 276.1 %reduce-scatter.11.cloned.1.call-start = ((), (), s32[]{:S(2)}) async-start(), calls=%async_computation.16 | async-start | bytes 5013504 | tf_op jit(solution)/shard_map/while/body/eval_jaxpr/reduce_scatter | solution.py:349
  462.5 327.9 %all-reduce.24.cloned.1.call-start = ((), (), s32[]{:S(2)}) async-start(), calls=%async_computation.17 | async-start | bytes 3538944 | tf_op jit(solution)/shard_map/while/body/eval_jaxpr/psum | solution.py:265
  557.9 24.3 %copy-start.24 = (f32[576]{0:T(1024)S(1)}, f32[576]{0:T(1024)}, u32[]{:S(2)}) copy-start(f32[576]{0:T(1024)} %copy-done.23) | copy-start | bytes 6916 | tf_op jit(solution)/shard_map/while
  557.9 353.4 %all-reduce.22.cloned.1.call-start = ((), (), s32[]{:S(2)}) async-start(), calls=%async_computation.13 | async-start | bytes 9437184 | tf_op jit(solution)/shard_map/while
  593.6 140.6 %copy-start.15 = (bf16[576,768]{1,0:T(8,128)(2,1)S(1)}, bf16[576,768]{1,0:T(8,128)(2,1)}, u32[]{:S(2)}) copy-start(bf16[576,768]{1,0:T(8,128)(2,1)} %reduce-scatter.5.cloned.1.call-done) | copy-start | bytes 2654212 | tf_op jit(solution)/shard_map/while
  790.4 122.7 %copy-start.11 = (bf16[576,768]{1,0:T(8,128)(2,1)S(1)}, bf16[576,768]{1,0:T(8,128)(2,1)}, u32[]{:S(2)}) copy-start(bf16[576,768]{1,0:T(8,128)(2,1)} %get-tuple-element.1307) | copy-start | bytes 2654212 | tf_op jit(solution)/shard_map/while
  916.9 45.8 %all-gather.12.cloned.1.call-start = ((), (), s32[]{:S(2)}) async-start(), calls=%async_computation.6 | async-start | bytes 1880064 | tf_op jit(solution)/shard_map/while/body/eval_jaxpr/all_gather | solution.py:337
  917.4 125.6 %all-gather.14.cloned.1.call-start = ((), (), s32[]{:S(2)}) async-start(), calls=%async_computation.7 | async-start | bytes 2211840 | tf_op jit(solution)/shard_map/while/body/eval_jaxpr/all_gather | solution.py:224
  921.5 63.0 %copy-start.13 = (f32[12,48,64,1]{2,1,3,0:T(8,128)}, f32[12,48,64,1]{2,1,3,0:T(8,128)S(1)}, u32[]{:S(2)}) copy-start(f32[12,48,64,1]{2,1,3,0:T(8,128)S(1)} %convolution_bitcast_fusion.16) | copy-start | bytes 442372 | tf_op jit(solution)/shard_map/while
  924.2 38.5 %copy-start.23 = (f32[576]{0:T(1024)}, f32[576]{0:T(1024)S(1)}, u32[]{:S(2)}) copy-start(f32[576]{0:T(1024)S(1)} %broadcast_multiply_fusion.11) | copy-start | bytes 6916 | tf_op jit(solution)/shard_map/while
  924.6 38.1 %copy-start.25 = (f32[576]{0:T(1024)}, f32[576]{0:T(1024)S(1)}, u32[]{:S(2)}) copy-start(f32[576]{0:T(1024)S(1)} %add_rsqrt_fusion.4) | copy-start | bytes 6916 | tf_op jit(solution)/shard_map/while
  962.7 141.5 %copy-start.6 = (bf16[768,384]{1,0:T(8,128)(2,1)}, bf16[768,384]{1,0:T(8,128)(2,1)S(1)}, u32[]{:S(2)}) copy-start(bf16[768,384]{1,0:T(8,128)(2,1)S(1)} %all_gather.72) | copy-start | bytes 1769476 | tf_op jit(solution)/shard_map/while
  971.5 114.7 %all-gather.16.cloned.1.call-start = ((), (), s32[]{:S(2)}) async-start(), calls=%async_computation.8 | async-start | bytes 2211840 | tf_op jit(solution)/shard_map/while/body/eval_jaxpr/all_gather | solution.py:225
  1005.5 35.3 %copy-start.30 = (f32[384]{0:T(512)S(1)}, f32[384]{0:T(512)}, u32[]{:S(2)}) copy-start(f32[384]{0:T(512)} %get-tuple-element.1292) | copy-start | bytes 4612 | tf_op jit(solution)/shard_map/while
  1042.8 101.6 %all-reduce.18.cloned.1.call-start = ((), (), s32[]{:S(2)}) async-start(), calls=%async_computation.9 | async-start | bytes 1769472 | tf_op jit(solution)/shard_map/while/body/eval_jaxpr/psum | solution.py:117
  1106.6 81.7 %all-gather.10.cloned.1.call-start = ((), (), s32[]{:S(2)}) async-start(), calls=%async_computation.5 | async-start | bytes 2506752 | tf_op jit(solution)/shard_map/while/body/eval_jaxpr/all_gather | solution.py:339
  1107.2 124.5 %all-gather.18.cloned.1.call-start = ((), (), s32[]{:S(2)}) async-start(), calls=%async_computation.10 | async-start | bytes 2506752 | tf_op jit(solution)/shard_map/while/body/eval_jaxpr/all_gather | solution.py:340
  1107.9 170.0 %all-reduce.20.cloned.1.call-start = ((), (), s32[]{:S(2)}) async-start(), calls=%async_computation.11 | async-start | bytes 1769472 | tf_op jit(solution)/shard_map/while/body/eval_jaxpr/psum | solution.py:189
  1144.4 43.9 %copy-start.32 = (f32[1536]{0:T(1024)S(1)}, f32[1536]{0:T(1024)}, u32[]{:S(2)}) copy-start(f32[1536]{0:T(1024)} %get-tuple-element.1445) | copy-start | bytes 18436 | tf_op jit(solution)/shard_map/while
  1144.4 43.9 %copy-start.33 = (f32[768]{0:T(1024)S(1)}, f32[768]{0:T(1024)}, u32[]{:S(2)}) copy-start(f32[768]{0:T(1024)} %get-tuple-element.1443) | copy-start | bytes 9220 | tf_op jit(solution)/shard_map/while
  1242.0 205.7 %reduce-scatter.5.cloned.1.call-start = ((), (), s32[]{:S(2)}) async-start(), calls=%async_computation.12 | async-start | bytes 4423680 | tf_op jit(solution)/shard_map/while/body/eval_jaxpr/reduce_scatter | solution.py:229
  1343.1 133.6 %reduce-scatter.7.cloned.1.call-start = ((), (), s32[]{:S(2)}) async-start(), calls=%async_computation.14 | async-start | bytes 1253376 | tf_op jit(solution)/shard_map/while/body/eval_jaxpr/reduce_scatter | solution.py:347
  1346.0 203.6 %reduce-scatter.9.cloned.1.call-start = ((), (), s32[]{:S(2)}) async-start(), calls=%async_computation.15 | async-start | bytes 5013504 | tf_op jit(solution)/shard_map/while/body/eval_jaxpr/reduce_scatter | solution.py:348
  1352.4 276.1 %reduce-scatter.11.cloned.1.call-start = ((), (), s32[]{:S(2)}) async-start(), calls=%async_computation.16 | async-start | bytes 5013504 | tf_op jit(solution)/shard_map/while/body/eval_jaxpr/reduce_scatter | solution.py:349
  1358.4 328.0 %all-reduce.24.cloned.1.call-start = ((), (), s32[]{:S(2)}) async-start(), calls=%async_computation.17 | async-start | bytes 3538944 | tf_op jit(solution)/shard_map/while/body/eval_jaxpr/psum | solution.py:265
  1453.8 24.5 %copy-start.24 = (f32[576]{0:T(1024)S(1)}, f32[576]{0:T(1024)}, u32[]{:S(2)}) copy-start(f32[576]{0:T(1024)} %copy-done.23) | copy-start | bytes 6916 | tf_op jit(solution)/shard_map/while
  1453.8 24.5 %copy-start.26 = (f32[576]{0:T(1024)S(1)}, f32[576]{0:T(1024)}, u32[]{:S(2)}) copy-start(f32[576]{0:T(1024)} %copy-done.25) | copy-start | bytes 6916 | tf_op jit(solution)/shard_map/while
  1453.8 353.3 %all-reduce.22.cloned.1.call-start = ((), (), s32[]{:S(2)}) async-start(), calls=%async_computation.13 | async-start | bytes 9437184 | tf_op jit(solution)/shard_map/while
  1489.6 140.6 %copy-start.15 = (bf16[576,768]{1,0:T(8,128)(2,1)S(1)}, bf16[576,768]{1,0:T(8,128)(2,1)}, u32[]{:S(2)}) copy-start(bf16[576,768]{1,0:T(8,128)(2,1)} %reduce-scatter.5.cloned.1.call-done) | copy-start | bytes 2654212 | tf_op jit(solution)/shard_map/while
  1686.4 122.6 %copy-start.11 = (bf16[576,768]{1,0:T(8,128)(2,1)S(1)}, bf16[576,768]{1,0:T(8,128)(2,1)}, u32[]{:S(2)}) copy-start(bf16[576,768]{1,0:T(8,128)(2,1)} %get-tuple-element.1307) | copy-start | bytes 2654212 | tf_op jit(solution)/shard_map/while
  1813.8 97.2 %all-reduce.16.cloned.1.call-start = ((), (), s32[]{:S(2)}) async-start(), calls=%async_computation.4 | async-start | bytes 202752 | tf_op jit(solution)/shard_map/psum | solution.py:357
  (53 other events, 327.2 us)
Sparse Core Ops, SparseCore 0:
  22.9 43.1 all-gather.11
  76.1 39.7 all-gather.13
  147.5 39.7 all-gather.15
  211.5 37.0 all-reduce.17
  250.8 41.6 all-gather.9
  294.7 41.0 all-gather.17
  346.2 35.7 all-reduce.19
  447.4 66.1 reduce-scatter.4
  517.2 58.5 reduce-scatter.6
  579.5 74.0 reduce-scatter.8
  657.9 74.6 reduce-scatter.10
  734.8 55.6 all-reduce.23
  794.5 116.7 all-reduce.21
  919.6 41.7 all-gather.11
  971.6 40.2 all-gather.13
  1042.9 40.1 all-gather.15
  1106.7 37.5 all-reduce.17
  1146.5 41.6 all-gather.9
  1190.6 41.0 all-gather.17
  1242.1 35.7 all-reduce.19
  1343.3 66.1 reduce-scatter.4
  1413.1 58.4 reduce-scatter.6
  1475.4 74.0 reduce-scatter.8
  1553.8 74.6 reduce-scatter.10
  1630.8 55.5 all-reduce.23
  1690.3 116.7 all-reduce.21
Sparse Core Ops, SparseCore 1:
  1820.3 90.7 all-reduce.15
where the time goes:
time: 1940 us; the launch traced here: 1930 us
  waiting for transfers between devices  1010 us (52%)
  matrix products  365 us (19%)
  local copies, waits for them, and re-layouts  270 us (14%)
  other arithmetic  174 us (9%)
  blocking collectives  94.5 us (5%)
    while x28, waiting for transfers between devices  237 us
    reduce_scatter x2, waiting for transfers between devices, per_batch(): lax.psum_scatter(big_grads[3], ('fsdp', 'ctx'), scatter_dimension=0, tile...  154 us
    reduce_scatter x2, waiting for transfers between devices, per_batch(): lax.psum_scatter(big_grads[2], ('fsdp', 'ctx'), scatter_dimension=0, tile...  120 us
    psum x2, waiting for transfers between devices, micro_step(): lax.psum(normed_part.astype(jnp.bfloat16), 'tp').astype(jnp.float32)  110 us
    psum x1, waiting for transfers between devices, local(): small_final = lax.psum(small_totals, ('fsdp', 'ctx'))  94.9 us
    all_gather x2, waiting for transfers between devices, per_batch(): lax.all_gather(up_weight, ('fsdp', 'ctx'), axis=0, tiled=True)  83.5 us
    add x6, local copies, waits for them, and re-layouts, piece_scores(): term_h[..., :, None] + term_w[..., None, :]  82.5 us
    all_gather x2, blocking collectives, per_batch(): lax.all_gather(proj_weight, ('fsdp', 'ctx'), axis=0, tiled=True)  77.5 us
  transfers between devices with their start and end apart: 27, of which 17 were waited for; matrix products, arithmetic and copies ran while one was open for 29% of the time, Pallas kernels for 0%

commit v1 on v0

--- a/solution.py
+++ b/solution.py
@@ -2,7 +2,11 @@
 
 import jax
 import jax.numpy as jnp
+import ml_dtypes
+import numpy as np
 from jax import lax
+from jax.experimental import pallas as pl
+from jax.experimental.pallas import tpu as pltpu
 from jax.sharding import PartitionSpec as P
 
 G = 48
@@ -11,6 +15,696 @@
 
 eps = 1e-06
 highest = lax.Precision.HIGHEST
+bf16, f32 = jnp.bfloat16, jnp.float32
+VMEM_BYTES = 56 * 1024 * 1024
+NN = (((1,), (0,)), ((), ()))
+NT = (((1,), (1,)), ((), ()))
+LH, LW = 64, 112
+
+
+def mm(a, b, dims=NN):
+    return lax.dot_general(a, b, dims, preferred_element_type=f32)
+
+
+def roll(x, shift, stride=None):
+    extra = {} if stride is None else dict(stride=stride, stride_axis=0)
+    return pltpu.roll(x, shift, 1, **extra)
+
+
+def lane_iota(shape):
+    return lax.broadcasted_iota(jnp.int32, shape, 1)
+
+
+def prep_kernel(order_ref, x_ref, w_ref, b_ref, tab_ref, hot_ref, q_ref, k_ref, v_ref, *, heads, sets, zparts):
+    rows = x_ref.shape[1]
+    part = rows // zparts
+    where = order_ref[pl.program_id(0)]
+    qkv = (mm(x_ref[0], w_ref[...]) + b_ref[...]).astype(bf16)
+    lane = lane_iota((G, 128))
+    hot_a = hot_ref[0, :, :128].astype(f32)
+    hot_b = hot_ref[0, :, 128:]
+    lane_all = lane_iota((rows, 128))
+    for h in range(heads):
+        q = qkv[:, h * 128:(h + 1) * 128]
+        k = qkv[:, (heads + h) * 128:(heads + h + 1) * 128].astype(f32)
+        v = qkv[:, (2 * heads + h) * 128:(2 * heads + h + 1) * 128].astype(f32)
+        k_ref[h, :, :128] = jnp.where(lane_all < 64, k, hot_a).astype(bf16)
+        k_ref[h, :, 128:] = hot_b
+        v_ref[h] = jnp.where(lane_all < 64, v, jnp.where(lane_all < 67, 1.0, 0.0)).astype(bf16)
+        turned = mm(q, tab_ref[...])
+        qf = q.astype(f32) * (HD ** -0.5)
+        for g in range(rows // G):
+            zsrc, inner = divmod(g, part // G)
+            r = zsrc * (sets * part // G) + where * (part // G) + inner
+            along_h = turned[g * G:(g + 1) * G, :128]
+            along_w = turned[g * G:(g + 1) * G, 128:]
+            h_a = roll(along_h, (LH - (G - 1) + 128 + r) % 128)
+            h_b = roll(along_h, (32 - (G - 1) + 128 + r) % 128)
+            w_a = roll(along_w, (LW - (G - 1)) % 128, 1)
+            w_b = roll(along_w, (80 - (G - 1)) % 128, 1)
+            h_lo = h_b - h_b.astype(bf16).astype(f32)
+            w_lo = w_b - w_b.astype(bf16).astype(f32)
+            first = jnp.where(lane < LH, qf[g * G:(g + 1) * G], jnp.where(lane < LW, h_a, w_a))
+            second = jnp.where(lane < 32, w_a, jnp.where(lane < 80, h_lo, w_lo))
+            q_ref[h, g * G:(g + 1) * G, :128] = first.astype(bf16)
+            q_ref[h, g * G:(g + 1) * G, 128:] = second.astype(bf16)
+
+
+def prep(x, w, b, tab, hot, order, heads, zparts):
+    sets, rows, d = x.shape
+    tokens = sets * rows
+    return pl.pallas_call(
+        partial(prep_kernel, heads=heads, sets=sets, zparts=zparts),
+        out_shape=(
+            jax.ShapeDtypeStruct((heads, tokens, 256), bf16),
+            jax.ShapeDtypeStruct((heads, tokens, 256), bf16),
+            jax.ShapeDtypeStruct((heads, tokens, 128), bf16),
+        ),
+        grid_spec=pltpu.PrefetchScalarGridSpec(
+            num_scalar_prefetch=1,
+            grid=(sets,),
+            in_specs=[
+                pl.BlockSpec((1, rows, d), lambda i, o: (i, 0, 0)),
+                pl.BlockSpec(w.shape, lambda i, o: (0, 0)),
+                pl.BlockSpec(b.shape, lambda i, o: (0, 0)),
+                pl.BlockSpec(tab.shape, lambda i, o: (0, 0)),
+                pl.BlockSpec((1, rows, 256), lambda i, o: (o[i], 0, 0)),
+            ],
+            out_specs=[
+                pl.BlockSpec((heads, rows, 256), lambda i, o: (0, o[i], 0)),
+                pl.BlockSpec((heads, rows, 256), lambda i, o: (0, o[i], 0)),
+                pl.BlockSpec((heads, rows, 128), lambda i, o: (0, o[i], 0)),
+            ],
+        ),
+        compiler_params=pltpu.CompilerParams(vmem_limit_bytes=VMEM_BYTES),
+        cost_estimate=pl.CostEstimate(flops=2 * tokens * d * w.shape[1], bytes_accessed=tokens * d * 2 + heads * tokens * 640 * 2, transcendentals=0),
+        name="prep",
+    )(order, x, w, b, tab, hot)
+
+
+def fwd_kernel(q_ref, k_ref, v_ref, att_ref, mix_ref, q2_ref, *, tile):
+    lane = lane_iota((tile, 128))
+    for i in range(q_ref.shape[1] // tile):
+        at = pl.ds(i * tile, tile)
+        q = q_ref[0, at, :]
+        s = mm(q, k_ref[0], NT)
+        m = jnp.max(s, axis=1, keepdims=True)
+        p = jnp.exp(s - m)
+        o = mm(p.astype(bf16), v_ref[0])
+        total = o[:, 64:65]
+        att = o / total
+        lse = m + jnp.log(total)
+        att_ref[0, at, :] = att
+        mix_ref[0, at, :] = att[:, :64].astype(bf16)
+        a = q[:, :128].astype(f32)
+        b = q[:, 128:].astype(f32)
+        full = a + roll(b, 32) - lse
+        high = full.astype(bf16)
+        low = roll(full - high.astype(f32), 96)
+        q2_ref[0, at, :128] = jnp.where((lane >= LH) & (lane < LW), high.astype(f32), a).astype(bf16)
+        q2_ref[0, at, 128:] = jnp.where((lane >= 32) & (lane < 80), low, b).astype(bf16)
+
+
+def attend(q, k, v, head, steps, tile):
+    heads, tokens, _ = q.shape
+    block = tokens // steps
+    return pl.pallas_call(
+        partial(fwd_kernel, tile=tile),
+        out_shape=(
+            jax.ShapeDtypeStruct((1, tokens, 128), f32),
+            jax.ShapeDtypeStruct((1, tokens, 64), bf16),
+            jax.ShapeDtypeStruct((1, tokens, 256), bf16),
+        ),
+        grid=(steps,),
+        in_specs=[
+            pl.BlockSpec((1, block, 256), lambda i: (head, i, 0)),
+            pl.BlockSpec((1, tokens, 256), lambda i: (head, 0, 0)),
+            pl.BlockSpec((1, tokens, 128), lambda i: (head, 0, 0)),
+        ],
+        out_specs=[
+            pl.BlockSpec((1, block, 128), lambda i: (0, i, 0)),
+            pl.BlockSpec((1, block, 64), lambda i: (0, i, 0)),
+            pl.BlockSpec((1, block, 256), lambda i: (0, i, 0)),
+        ],
+        compiler_params=pltpu.CompilerParams(vmem_limit_bytes=VMEM_BYTES),
+        cost_estimate=pl.CostEstimate(flops=2 * tokens * tokens * 512, bytes_accessed=tokens * 2000, transcendentals=tokens * tokens),
+        name="attend",
+    )(q, k, v)
+
+
+def bwd_kernel(q_ref, k_ref, v_ref, g_ref, att_ref, tab_ref, turn_ref, dq_ref, dk_ref, dv_ref, gr_ref, go_ref, kt_ref, acc_ref, lo_ref, *, tile, sets, zparts):
+    step = pl.program_id(0)
+    tokens = q_ref.shape[1]
+    lane = lane_iota((tokens, 128))
+
+    @pl.when(step == 0)
+    def _():
+        go = jnp.concatenate([g_ref[0].astype(f32), jnp.zeros((tokens, 64), f32)], axis=1)
+        dot = jnp.sum(go * att_ref[0], axis=1, keepdims=True)
+        high = dot.astype(bf16).astype(f32)
+        mid = (dot - high).astype(bf16).astype(f32)
+        low = dot - high - mid
+        go_ref[...] = jnp.where(lane < 64, go, jnp.where(lane == 64, -high, jnp.where(lane == 65, -mid, jnp.where(lane == 66, -low, 0.0)))).astype(bf16)
+        acc_ref[...] = jnp.zeros_like(acc_ref)
+        kt_ref[:LW] = k_ref[0, :, :128].T[:LW]
+        kt_ref[LW:] = turn_ref[...]
+
+    keys = k_ref.shape[1] // pl.num_programs(0)
+    for i in range(keys // tile):
+        at = pl.ds(pl.multiple_of(step * keys + i * tile, tile), tile)
+        s = mm(k_ref[0, at, :], q_ref[0], NT)
+        p = jnp.exp(s)
+        pb = p.astype(bf16)
+        d = (p * mm(v_ref[0, at, :], go_ref[...], NT)).astype(bf16)
+        dv_ref[0, i * tile:(i + 1) * tile, :] = mm(pb, go_ref[...]).astype(bf16)
+        dk_ref[0, i * tile:(i + 1) * tile, :] = mm(d, q_ref[0, :, :128]).astype(bf16)
+        acc_ref[...] += mm(kt_ref[:, at], d)
+
+    @pl.when(step == pl.num_programs(0) - 1)
+    def _():
+        rows = tokens // sets
+        part = rows // zparts
+        small = lane_iota((G, 128))
+        a = acc_ref[:128].T
+        b = jnp.concatenate([acc_ref[128:160], jnp.zeros((96, tokens), f32)], axis=0).T
+        for g in range(tokens // G):
+            st, rest = divmod(g, rows // G)
+            zsrc, inner = divmod(rest, part // G)
+            r = zsrc * (sets * part // G) + st * (part // G) + inner
+            ag = a[g * G:(g + 1) * G]
+            bg = b[g * G:(g + 1) * G]
+            along_h = jnp.where((small >= LH) & (small < LW), ag, 0.0)
+            along_w = jnp.where(small >= LW, ag, jnp.where(small < 32, bg, 0.0))
+            along_h = roll(along_h, (G - 1 - LH - r) % 128)
+            along_w = roll(along_w, (128 - LW) % 128, 1)
+            h_hi = along_h.astype(bf16)
+            w_hi = along_w.astype(bf16)
+            gr_ref[0, g * G:(g + 1) * G, :128] = h_hi
+            gr_ref[0, g * G:(g + 1) * G, 128:] = w_hi
+            lo_ref[g * G:(g + 1) * G, :128] = (along_h - h_hi.astype(f32)).astype(bf16)
+            lo_ref[g * G:(g + 1) * G, 128:] = (along_w - w_hi.astype(f32)).astype(bf16)
+        turned = mm(gr_ref[0], tab_ref[...], NT) + mm(lo_ref[...], tab_ref[...], NT)
+        dq_ref[0] = jnp.where(lane < 64, a * (HD ** -0.5) + turned, 0.0).astype(bf16)
+
+
+def attend_back(q2, k, v, g, att, tab, turn, head, steps, tile, sets, zparts):
+    _, tokens, _ = q2.shape
+    block = tokens // steps
+    return pl.pallas_call(
+        partial(bwd_kernel, tile=tile, sets=sets, zparts=zparts),
+        out_shape=(
+            jax.ShapeDtypeStruct((1, tokens, 128), bf16),
+            jax.ShapeDtypeStruct((1, tokens, 128), bf16),
+            jax.ShapeDtypeStruct((1, tokens, 128), bf16),
+            jax.ShapeDtypeStruct((1, tokens, 256), bf16),
+        ),
+        grid=(steps,),
+        in_specs=[
+            pl.BlockSpec((1, tokens, 256), lambda i: (0, 0, 0)),
+            pl.BlockSpec((1, tokens, 256), lambda i: (head, 0, 0)),
+            pl.BlockSpec((1, tokens, 128), lambda i: (head, 0, 0)),
+            pl.BlockSpec((1, tokens, 64), lambda i: (0, 0, 0)),
+            pl.BlockSpec((1, tokens, 128), lambda i: (0, 0, 0)),
+            pl.BlockSpec(tab.shape, lambda i: (0, 0)),
+            pl.BlockSpec(turn.shape, lambda i: (0, 0)),
+        ],
+        out_specs=[
+            pl.BlockSpec((1, tokens, 128), lambda i: (0, 0, 0)),
+            pl.BlockSpec((1, block, 128), lambda i: (0, i, 0)),
+            pl.BlockSpec((1, block, 128), lambda i: (0, i, 0)),
+            pl.BlockSpec((1, tokens, 256), lambda i: (0, 0, 0)),
+        ],
+        scratch_shapes=[
+            pltpu.VMEM((tokens, 128), bf16),
+            pltpu.VMEM((160, tokens), bf16),
+            pltpu.VMEM((160, tokens), f32),
+            pltpu.VMEM((tokens, 256), bf16),
+        ],
+        compiler_params=pltpu.CompilerParams(vmem_limit_bytes=VMEM_BYTES),
+        cost_estimate=pl.CostEstimate(flops=2 * tokens * tokens * 1280, bytes_accessed=tokens * 3000, transcendentals=tokens * tokens),
+        name="attend_back",
+    )(q2, k, v, g, att, tab, turn)
+
+
+TN = (((0,), (0,)), ((), ()))
+GC = 384
+
+
+def norm(v, gain, bias):
+    mean = jnp.mean(v, axis=1, keepdims=True)
+    centered = v - mean
+    inverse = lax.rsqrt(jnp.mean(centered * centered, axis=1, keepdims=True) + eps)
+    unit = centered * inverse
+    return unit * gain + bias, unit, inverse
+
+
+def norm_back(upstream, unit, inverse, gain):
+    scaled = upstream * gain
+    return inverse * (scaled - jnp.mean(scaled, axis=1, keepdims=True) - unit * jnp.mean(scaled * unit, axis=1, keepdims=True))
+
+
+def mlp_kernel(mix_ref, src_ref, top_ref, up_ref, down_ref, proj_ref, ub_ref, vec_ref,
+               out_ref, act_ref, hg_ref, n2_ref, mg_ref, br_ref, mgrad_ref, ubg_ref, vg_ref,
+               mid_ref, unit_ref, inv_ref, acc_ref, ng_ref):
+    step = pl.program_id(0)
+    last = pl.num_programs(0) - 1
+    d = src_ref.shape[1]
+    half = proj_ref.shape[3]
+
+    def proj(i):
+        return proj_ref[:, i].reshape(d, half)
+
+    @pl.when(step == 0)
+    def _():
+        mid = src_ref[...].astype(f32) + vec_ref[0:1] + mm(mix_ref[:, :half], proj(0), NT) + mm(mix_ref[:, half:], proj(1), NT)
+        normed, unit, inverse = norm(mid, vec_ref[1:2], vec_ref[2:3])
+        mid_ref[...] = mid
+        unit_ref[...] = unit
+        inv_ref[...] = inverse
+        n2_ref[...] = normed.astype(bf16)
+
+    tile = up_ref.shape[3]
+    up = up_ref[:, 0].reshape(d, tile)
+    down = down_ref[:, 0].reshape(d, tile)
+    hidden = mm(n2_ref[...], up) + ub_ref[...]
+    phi_all = 0.5 + 0.5 * lax.erf(hidden * (0.5 ** 0.5))
+    slope = phi_all + hidden * (jnp.exp(-0.5 * hidden * hidden) * 0.3989422804014327)
+    active = (hidden * phi_all).astype(bf16)
+    hg = (mm(top_ref[...], down) * slope).astype(bf16)
+    act_ref[...] = active
+    hg_ref[...] = hg
+    ubg_ref[...] = jnp.sum(hg.astype(f32), axis=0, keepdims=True)
+    out = mm(active, down, NT)
+    ng = mm(hg, up, NT)
+
+    @pl.when(step == 0)
+    def _():
+        acc_ref[...] = out
+        ng_ref[...] = ng
+
+    @pl.when(step > 0)
+    def _():
+        acc_ref[...] += out
+        ng_ref[...] += ng
+
+    @pl.when(step == last)
+    def _():
+        top = top_ref[...].astype(f32)
+        grad = ng_ref[...]
+        unit = unit_ref[...]
+        out_ref[...] = (mid_ref[...] + acc_ref[...] + vec_ref[3:4]).astype(bf16)
+        middle = top + norm_back(grad, unit, inv_ref[...], vec_ref[1:2])
+        branch = middle.astype(bf16)
+        mg_ref[...] = middle
+        br_ref[...] = branch
+        mgrad_ref[:, :half] = mm(branch, proj(0)).astype(bf16)
+        mgrad_ref[:, half:] = mm(branch, proj(1)).astype(bf16)
+        vg_ref[0:1] = jnp.sum(branch.astype(f32), axis=0, keepdims=True)
+        vg_ref[1:2] = jnp.sum(grad * unit, axis=0, keepdims=True)
+        vg_ref[2:3] = jnp.sum(grad, axis=0, keepdims=True)
+        vg_ref[3:4] = jnp.sum(top, axis=0, keepdims=True)
+
+
+def mlp(mixed, src, top, packed, up_bias, vecs, half_ff, tile=512):
+    rows, d = mixed.shape
+    blocks, halves, depth, _ = packed.shape
+    per = half_ff // tile
+    steps = halves * per
+    half = d // halves
+    whole = lambda i: (0, 0)
+    return pl.pallas_call(
+        mlp_kernel,
+        out_shape=(
+            jax.ShapeDtypeStruct((rows, d), bf16),
+            jax.ShapeDtypeStruct((rows, halves * half_ff), bf16),
+            jax.ShapeDtypeStruct((rows, halves * half_ff), bf16),
+            jax.ShapeDtypeStruct((rows, d), bf16),
+            jax.ShapeDtypeStruct((rows, d), f32),
+            jax.ShapeDtypeStruct((rows, d), bf16),
+            jax.ShapeDtypeStruct((rows, d), bf16),
+            jax.ShapeDtypeStruct((1, halves * half_ff), f32),
+            jax.ShapeDtypeStruct((4, d), f32),
+        ),
+        grid=(steps,),
+        in_specs=[
+            pl.BlockSpec((rows, d), whole),
+            pl.BlockSpec((rows, d), whole),
+            pl.BlockSpec((rows, d), whole),
+            pl.BlockSpec((blocks, 1, depth, tile), lambda i: (0, i // per, 0, i % per)),
+            pl.BlockSpec((blocks, 1, depth, tile), lambda i: (0, i // per, 0, per + i % per)),
+            pl.BlockSpec((blocks, halves, depth, half), lambda i: (0, 0, 0, 2 * half_ff // half)),
+            pl.BlockSpec((1, tile), lambda i: (0, i)),
+            pl.BlockSpec(vecs.shape, whole),
+        ],
+        out_specs=[
+            pl.BlockSpec((rows, d), whole),
+            pl.BlockSpec((rows, tile), lambda i: (0, i)),
+            pl.BlockSpec((rows, tile), lambda i: (0, i)),
+            pl.BlockSpec((rows, d), whole),
+            pl.BlockSpec((rows, d), whole),
+            pl.BlockSpec((rows, d), whole),
+            pl.BlockSpec((rows, d), whole),
+            pl.BlockSpec((1, tile), lambda i: (0, i)),
+            pl.BlockSpec((4, d), whole),
+        ],
+        scratch_shapes=[
+            pltpu.VMEM((rows, d), f32),
+            pltpu.VMEM((rows, d), f32),
+            pltpu.VMEM((rows, 1), f32),
+            pltpu.VMEM((rows, d), f32),
+            pltpu.VMEM((rows, d), f32),
+        ],
+        compiler_params=pltpu.CompilerParams(vmem_limit_bytes=VMEM_BYTES),
+        cost_estimate=pl.CostEstimate(flops=2 * rows * d * (4 * halves * half_ff + 2 * d), bytes_accessed=4 * d * halves * half_ff + 20 * rows * d, transcendentals=2 * rows * halves * half_ff),
+        name="mlp",
+    )(mixed, src, top, packed, packed, packed, up_bias, vecs)
+
+
+def wgrad_kernel(n2_ref, top_ref, br_ref, hg_ref, act_ref, mix_ref, out_ref, left_ref, *, per):
+    half, block = pl.program_id(0), pl.program_id(1)
+    blocks, depth = out_ref.shape[0], out_ref.shape[2]
+
+    @pl.when((half == 0) & (block == 0))
+    def _():
+        left_ref[0] = n2_ref[...].T
+        left_ref[1] = top_ref[...].T
+        left_ref[2] = br_ref[...].T
+
+    def put(i, right):
+        out_ref[:, 0] = mm(left_ref[i], right[...]).astype(bf16).reshape(blocks, depth, -1)
+
+    @pl.when(block < per)
+    def _():
+        put(0, hg_ref)
+
+    @pl.when((block >= per) & (block < 2 * per))
+    def _():
+        put(1, act_ref)
+
+    @pl.when(block == 2 * per)
+    def _():
+        put(2, mix_ref)
+
+
+def wgrad(n2, top, branch, hg, active, mixed, blocks, halves):
+    rows, d = n2.shape
+    ff = hg.shape[1]
+    tile = d // halves
+    per = ff // halves // tile
+    depth = d // blocks
+    whole = lambda s, j: (0, 0)
+    return pl.pallas_call(
+        partial(wgrad_kernel, per=per),
+        out_shape=jax.ShapeDtypeStruct((blocks, halves, depth, (2 * per + 1) * tile), bf16),
+        grid=(halves, 2 * per + 1),
+        in_specs=[
+            pl.BlockSpec((rows, d), whole),
+            pl.BlockSpec((rows, d), whole),
+            pl.BlockSpec((rows, d), whole),
+            pl.BlockSpec((rows, tile), lambda s, j: (0, s * per + jnp.minimum(j, per - 1))),
+            pl.BlockSpec((rows, tile), lambda s, j: (0, s * per + jnp.clip(j - per, 0, per - 1))),
+            pl.BlockSpec((rows, tile), lambda s, j: (0, s)),
+        ],
+        out_specs=pl.BlockSpec((blocks, 1, depth, tile), lambda s, j: (0, s, 0, j)),
+        scratch_shapes=[pltpu.VMEM((3, d, rows), bf16)],
+        compiler_params=pltpu.CompilerParams(vmem_limit_bytes=VMEM_BYTES),
+        cost_estimate=pl.CostEstimate(flops=2 * rows * d * (2 * ff + d), bytes_accessed=4 * d * ff + 8 * rows * ff, transcendentals=0),
+        name="wgrad",
+    )(n2, top, branch, hg, active, mixed)
+
+
+def close_kernel(order_ref, x_ref, w_ref, *refs, heads):
+    parts, (ng_ref, wg_ref, bg_ref, acc_ref) = refs[:3 * heads], refs[3 * heads:]
+    step = pl.program_id(0)
+    whole = jnp.concatenate([p[0] for p in parts], axis=1)
+    ng_ref[0] = mm(whole, w_ref[...], NT).astype(bf16)
+    add = mm(x_ref[0].T, whole)
+    sums = jnp.sum(whole.astype(f32), axis=0, keepdims=True)
+
+    @pl.when(step == 0)
+    def _():
+        acc_ref[...] = add
+        bg_ref[...] = sums
+
+    @pl.when(step > 0)
+    def _():
+        acc_ref[...] += add
+        bg_ref[...] += sums
+
+    @pl.when(step == pl.num_programs(0) - 1)
+    def _():
+        wg_ref[...] = acc_ref[...].astype(bf16)
+
+
+def close(x, w, grads, order, heads):
+    sets, rows, d = x.shape
+    width = w.shape[1]
+    return pl.pallas_call(
+        partial(close_kernel, heads=heads),
+        out_shape=(
+            jax.ShapeDtypeStruct((sets, rows, d), bf16),
+            jax.ShapeDtypeStruct((d, width), bf16),
+            jax.ShapeDtypeStruct((1, width), f32),
+        ),
+        grid_spec=pltpu.PrefetchScalarGridSpec(
+            num_scalar_prefetch=1,
+            grid=(sets,),
+            in_specs=[
+                pl.BlockSpec((1, rows, d), lambda i, o: (i, 0, 0)),
+                pl.BlockSpec(w.shape, lambda i, o: (0, 0)),
+            ] + [pl.BlockSpec((1, rows, 128), lambda i, o: (0, o[i], 0))] * (3 * heads),
+            out_specs=[
+                pl.BlockSpec((1, rows, d), lambda i, o: (i, 0, 0)),
+                pl.BlockSpec((d, width), lambda i, o: (0, 0)),
+                pl.BlockSpec((1, width), lambda i, o: (0, 0)),
+            ],
+            scratch_shapes=[pltpu.VMEM((d, width), f32)],
+        ),
+        compiler_params=pltpu.CompilerParams(vmem_limit_bytes=VMEM_BYTES),
+        cost_estimate=pl.CostEstimate(flops=4 * sets * rows * d * width, bytes_accessed=2 * sets * rows * (2 * d + width), transcendentals=0),
+        name="close",
+    )(order, x, w, *grads)
+
+
+def pairs_of(shape, move):
+    nf, nc, nt = shape["fsdp"], shape["ctx"], shape["tp"]
+    out = []
+    for f in range(nf):
+        for z in range(nc):
+            for t in range(nt):
+                g, w, u = move(f, z, t)
+                out.append(((f * nc + z) * nt + t, (g * nc + w) * nt + u))
+    return out
+
+
+AXES = ("fsdp", "ctx", "tp")
+
+
+def grouped(
+    shape,
+    images,
+    norm1_gain,
+    norm1_bias,
+    qkv_weight,
+    qv_bias,
+    rel_pos_h,
+    rel_pos_w,
+    proj_weight,
+    proj_bias,
+    norm2_gain,
+    norm2_bias,
+    up_weight,
+    up_bias,
+    down_weight,
+    down_bias,
+    out_cotangent,
+):
+    nf, nc, nt = shape["fsdp"], shape["ctx"], shape["tp"]
+    batch, quarter, d = images.shape
+    sets = 2 * nt
+    chunk = quarter // sets
+    rows = nc * chunk
+    tokens = sets * rows
+    half = qkv_weight.shape[2]
+    width = half // 2
+    heads = width // HD
+    depth = qkv_weight.shape[1]
+    blocks = nf * nc
+    half_ff = up_weight.shape[1]
+    fi, z, t = lax.axis_index("fsdp"), lax.axis_index("ctx"), lax.axis_index("tp")
+    c = fi % 2
+    me = 2 * t + c
+
+    def send(x, move):
+        return lax.ppermute(x, AXES, pairs_of(shape, move))
+
+    core = lambda x: send(x, lambda f, w, u: (f ^ 1, w, u))
+    across = lambda x: send(x, lambda f, w, u: (f, w, u ^ 1))
+    diagonal = lambda x: send(x, lambda f, w, u: (f ^ 1, w, u ^ 1))
+    xswap = lambda x: send(x, lambda f, w, u: (f ^ 2, w, u))
+    zswap = lambda x, k: send(x, lambda f, w, u: (f, w ^ k, u))
+
+    def pick(x, i, axis=0):
+        return lax.dynamic_index_in_dim(x, i, axis, keepdims=False)
+
+    def ordered(bit, mine, other, axis=0):
+        return jnp.where(bit == 0, jnp.concatenate([mine, other], axis), jnp.concatenate([other, mine], axis))
+
+    f = lambda v: v.astype(f32)
+
+    packed = lax.all_gather(
+        jnp.concatenate([up_weight, down_weight, proj_weight], axis=1), AXES, axis=0, tiled=False
+    ).reshape(blocks, nt, depth, 2 * half_ff + half)
+
+    def scatter_tokens(x):
+        parts = x.reshape(batch, sets, chunk, d)
+        four = ordered(c, pick(parts, me, 1), core(pick(parts, me ^ 1, 1)))
+        return lax.all_to_all(four, "ctx", 0, 0, tiled=True).reshape(rows, d)
+
+    def gather_tokens(x):
+        four = lax.all_to_all(x.reshape(nc, chunk, d), "ctx", 0, 0, tiled=True).reshape(2, batch, 1, chunk, d)
+        mine = ordered(c, pick(four, c), core(pick(four, 1 - c)), 1)
+        return ordered(t, mine, across(mine), 1).reshape(batch, quarter, d)
+
+    src = scatter_tokens(images)
+    normed_f, unit1, inverse1 = norm(f(src), f(norm1_gain), f(norm1_bias))
+    normed = normed_f.astype(bf16)
+    other = across(normed)
+    near = core(jnp.stack([normed, other]))
+    all_normed = jnp.stack([normed, near[0], other, near[1]])
+    order = jnp.arange(sets, dtype=jnp.int32) ^ me
+
+    cols = qkv_weight.reshape(3, depth, 2, width)
+    w = ordered(c, pick(cols, c, 2)[None], core(pick(cols, 1 - c, 2))[None])
+    step = 1
+    w = w[None]
+    while step < nc:
+        w = ordered((z // step) % 2, w, zswap(w, step))
+        step *= 2
+    w = w[None]
+    w = ordered(fi // 2, w, xswap(w))
+    w = w.transpose(0, 2, 1, 4, 3, 5).reshape(d, 3, heads, HD)
+    w = jnp.pad(w, ((0, 0), (0, 0), (0, 0), (0, HD))).reshape(d, 3 * heads * 2 * HD)
+    bias = pick(qv_bias.reshape(2, 2, heads, HD), c, 1)
+    bias = jnp.stack([bias[0], jnp.zeros_like(bias[0]), bias[1]])
+    bias = jnp.pad(f(bias), ((0, 0), (0, 0), (0, HD))).reshape(1, -1)
+
+    flip = lambda v: jnp.pad(v[::-1].T, ((0, HD), (0, 128 - (2 * G - 1))))
+    plain = lambda v: jnp.pad(v.T, ((0, HD), (0, 128 - (2 * G - 1))))
+    tab = jnp.concatenate([flip(rel_pos_h), flip(rel_pos_w)], axis=1)
+    tab_back = jnp.concatenate([flip(rel_pos_h), plain(rel_pos_w)], axis=1)
+    place = np.array([w_ * quarter + s * chunk + i for s in range(sets) for w_ in range(nc) for i in range(chunk)])
+    at = np.arange(tokens)
+    hot = np.zeros((tokens, 256), np.float32)
+    for base, index in ((LH, place // G), (LW, place % G), (160, place // G), (208, place % G)):
+        hot[at, base + index] = 1
+    turn = np.zeros((G, tokens), np.float32)
+    turn[G - 1 - place % G, at] = 1
+    hot = jnp.asarray(hot.astype(ml_dtypes.bfloat16).reshape(sets, rows, 256))
+    turn = jnp.asarray(turn.astype(ml_dtypes.bfloat16))
+
+    q, k, v = prep(all_normed, w, bias, tab, hot, order, heads, nc)
+    forward = [attend(q, k, v, h, 3, 256) for h in range(heads)]
+
+    def swap_blocks(x):
+        got = jnp.stack([pick(x, me), core(pick(x, me ^ 1)), across(pick(x, me ^ 2)), diagonal(pick(x, me ^ 3))])
+        return jnp.stack([pick(got, i ^ me) for i in range(sets)])
+
+    mixed = jnp.concatenate([m[1][0] for m in forward], axis=1).reshape(sets, rows, width)
+    mixed = swap_blocks(mixed).transpose(1, 0, 2).reshape(rows, d)
+
+    top = scatter_tokens(out_cotangent)
+    full_bias = f(jnp.where(t == 0, jnp.concatenate([up_bias, up_bias]), jnp.concatenate([up_bias, up_bias])))
+    other_bias = f(across(up_bias))
+    full_bias = ordered(t, f(up_bias), other_bias)[None]
+    vecs = jnp.stack([f(proj_bias), f(norm2_gain), f(norm2_bias), f(down_bias)])
+    result, active, hidden_grad, normed2, middle_grad, branch, mixed_grad, up_bias_grad, vec_grads = mlp(
+        mixed, src, top, packed, full_bias, vecs, half_ff, 512
+    )
+    big = wgrad(normed2, top, branch, hidden_grad, active, mixed, blocks, nt)
+    big = lax.psum_scatter(big.reshape(blocks * nt, depth, -1), AXES, scatter_dimension=0, tiled=True)
+    big = f(big.reshape(depth, -1))
+
+    back = swap_blocks(mixed_grad.reshape(rows, sets, width).transpose(1, 0, 2))
+    back = back.reshape(tokens, heads, HD).transpose(1, 0, 2)
+    grads = [
+        attend_back(forward[h][2], k, v, back[h:h + 1], forward[h][0], tab_back, turn, h, 3, 256, sets, nc)
+        for h in range(heads)
+    ]
+    tables = sum(
+        lax.dot_general(g[3][0], q[h, :, :HD], (((0,), (0,)), ((), ())), preferred_element_type=f32)
+        for h, g in enumerate(grads)
+    ) * HD ** 0.5
+    small_part, weight_part, sums = close(
+        all_normed, w, [g[j] for j in range(3) for g in grads], order, heads
+    )
+
+    got = core(jnp.stack([small_part[1], small_part[3]]))
+    normed_grad = f(small_part[0]) + f(got[0]) + f(across((f(small_part[2]) + f(got[1])).astype(bf16)))
+    input_grad = (middle_grad + norm_back(normed_grad, unit1, inverse1, f(norm1_gain))).astype(bf16)
+    result = gather_tokens(result)
+    input_grad = gather_tokens(input_grad)
+
+    wg = weight_part.reshape(nf // 2, 2, nc, depth, 3, heads, 2 * HD)[..., :HD].reshape(nf // 2, 2, nc, depth, 3, width)
+    wg = wg.transpose(0, 2, 1, 4, 3, 5)
+    wg = f(pick(wg, fi // 2)) + f(xswap(pick(wg, 1 - fi // 2)))
+    step = nc // 2
+    while step:
+        bit = (z // step) % 2
+        wg = wg.reshape((2, step) + wg.shape[1:])
+        wg = pick(wg, bit) + f(zswap(pick(wg, 1 - bit).astype(bf16), step))
+        step //= 2
+    wg = wg[0].astype(bf16)
+    wg = f(ordered(c, pick(wg, c)[:, :, None], core(pick(wg, 1 - c))[:, :, None], 2).reshape(3, depth, half))
+
+    def total(x):
+        for move in (core, across, xswap):
+            x = x + move(x)
+        step = 1
+        while step < nc:
+            x = x + zswap(x, step)
+            step *= 2
+        return x
+
+    sums = sums.reshape(3, heads, 2 * HD)[:, :, :HD].reshape(3, width)[::2]
+    sums = jnp.where(jnp.arange(sets)[:, None, None] == me, sums[None], 0.0)
+    sums = sums.transpose(1, 0, 2).reshape(2, d)
+    vectors = jnp.concatenate(
+        [
+            jnp.sum(normed_grad * unit1, axis=0),
+            jnp.sum(normed_grad, axis=0),
+            vec_grads.reshape(-1),
+            sums.reshape(-1),
+            up_bias_grad.reshape(-1),
+            tables.reshape(-1),
+        ]
+    )
+    vectors = total(vectors.reshape(-1, 128)).reshape(-1)
+    at = 0
+    cut = []
+    for size in (d, d, d, d, d, d, 2 * d, nt * half_ff, 256 * HD):
+        cut.append(lax.slice(vectors, (at,), (at + size,)))
+        at += size
+    g1, b1, pb, g2, b2, db, qv, ub, tg = cut
+    tg = tg.reshape(256, HD)
+    return (
+        result,
+        input_grad,
+        g1,
+        b1,
+        wg,
+        pick(qv.reshape(2, nt, half), t, 1),
+        tg[: 2 * G - 1][::-1],
+        tg[128 : 128 + 2 * G - 1],
+        big[:, 2 * half_ff :],
+        pb,
+        g2,
+        b2,
+        big[:, :half_ff],
+        pick(ub.reshape(nt, half_ff), t),
+        big[:, half_ff : 2 * half_ff],
+        db,
+    )
 
 
 def layer_norm(values, gain_vec, shift_vec):
@@ -20,7 +714,7 @@
     return (standard * gain_vec + shift_vec, standard, inverse)
 
 
-def norm_back(upstream, standard, inverse, gain_vec):
+def norm_back_plain(upstream, standard, inverse, gain_vec):
     scaled = upstream * gain_vec
     mean_term = jnp.mean(scaled, axis=-1, keepdims=True)
     proj_term = jnp.mean(scaled * standard, axis=-1, keepdims=True)
@@ -189,7 +883,7 @@
     normed2_grad = lax.psum(contract_last(hidden_grad, up_full).astype(jnp.bfloat16), "tp").astype(
         jnp.float32
     )
-    middle_grad = top_f + norm_back(normed2_grad, standard_two, inverse_two, gain_two)
+    middle_grad = top_f + norm_back_plain(normed2_grad, standard_two, inverse_two, gain_two)
     gain_two_grad = jnp.sum(normed2_grad * standard_two, axis=0)
     shift_two_grad = jnp.sum(normed2_grad, axis=0)
     branch_grad = middle_grad.astype(jnp.bfloat16)
@@ -266,7 +960,7 @@
         lax.psum(table_h_part.astype(jnp.bfloat16), "tp").astype(jnp.float32),
         lax.psum(table_w_part.astype(jnp.bfloat16), "tp").astype(jnp.float32),
     )
-    input_grad = (middle_grad + norm_back(normed_grad, standard_one, inverse_one, gain_one)).astype(
+    input_grad = (middle_grad + norm_back_plain(normed_grad, standard_one, inverse_one, gain_one)).astype(
         jnp.bfloat16
     )
     gain_one_grad = jnp.sum(normed_grad * standard_one, axis=0)
@@ -376,6 +1070,8 @@
 
 
 def solution(mesh):
+    shape = dict(mesh.shape)
+    body = partial(grouped, shape) if shape["fsdp"] == 4 and shape["ctx"] == 4 and shape["tp"] == 2 else local
     placed = (
         P("fsdp", "ctx", None),
         P(),
@@ -395,7 +1091,7 @@
         P("fsdp", "ctx", None),
     )
     return jax.shard_map(
-        local,
+        body,
         mesh=mesh,
         in_specs=placed,
         out_specs=(

time: 1940 us -> 505 us (0.26)
  waiting for transfers between devices: 1010 us -> 164 us
  matrix products: 365 us -> 4.7 us
  local copies, waits for them, and re-layouts: 270 us -> 51.3 us
  Pallas kernels: 0 us -> 172 us
  other arithmetic: 174 us -> 34.8 us
  blocking collectives: 94.5 us -> 0 us
  starting transfers between devices: 2.98 us -> 53.8 us
    dot_general x56 -> x3, matrix products: 365 us -> 4.7 us  [grouped(): lax.dot_general(g[3][0], q[h, :, :HD], (((0,), (0,)), ((), ())), preferre...]
    psum x7 -> x0, waiting for transfers between devices: 348 us -> none  [the longest x2 110 us: micro_step(): lax.psum(normed_part.astype(jnp.bfloat16), 'tp').astype(jnp.float32)]
    reduce_scatter x8 -> x1, waiting for transfers between devices: 274 us -> 0.01 us  [grouped(): lax.psum_scatter(big.reshape(blocks * nt, depth, -1), AXES, scatter_dimen...]
    while x28 -> x0, waiting for transfers between devices: 237 us -> none
    pallas_call x0 -> x10, Pallas kernels: none -> 172 us  [the longest x3 61.6 us: attend_back(): pl.pallas_call(partial(bwd_kernel, tile=tile, sets=sets, zparts=zparts),...]
    all_gather x10 -> x1, waiting for transfers between devices: 145 us -> 0.01 us  [grouped(): lax.all_gather(jnp.concatenate([up_weight, down_weight, proj_weight], axi...]
    ppermute x0 -> x30, waiting for transfers between devices: none -> 122 us  [send(): return lax.ppermute(x, AXES, pairs_of(shape, move))]
    add x10 -> x0, local copies, waits for them, and re-layouts: 85.5 us -> none  [the longest x6 82.5 us: piece_scores(): term_h[..., :, None] + term_w[..., None, :]]
  transfers between devices with their start and end apart: 27 -> 36, of which waited for: 17 -> 19; matrix products, arithmetic and copies ran while one was open for 29% -> 17% of each run, Pallas kernels for 0% -> 25%
where the time goes in v1:
time: 505 us; the launch traced here: 496 us
  Pallas kernels  172 us (34%)
  waiting for transfers between devices  164 us (32%)
  starting transfers between devices  53.8 us (11%)
  local copies, waits for them, and re-layouts  51.3 us (10%)
  other arithmetic  34.8 us (7%)
  between operations  15.1 us (3%)
    ppermute x30, waiting for transfers between devices, send(): return lax.ppermute(x, AXES, pairs_of(shape, move))  122 us
    pallas_call x3, Pallas kernels, attend_back(): pl.pallas_call(partial(bwd_kernel, tile=tile, sets=sets, zparts=zparts),...  61.6 us
    pallas_call x3, Pallas kernels, attend(): pl.pallas_call(partial(fwd_kernel, tile=tile), out_shape=(jax.ShapeDtypeS...  34.7 us
    ppermute x30, starting transfers between devices, send(): return lax.ppermute(x, AXES, pairs_of(shape, move))  28.7 us
    all_to_all x2, waiting for transfers between devices, scatter_tokens(): return lax.all_to_all(four, 'ctx', 0, 0, tiled=True).reshape(rows, d)  26.3 us
    pallas_call x1, Pallas kernels, mlp(): pl.pallas_call(mlp_kernel, out_shape=(jax.ShapeDtypeStruct((rows, d), bf1...  24.6 us
    pallas_call x1, Pallas kernels, wgrad(): pl.pallas_call(partial(wgrad_kernel, per=per), out_shape=jax.ShapeDtypeSt...  21.4 us
    pallas_call x1, Pallas kernels, close(): pl.pallas_call(partial(close_kernel, heads=heads), out_shape=(jax.ShapeDt...  18.2 us
  transfers between devices with their start and end apart: 36, of which 19 were waited for; matrix products, arithmetic and copies ran while one was open for 17% of the time, Pallas kernels for 25%

profile of v1, /device:TPU:8, one launch (start us, length us, event | category | flops | bytes accessed | tf_op | source)
XLA Modules:
  0.0 496.3 jit_solution(5167830332955828836)
XLA Ops:
  7.2 1.8 pad_maximum_fusion.8
  10.4 1.8 collective-permute-done
  13.2 5.3 %all-to-all-start = ((bf16[4,144,768]{2,1,0:T(8,128)(2,1)}), bf16[4,144,768]{2,1,0:T(8,128)(2,1)S(1)}, u32[]{:S(2)}, u32[]{:S(2)}) async-start(bf16[4,144,768]{2,1,0:T(8,128)(2,1)} %maximum_select_fusion.3), calls=%async_computation | async-start | bytes 1769472 | tf_op jit(solution)/shard_map/all_to_all | solution.py:562
  18.5 26.3 %all-to-all-done = bf16[4,144,768]{2,1,0:T(8,128)(2,1)S(1)} async-done(((bf16[4,144,768]{2,1,0:T(8,128)(2,1)}), bf16[4,144,768]{2,1,0:T(8,128)(2,1)S(1)}, u32[]{:S(2)}, u32[]{:S(2)}) %all-to-all-start) | async-done | bytes 884768 | tf_op jit(solution)/shard_map/all_to_all | solution.py:562
  48.3 23.1 %collective-permute-done.1 = bf16[576,768]{1,0:T(8,128)(2,1)S(1)} collective-permute-done((bf16[576,768]{1,0:T(8,128)(2,1)S(1)}, bf16[576,768]{1,0:T(8,128)(2,1)S(1)}, u32[]{:S(2)}, u32[]{:S(2)}) %collective-permute-start.1) | collective-permute-done | bytes 884768 | tf_op jit(solution)/shard_map/ppermute | solution.py:539
  77.0 2.5 collective-permute-start.4
  79.9 12.9 %collective-permute-done.4 = bf16[1,2,3,48,192]{4,3,2,1,0:T(8,128)(2,1)S(1)} collective-permute-done((bf16[1,2,3,48,192]{4,3,2,1,0:T(8,128)(2,1)S(1)}, bf16[1,2,3,48,192]{4,3,2,1,0:T(8,128)(2,1)S(1)}, u32[]{:S(2)}, u32[]{:S(2)}) %collective-permute-start.4) | collective-permute-done | bytes 110624 | tf_op jit(solution)/shard_map/ppermute | solution.py:539
  92.8 3.0 collective-permute-start.5
  96.6 21.8 %collective-permute-done.5 = bf16[2,2,3,48,192]{4,3,2,1,0:T(8,128)(2,1)S(1)} collective-permute-done((bf16[2,2,3,48,192]{4,3,2,1,0:T(8,128)(2,1)S(1)}, bf16[2,2,3,48,192]{4,3,2,1,0:T(8,128)(2,1)S(1)}, u32[]{:S(2)}, u32[]{:S(2)}) %collective-permute-start.5) | collective-permute-done | bytes 221216 | tf_op jit(solution)/shard_map/ppermute | solution.py:539
  125.1 7.5 %all-to-all-start.1 = ((bf16[4,144,768]{2,1,0:T(8,128)(2,1)}), bf16[4,144,768]{2,1,0:T(8,128)(2,1)}, u32[]{:S(2)}, u32[]{:S(2)}) async-start(bf16[4,144,768]{2,1,0:T(8,128)(2,1)} %maximum_select_fusion.4), calls=%async_computation.1 | async-start | bytes 1769472 | tf_op jit(solution)/shard_map/all_to_all | solution.py:562
  135.3 3.2 copy.56
  138.5 3.0 reshape.578
  142.9 2.2 copy.57.w_ref
  146.8 2.0 pad_maximum_fusion.x_ref
  148.8 11.8 %prep.1 = (bf16[3,2304,256]{2,1,0:T(8,128)(2,1)}, bf16[3,2304,256]{2,1,0:T(8,128)(2,1)}, bf16[3,2304,128]{2,1,0:T(8,128)(2,1)}) custom-call(s32[4]{0:T(128)} %iota_xor_fusion.order_ref, bf16[4,576,768]{2,1,0:T(8,128)(2,1)} %pad_maximum_fusion.x_ref, bf16[768,1152]{1,0:T(8,128)(2,1)} %copy.57.w_ref, f32[1,1152]{1,0:T(1,128)} %reshape.608.b_ref, ...), custom_call_target="tpu_custom_call" | custom-call | flops 4076863488 | bytes 12386304 | tf_op jit(solution)/shard_map/prep/pallas_call | solution.py:76
  160.5 11.4 %attend.3 = (f32[1,2304,128]{2,1,0:T(8,128)}, bf16[1,2304,64]{2,1,0:T(8,128)(2,1)}, bf16[1,2304,256]{2,1,0:T(8,128)(2,1)}) custom-call(bf16[3,2304,256]{2,1,0:T(8,128)(2,1)} %get-tuple-element.52.q_ref, bf16[3,2304,256]{2,1,0:T(8,128)(2,1)} %get-tuple-element.53.k_ref, bf16[3,2304,128]{2,1,0:T(8,128)(2,1)} %get-tuple-element.54.v_ref), custom_call_target="tpu_custom_call" | custom-call | flops 5435817984 | bytes 4608000 | tf_op jit(solution)/shard_map/attend/pallas_call | solution.py:131
  173.2 11.4 %attend.4 = (f32[1,2304,128]{2,1,0:T(8,128)}, bf16[1,2304,64]{2,1,0:T(8,128)(2,1)}, bf16[1,2304,256]{2,1,0:T(8,128)(2,1)}) custom-call(bf16[3,2304,256]{2,1,0:T(8,128)(2,1)} %get-tuple-element.52.q_ref, bf16[3,2304,256]{2,1,0:T(8,128)(2,1)} %get-tuple-element.53.k_ref, bf16[3,2304,128]{2,1,0:T(8,128)(2,1)} %get-tuple-element.54.v_ref), custom_call_target="tpu_custom_call" | custom-call | flops 5435817984 | bytes 4608000 | tf_op jit(solution)/shard_map/attend/pallas_call | solution.py:131
  186.0 11.9 %attend.5 = (f32[1,2304,128]{2,1,0:T(8,128)}, bf16[1,2304,64]{2,1,0:T(8,128)(2,1)}, bf16[1,2304,256]{2,1,0:T(8,128)(2,1)}) custom-call(bf16[3,2304,256]{2,1,0:T(8,128)(2,1)} %get-tuple-element.52.q_ref, bf16[3,2304,256]{2,1,0:T(8,128)(2,1)} %get-tuple-element.53.k_ref, bf16[3,2304,128]{2,1,0:T(8,128)(2,1)} %get-tuple-element.54.v_ref), custom_call_target="tpu_custom_call" | custom-call | flops 5435817984 | bytes 4608000 | tf_op jit(solution)/shard_map/attend/pallas_call | solution.py:131
  202.0 6.3 %collective-permute-done.8 = bf16[576,192]{0,1:T(8,128)(2,1)S(1)} collective-permute-done((bf16[576,192]{0,1:T(8,128)(2,1)S(1)}, bf16[576,192]{0,1:T(8,128)(2,1)S(1)}, u32[]{:S(2)}, u32[]{:S(2)}) %collective-permute-start.8) | collective-permute-done | bytes 221216 | tf_op jit(solution)/shard_map/ppermute | solution.py:539
  208.3 4.4 collective-permute-done.9
  214.5 24.6 %mlp.1 = (bf16[576,768]{1,0:T(8,128)(2,1)}, bf16[576,3072]{1,0:T(8,128)(2,1)}, bf16[576,3072]{1,0:T(8,128)(2,1)}, bf16[576,768]{1,0:T(8,128)(2,1)}, f32[576,768]...) custom-call(bf16[576,768]{1,0:T(8,128)(2,1)} %copy.61.mix_ref, ...), custom_call_target="tpu_custom_call" | custom-call | flops 12230590464 | bytes 18284544 | tf_op jit(solution)/shard_map/mlp/pallas_call | solution.py:335
  239.0 21.4 %wgrad.1 = bf16[16,2,48,3456]{3,2,1,0:T(8,128)(2,1)} custom-call(bf16[576,768]{1,0:T(8,128)(2,1)} %get-tuple-element.84.n2_ref, bf16[576,768]{1,0:T(8,128)(2,1)} %bitcast.29.top_ref, bf16[576,768]{1,0:T(8,128)(2,1)} %get-tuple-element.85.br_ref, bf16[576,3072]{1,0:T(8,128)(2,1)} %get-tuple-element.86.hg_ref, bf16[576,3072]{1,0:T(8,128)(2,1)} %get-tuple-element.87.act_ref, ...), custom_call_target="tpu_custom_call" | custom-call | flops 6115295232 | bytes 23592960 | tf_op jit(solution)/shard_map/wgrad/pallas_call | solution.py:416
  264.3 7.2 %collective-permute-done.15 = bf16[576,192]{0,1:T(8,128)(2,1)S(1)} collective-permute-done((bf16[576,192]{0,1:T(8,128)(2,1)S(1)}, bf16[576,192]{0,1:T(8,128)(2,1)S(1)}, u32[]{:S(2)}, u32[]{:S(2)}) %collective-permute-start.15) | collective-permute-done | bytes 221216 | tf_op jit(solution)/shard_map/ppermute | solution.py:539
  271.4 3.9 collective-permute-done.16
  279.6 20.6 %attend_back.5 = (bf16[1,2304,128]{2,1,0:T(8,128)(2,1)}, bf16[1,2304,128]{2,1,0:T(8,128)(2,1)}, bf16[1,2304,128]{2,1,0:T(8,128)(2,1)}, bf16[1,2304,256]{2,1,0:T(8,128)(2,1)}) custom-call(bf16[1,2304,256]{2,1,0:T(8,128)(2,1)} %get-tuple-element.67.q_ref, bf16[3,2304,256]{2,1,0:T(8,128)(2,1)} %get-tuple-element.53.k_ref, ...), custom_call_target="tpu_custom_call" | custom-call | flops 13589544960 | bytes 6912000 | tf_op jit(solution)/shard_map/attend_back/pallas_call | solution.py:213
  300.2 20.4 %attend_back.4 = (bf16[1,2304,128]{2,1,0:T(8,128)(2,1)}, bf16[1,2304,128]{2,1,0:T(8,128)(2,1)}, bf16[1,2304,128]{2,1,0:T(8,128)(2,1)}, bf16[1,2304,256]{2,1,0:T(8,128)(2,1)}) custom-call(bf16[1,2304,256]{2,1,0:T(8,128)(2,1)} %get-tuple-element.64.q_ref, bf16[3,2304,256]{2,1,0:T(8,128)(2,1)} %get-tuple-element.53.k_ref, ...), custom_call_target="tpu_custom_call" | custom-call | flops 13589544960 | bytes 6912000 | tf_op jit(solution)/shard_map/attend_back/pallas_call | solution.py:213
  320.6 20.6 %attend_back.3 = (bf16[1,2304,128]{2,1,0:T(8,128)(2,1)}, bf16[1,2304,128]{2,1,0:T(8,128)(2,1)}, bf16[1,2304,128]{2,1,0:T(8,128)(2,1)}, bf16[1,2304,256]{2,1,0:T(8,128)(2,1)}) custom-call(bf16[1,2304,256]{2,1,0:T(8,128)(2,1)} %get-tuple-element.60.q_ref, bf16[3,2304,256]{2,1,0:T(8,128)(2,1)} %get-tuple-element.53.k_ref, ...), custom_call_target="tpu_custom_call" | custom-call | flops 13589544960 | bytes 6912000 | tf_op jit(solution)/shard_map/attend_back/pallas_call | solution.py:213
  341.2 18.2 %close.1 = (bf16[4,576,768]{2,1,0:T(8,128)(2,1)}, bf16[768,1152]{1,0:T(8,128)(2,1)}, f32[1,1152]{1,0:T(1,128)}) custom-call(s32[4]{0:T(128)} %iota_xor_fusion.order_ref, bf16[4,576,768]{2,1,0:T(8,128)(2,1)} %pad_maximum_fusion.x_ref, bf16[768,1152]{1,0:T(8,128)(2,1)} %copy.57.w_ref, bf16[1,2304,128]{2,1,0:T(8,128)(2,1)} %get-tuple-element.63.refs_0_, ...), custom_call_target="tpu_custom_call" | custom-call | flops 8153726976 | bytes 12386304 | tf_op jit(solution)/shard_map/close/pallas_call | solution.py:462
  363.8 6.6 %all-to-all-start.2 = ((bf16[4,144,768]{2,1,0:T(8,128)(2,1)}), bf16[4,144,768]{2,1,0:T(8,128)(2,1)S(1)}, u32[]{:S(2)}, u32[]{:S(2)}) async-start(bf16[4,144,768]{2,1,0:T(8,128)(2,1)} %bitcast.31), calls=%async_computation.2 | async-start | bytes 1769472 | tf_op jit(solution)/shard_map/all_to_all | solution.py:565
  370.4 3.3 reshape.599
  373.7 3.2 reshape.616
  376.9 2.0 constant_dynamic-slice_fusion.6
  386.5 1.8 fusion.7
  389.7 5.5 %collective-permute-done.26 = bf16[4,2,3,48,192]{4,3,2,0,1:T(8,128)(2,1)S(1)} collective-permute-done((bf16[4,2,3,48,192]{4,3,2,0,1:T(8,128)(2,1)}, bf16[4,2,3,48,192]{4,3,2,0,1:T(8,128)(2,1)S(1)}, u32[]{:S(2)}, u32[]{:S(2)}) %collective-permute-start.26) | collective-permute-done | bytes 442400 | tf_op jit(solution)/shard_map/ppermute | solution.py:539
  395.4 2.7 fusion.20
  399.7 2.4 collective-permute-start.27
  403.7 17.3 %collective-permute-done.27 = bf16[2,2,3,48,192]{4,3,2,1,0:T(8,128)(2,1)S(1)} collective-permute-done((bf16[2,2,3,48,192]{4,3,2,1,0:T(8,128)(2,1)S(1)}, bf16[2,2,3,48,192]{4,3,2,1,0:T(8,128)(2,1)S(1)}, u32[]{:S(2)}, u32[]{:S(2)}) %collective-permute-start.27) | collective-permute-done | bytes 221216 | tf_op jit(solution)/shard_map/ppermute | solution.py:539
  424.3 2.8 multiply_reduce_fusion
  427.2 3.3 add_convert_fusion
  430.4 5.2 %all-to-all-start.3 = ((bf16[4,144,768]{2,1,0:T(8,128)(2,1)}), bf16[4,144,768]{2,1,0:T(8,128)(2,1)S(1)}, u32[]{:S(2)}, u32[]{:S(2)}) async-start(bf16[4,144,768]{2,1,0:T(8,128)(2,1)} %bitcast.48), calls=%async_computation.3 | async-start | bytes 1769472 | tf_op jit(solution)/shard_map/all_to_all | solution.py:565
  439.6 15.6 %all-to-all-done.3 = bf16[4,144,768]{2,1,0:T(8,128)(2,1)S(1)} async-done(((bf16[4,144,768]{2,1,0:T(8,128)(2,1)}), bf16[4,144,768]{2,1,0:T(8,128)(2,1)S(1)}, u32[]{:S(2)}, u32[]{:S(2)}) %all-to-all-start.3) | async-done | bytes 884768 | tf_op jit(solution)/shard_map/all_to_all | solution.py:565
  456.0 6.5 %collective-permute-done.22 = f32[200,128]{1,0:T(8,128)S(1)} collective-permute-done((f32[200,128]{1,0:T(8,128)S(1)}, f32[200,128]{1,0:T(8,128)S(1)}, u32[]{:S(2)}, u32[]{:S(2)}) %collective-permute-start.22) | collective-permute-done | bytes 102432 | tf_op jit(solution)/shard_map/ppermute | solution.py:539
  463.9 3.4 collective-permute-done.23
  470.0 2.1 collective-permute-done.24
  472.1 2.4 collective-permute-start.25
  476.0 1.8 collective-permute-done.25
  481.3 2.5 collective-permute-done.20
  483.8 3.0 maximum_select_fusion.1
  (223 shorter events, 77.3 us)
Async XLA Ops:
  7.2 207.3 %all-gather.3.cloned.1.call-start = ((), (), s32[]{:S(2)}) async-start(), calls=%async_computation.6 | async-start | bytes 10948608 | tf_op jit(solution)/shard_map/all_gather | solution.py:555
  10.3 1.9 collective-permute-start
  12.1 6.4 %copy-start.19 = (bf16[768]{0:T(1024)(128)(2,1)S(1)}, bf16[768]{0:T(1024)(128)(2,1)}, u32[]{:S(2)}) copy-start(bf16[768]{0:T(1024)(128)(2,1)} %param.20) | copy-start | bytes 4612
  13.2 31.7 %all-to-all-start = ((bf16[4,144,768]{2,1,0:T(8,128)(2,1)}), bf16[4,144,768]{2,1,0:T(8,128)(2,1)S(1)}, u32[]{:S(2)}, u32[]{:S(2)}) async-start(bf16[4,144,768]{2,1,0:T(8,128)(2,1)} %maximum_select_fusion.3), calls=%async_computation | async-start | bytes 1769472 | tf_op jit(solution)/shard_map/all_to_all | solution.py:562
  18.5 29.2 %copy-start.11 = (bf16[3,48,384]{2,1,0:T(8,128)(2,1)S(1)}, bf16[3,48,384]{2,1,0:T(8,128)(2,1)}, u32[]{:S(2)}) copy-start(bf16[3,48,384]{2,1,0:T(8,128)(2,1)} %param.21) | copy-start | bytes 331780
  46.1 25.3 %collective-permute-start.1 = (bf16[576,768]{1,0:T(8,128)(2,1)S(1)}, bf16[576,768]{1,0:T(8,128)(2,1)S(1)}, u32[]{:S(2)}, u32[]{:S(2)}) collective-permute-start(bf16[576,768]{1,0:T(8,128)(2,1)S(1)} %add_convert_fusion.2), channel_id=1, source_target_pairs={{0,1},{1,0},{2,3},{3,2},{4,5},{5,4},{6,7},{7,6},{8,9},{9,8},{10,11... | collective-permute-start | bytes 2654216 | tf_op jit(solution)/shard_map/ppermute | solution.py:539
  73.0 6.6 %copy-start.14 = (bf16[95,64]{0,1:T(8,128)(2,1)S(1)}, bf16[95,64]{0,1:T(8,128)(2,1)}, u32[]{:S(2)}) copy-start(bf16[95,64]{0,1:T(8,128)(2,1)} %param.23) | copy-start | bytes 36484
  73.0 6.7 %copy-start.12 = (bf16[95,64]{0,1:T(8,128)(2,1)S(1)}, bf16[95,64]{0,1:T(8,128)(2,1)}, u32[]{:S(2)}) copy-start(bf16[95,64]{0,1:T(8,128)(2,1)} %param.24) | copy-start | bytes 36484
  73.0 6.8 %copy-start.20 = (bf16[768]{0:T(1024)(128)(2,1)S(1)}, bf16[768]{0:T(1024)(128)(2,1)}, u32[]{:S(2)}) copy-start(bf16[768]{0:T(1024)(128)(2,1)} %param.26) | copy-start | bytes 4612
  73.0 6.8 %copy-start.21 = (bf16[768]{0:T(1024)(128)(2,1)S(1)}, bf16[768]{0:T(1024)(128)(2,1)}, u32[]{:S(2)}) copy-start(bf16[768]{0:T(1024)(128)(2,1)} %param.27) | copy-start | bytes 4612
  73.0 6.8 %copy-start.22 = (bf16[768]{0:T(1024)(128)(2,1)S(1)}, bf16[768]{0:T(1024)(128)(2,1)}, u32[]{:S(2)}) copy-start(bf16[768]{0:T(1024)(128)(2,1)} %param.28) | copy-start | bytes 4612
  73.0 6.8 %copy-start.23 = (bf16[768]{0:T(1024)(128)(2,1)S(1)}, bf16[768]{0:T(1024)(128)(2,1)}, u32[]{:S(2)}) copy-start(bf16[768]{0:T(1024)(128)(2,1)} %param.32) | copy-start | bytes 4612
  73.0 72.1 %collective-permute-start.2 = (bf16[2,576,768]{2,1,0:T(8,128)(2,1)}, bf16[2,576,768]{2,1,0:T(8,128)(2,1)}, u32[]{:S(2)}, u32[]{:S(2)}) collective-permute-start(bf16[2,576,768]{2,1,0:T(8,128)(2,1)} %pad_maximum_fusion.1), channel_id=1, source_target_pairs={{0,8},{1,9},{2,10},{3,11},{4,12},{5,13},{6,14},{7,15},{8,0},{9,1},... | collective-permute-start | bytes 5308424 | tf_op jit(solution)/shard_map/ppermute | solution.py:539
  73.4 3.5 collective-permute-start.3
  74.1 50.0 %collective-permute-start.10 = (bf16[2,144,768]{2,1,0:T(8,128)(2,1)S(1)}, bf16[2,144,768]{2,1,0:T(8,128)(2,1)S(1)}, u32[]{:S(2)}, u32[]{:S(2)}) collective-permute-start(bf16[2,144,768]{2,1,0:T(8,128)(2,1)S(1)} %get-tuple-element.130), channel_id=1, source_target_pairs={{0,8},{1,9},{2,10},{3,11},{4,12},{5,13},{6,14},{7,15},{8,0},{9,1},... | collective-permute-start | bytes 1327112 | tf_op jit(solution)/shard_map/ppermute | solution.py:539
  74.1 49.3 %collective-permute-start.11 = (bf16[1536]{0:T(1024)(128)(2,1)}, bf16[1536]{0:T(1024)(128)(2,1)}, u32[]{:S(2)}, u32[]{:S(2)}) collective-permute-start(bf16[1536]{0:T(1024)(128)(2,1)} %param.30), channel_id=1, source_target_pairs={{0,1},{1,0},{2,3},{3,2},{4,5},{5,4},{6,7},{7,6},{8,9},{9,8},{10,11... | collective-permute-start | bytes 9224 | tf_op jit(solution)/shard_map/ppermute | solution.py:539
  77.0 15.7 %collective-permute-start.4 = (bf16[1,2,3,48,192]{4,3,2,1,0:T(8,128)(2,1)S(1)}, bf16[1,2,3,48,192]{4,3,2,1,0:T(8,128)(2,1)S(1)}, u32[]{:S(2)}, u32[]{:S(2)}) collective-permute-start(bf16[1,2,3,48,192]{4,3,2,1,0:T(8,128)(2,1)S(1)} %maximum_select_fusion.9), channel_id=1, source_target_pairs={{0,2},{1,3},{2,0},{3,1},{4,6},{5,7},{6,4},{7,5},{8,10},{9,11},{10,... | collective-permute-start | bytes 331784 | tf_op jit(solution)/shard_map/ppermute | solution.py:539
  92.8 25.5 %collective-permute-start.5 = (bf16[2,2,3,48,192]{4,3,2,1,0:T(8,128)(2,1)S(1)}, bf16[2,2,3,48,192]{4,3,2,1,0:T(8,128)(2,1)S(1)}, u32[]{:S(2)}, u32[]{:S(2)}) collective-permute-start(bf16[2,2,3,48,192]{4,3,2,1,0:T(8,128)(2,1)S(1)} %maximum_select_fusion.8), channel_id=1, source_target_pairs={{0,4},{1,5},{2,6},{3,7},{4,0},{5,1},{6,2},{7,3},{8,12},{9,13},{10,... | collective-permute-start | bytes 663560 | tf_op jit(solution)/shard_map/ppermute | solution.py:539
  118.6 15.3 %collective-permute-start.6 = (bf16[1,4,2,3,48,192]{5,4,3,2,1,0:T(8,128)(2,1)S(1)}, bf16[1,4,2,3,48,192]{5,4,3,2,1,0:T(8,128)(2,1)S(1)}, u32[]{:S(2)}, u32[]{:S(2)}) collective-permute-start(bf16[1,4,2,3,48,192]{5,4,3,2,1,0:T(8,128)(2,1)S(1)} %maximum_select_fusion.7), channel_id=1, source_target_pairs={{0,16},{1,17},{2,18},{3,19},{4,20},{5,21},{6,22},{7,23},{8,24},{9,... | collective-permute-start | bytes 1327112 | tf_op jit(solution)/shard_map/ppermute | solution.py:539
  125.1 89.3 %all-to-all-start.1 = ((bf16[4,144,768]{2,1,0:T(8,128)(2,1)}), bf16[4,144,768]{2,1,0:T(8,128)(2,1)}, u32[]{:S(2)}, u32[]{:S(2)}) async-start(bf16[4,144,768]{2,1,0:T(8,128)(2,1)} %maximum_select_fusion.4), calls=%async_computation.1 | async-start | bytes 1769472 | tf_op jit(solution)/shard_map/all_to_all | solution.py:562
  132.7 354.1 %reduce-scatter.2.cloned.1.call-start = ((), (), s32[]{:S(2)}) async-start(), calls=%async_computation.5 | async-start | bytes 10948608 | tf_op jit(solution)/shard_map/reduce_scatter | solution.py:625
  199.4 2.6 collective-permute-start.7
  199.5 8.8 %collective-permute-start.8 = (bf16[576,192]{0,1:T(8,128)(2,1)S(1)}, bf16[576,192]{0,1:T(8,128)(2,1)S(1)}, u32[]{:S(2)}, u32[]{:S(2)}) collective-permute-start(bf16[576,192]{0,1:T(8,128)(2,1)S(1)} %get-tuple-element.151), channel_id=1, source_target_pairs={{0,1},{1,0},{2,3},{3,2},{4,5},{5,4},{6,7},{7,6},{8,9},{9,8},{10,11... | collective-permute-start | bytes 663560 | tf_op jit(solution)/shard_map/ppermute | solution.py:539
  201.1 11.5 %collective-permute-start.9 = (bf16[576,192]{0,1:T(8,128)(2,1)S(1)}, bf16[576,192]{0,1:T(8,128)(2,1)S(1)}, u32[]{:S(2)}, u32[]{:S(2)}) collective-permute-start(bf16[576,192]{0,1:T(8,128)(2,1)S(1)} %get-tuple-element.150), channel_id=1, source_target_pairs={{0,9},{1,8},{2,11},{3,10},{4,13},{5,12},{6,15},{7,14},{8,1},{9,0},... | collective-permute-start | bytes 663560 | tf_op jit(solution)/shard_map/ppermute | solution.py:539
  262.3 2.0 collective-permute-start.14
  262.7 8.8 %collective-permute-start.15 = (bf16[576,192]{0,1:T(8,128)(2,1)S(1)}, bf16[576,192]{0,1:T(8,128)(2,1)S(1)}, u32[]{:S(2)}, u32[]{:S(2)}) collective-permute-start(bf16[576,192]{0,1:T(8,128)(2,1)S(1)} %get-tuple-element.143), channel_id=1, source_target_pairs={{0,1},{1,0},{2,3},{3,2},{4,5},{5,4},{6,7},{7,6},{8,9},{9,8},{10,11... | collective-permute-start | bytes 663560 | tf_op jit(solution)/shard_map/ppermute | solution.py:539
  264.2 11.1 %collective-permute-start.16 = (bf16[576,192]{0,1:T(8,128)(2,1)S(1)}, bf16[576,192]{0,1:T(8,128)(2,1)S(1)}, u32[]{:S(2)}, u32[]{:S(2)}) collective-permute-start(bf16[576,192]{0,1:T(8,128)(2,1)S(1)} %get-tuple-element.142), channel_id=1, source_target_pairs={{0,9},{1,8},{2,11},{3,10},{4,13},{5,12},{6,15},{7,14},{8,1},{9,0},... | collective-permute-start | bytes 663560 | tf_op jit(solution)/shard_map/ppermute | solution.py:539
  362.3 33.0 %collective-permute-start.17 = (bf16[2,576,768]{2,1,0:T(8,128)(2,1)}, bf16[2,576,768]{2,1,0:T(8,128)(2,1)}, u32[]{:S(2)}, u32[]{:S(2)}) collective-permute-start(bf16[2,576,768]{2,1,0:T(8,128)(2,1)} %pad_maximum_fusion.2), channel_id=1, source_target_pairs={{0,8},{1,9},{2,10},{3,11},{4,12},{5,13},{6,14},{7,15},{8,0},{9,1},... | collective-permute-start | bytes 5308424 | tf_op jit(solution)/shard_map/ppermute | solution.py:539
  363.8 59.6 %all-to-all-start.2 = ((bf16[4,144,768]{2,1,0:T(8,128)(2,1)}), bf16[4,144,768]{2,1,0:T(8,128)(2,1)S(1)}, u32[]{:S(2)}, u32[]{:S(2)}) async-start(bf16[4,144,768]{2,1,0:T(8,128)(2,1)} %bitcast.31), calls=%async_computation.2 | async-start | bytes 1769472 | tf_op jit(solution)/shard_map/all_to_all | solution.py:565
  378.9 9.4 %copy-start.6 = (bf16[1,2304,256]{2,1,0:T(8,128)(2,1)S(1)}, bf16[1,2304,256]{2,1,0:T(8,128)(2,1)}, u32[]{:S(2)}) copy-start(bf16[1,2304,256]{2,1,0:T(8,128)(2,1)} %get-tuple-element.82) | copy-start | bytes 3538948
  379.8 15.3 %collective-permute-start.26 = (bf16[4,2,3,48,192]{4,3,2,0,1:T(8,128)(2,1)}, bf16[4,2,3,48,192]{4,3,2,0,1:T(8,128)(2,1)S(1)}, u32[]{:S(2)}, u32[]{:S(2)}) collective-permute-start(bf16[4,2,3,48,192]{4,3,2,0,1:T(8,128)(2,1)} %bitcast.171), channel_id=1, source_target_pairs={{0,16},{1,17},{2,18},{3,19},{4,20},{5,21},{6,22},{7,23},{8,24},{9,... | collective-permute-start | bytes 1327112 | tf_op jit(solution)/shard_map/ppermute | solution.py:539
  395.3 6.8 %copy-start.7 = (bf16[1,2304,256]{2,1,0:T(8,128)(2,1)S(1)}, bf16[1,2304,256]{2,1,0:T(8,128)(2,1)}, u32[]{:S(2)}) copy-start(bf16[1,2304,256]{2,1,0:T(8,128)(2,1)} %get-tuple-element.80) | copy-start | bytes 3538948
  398.0 26.3 %collective-permute-start.18 = (bf16[576,768]{1,0:T(8,128)(2,1)}, bf16[576,768]{1,0:T(8,128)(2,1)S(1)}, u32[]{:S(2)}, u32[]{:S(2)}) collective-permute-start(bf16[576,768]{1,0:T(8,128)(2,1)} %fusion.20), channel_id=1, source_target_pairs={{0,1},{1,0},{2,3},{3,2},{4,5},{5,4},{6,7},{7,6},{8,9},{9,8},{10,11... | collective-permute-start | bytes 2654216 | tf_op jit(solution)/shard_map/ppermute | solution.py:539
  399.7 21.3 %collective-permute-start.27 = (bf16[2,2,3,48,192]{4,3,2,1,0:T(8,128)(2,1)S(1)}, bf16[2,2,3,48,192]{4,3,2,1,0:T(8,128)(2,1)S(1)}, u32[]{:S(2)}, u32[]{:S(2)}) collective-permute-start(bf16[2,2,3,48,192]{4,3,2,1,0:T(8,128)(2,1)S(1)} %fusion.27), channel_id=1, source_target_pairs={{0,4},{1,5},{2,6},{3,7},{4,0},{5,1},{6,2},{7,3},{8,12},{9,13},{10,... | collective-permute-start | bytes 663560 | tf_op jit(solution)/shard_map/ppermute | solution.py:539
  403.6 20.7 %copy-start.1 = (bf16[4,144,768]{2,1,0:T(8,128)(2,1)S(1)}, bf16[4,144,768]{2,1,0:T(8,128)(2,1)}, u32[]{:S(2)}) copy-start(bf16[4,144,768]{2,1,0:T(8,128)(2,1)} %copy-done) | copy-start | bytes 2654212
  421.7 15.0 %collective-permute-start.28 = (bf16[1,2,3,48,192]{4,3,2,1,0:T(8,128)(2,1)}, bf16[1,2,3,48,192]{4,3,2,1,0:T(8,128)(2,1)}, u32[]{:S(2)}, u32[]{:S(2)}) collective-permute-start(bf16[1,2,3,48,192]{4,3,2,1,0:T(8,128)(2,1)} %dynamic-slice_convert_fusion), channel_id=1, source_target_pairs={{0,2},{1,3},{2,0},{3,1},{4,6},{5,7},{6,4},{7,5},{8,10},{9,11},{10,... | collective-permute-start | bytes 331784 | tf_op jit(solution)/shard_map/ppermute | solution.py:539
  424.3 13.3 %collective-permute-start.12 = (bf16[2,1,144,768]{3,2,1,0:T(8,128)(2,1)}, bf16[2,1,144,768]{3,2,1,0:T(8,128)(2,1)}, u32[]{:S(2)}, u32[]{:S(2)}) collective-permute-start(bf16[2,1,144,768]{3,2,1,0:T(8,128)(2,1)} %get-tuple-element.156), channel_id=1, source_target_pairs={{0,8},{1,9},{2,10},{3,11},{4,12},{5,13},{6,14},{7,15},{8,0},{9,1},... | collective-permute-start | bytes 1327112 | tf_op jit(solution)/shard_map/ppermute | solution.py:539
  430.4 7.2 %copy-start.4 = (bf16[2,1,144,768]{3,2,1,0:T(8,128)(2,1)S(1)}, bf16[2,1,144,768]{3,2,1,0:T(8,128)(2,1)}, u32[]{:S(2)}) copy-start(bf16[2,1,144,768]{3,2,1,0:T(8,128)(2,1)} %get-tuple-element.155) | copy-start | bytes 1327108
  430.4 24.7 %all-to-all-start.3 = ((bf16[4,144,768]{2,1,0:T(8,128)(2,1)}), bf16[4,144,768]{2,1,0:T(8,128)(2,1)S(1)}, u32[]{:S(2)}, u32[]{:S(2)}) async-start(bf16[4,144,768]{2,1,0:T(8,128)(2,1)} %bitcast.48), calls=%async_computation.3 | async-start | bytes 1769472 | tf_op jit(solution)/shard_map/all_to_all | solution.py:565
  439.0 35.6 %collective-permute-start.13 = (bf16[2,2,144,768]{3,2,1,0:T(8,128)(2,1)S(1)}, bf16[2,2,144,768]{3,2,1,0:T(8,128)(2,1)S(1)}, u32[]{:S(2)}, u32[]{:S(2)}) collective-permute-start(bf16[2,2,144,768]{3,2,1,0:T(8,128)(2,1)S(1)} %maximum_select_fusion.5), channel_id=1, source_target_pairs={{0,1},{1,0},{2,3},{3,2},{4,5},{5,4},{6,7},{7,6},{8,9},{9,8},{10,11... | collective-permute-start | bytes 2654216 | tf_op jit(solution)/shard_map/ppermute | solution.py:539
  439.5 15.8 %collective-permute-start.21 = (f32[200,128]{1,0:T(8,128)S(1)}, f32[200,128]{1,0:T(8,128)S(1)}, u32[]{:S(2)}, u32[]{:S(2)}) collective-permute-start(f32[200,128]{1,0:T(8,128)S(1)} %bitcast.200), channel_id=1, source_target_pairs={{0,8},{1,9},{2,10},{3,11},{4,12},{5,13},{6,14},{7,15},{8,0},{9,1},... | collective-permute-start | bytes 307208 | tf_op jit(solution)/shard_map/ppermute | solution.py:539
  455.2 8.1 %collective-permute-start.19 = (bf16[2,1,144,768]{3,2,1,0:T(8,128)(2,1)S(1)}, bf16[2,1,144,768]{3,2,1,0:T(8,128)(2,1)S(1)}, u32[]{:S(2)}, u32[]{:S(2)}) collective-permute-start(bf16[2,1,144,768]{3,2,1,0:T(8,128)(2,1)S(1)} %get-tuple-element.154), channel_id=1, source_target_pairs={{0,8},{1,9},{2,10},{3,11},{4,12},{5,13},{6,14},{7,15},{8,0},{9,1},... | collective-permute-start | bytes 1327112 | tf_op jit(solution)/shard_map/ppermute | solution.py:539
  455.3 7.2 %collective-permute-start.22 = (f32[200,128]{1,0:T(8,128)S(1)}, f32[200,128]{1,0:T(8,128)S(1)}, u32[]{:S(2)}, u32[]{:S(2)}) collective-permute-start(f32[200,128]{1,0:T(8,128)S(1)} %bitcast_add_fusion.3), channel_id=1, source_target_pairs={{0,1},{1,0},{2,3},{3,2},{4,5},{5,4},{6,7},{7,6},{8,9},{9,8},{10,11... | collective-permute-start | bytes 307208 | tf_op jit(solution)/shard_map/ppermute | solution.py:539
  455.8 13.0 %collective-permute-start.29 = (bf16[3,48,192]{2,1,0:T(8,128)(2,1)S(1)}, bf16[3,48,192]{2,1,0:T(8,128)(2,1)S(1)}, u32[]{:S(2)}, u32[]{:S(2)}) collective-permute-start(bf16[3,48,192]{2,1,0:T(8,128)(2,1)S(1)} %get-tuple-element.160), channel_id=1, source_target_pairs={{0,8},{1,9},{2,10},{3,11},{4,12},{5,13},{6,14},{7,15},{8,0},{9,1},... | collective-permute-start | bytes 165896 | tf_op jit(solution)/shard_map/ppermute | solution.py:539
  462.6 4.7 collective-permute-start.23
  463.4 20.4 %collective-permute-start.20 = (bf16[2,2,144,768]{3,2,1,0:T(8,128)(2,1)S(1)}, bf16[2,2,144,768]{3,2,1,0:T(8,128)(2,1)}, u32[]{:S(2)}, u32[]{:S(2)}) collective-permute-start(bf16[2,2,144,768]{3,2,1,0:T(8,128)(2,1)S(1)} %maximum_select_fusion.6), channel_id=1, source_target_pairs={{0,1},{1,0},{2,3},{3,2},{4,5},{5,4},{6,7},{7,6},{8,9},{9,8},{10,11... | collective-permute-start | bytes 2654216 | tf_op jit(solution)/shard_map/ppermute | solution.py:539
  467.3 4.7 collective-permute-start.24
  472.1 5.7 %collective-permute-start.25 = (f32[200,128]{1,0:T(8,128)S(1)}, f32[200,128]{1,0:T(8,128)S(1)}, u32[]{:S(2)}, u32[]{:S(2)}) collective-permute-start(f32[200,128]{1,0:T(8,128)S(1)} %add.211), channel_id=1, source_target_pairs={{0,4},{1,5},{2,6},{3,7},{4,0},{5,1},{6,2},{7,3},{8,12},{9,13},{10,... | collective-permute-start | bytes 307208 | tf_op jit(solution)/shard_map/ppermute | solution.py:539
  (14 other events, 44.8 us)
Sparse Core Ops, SparseCore 0:
  10.9 106.5 all-gather.2
  260.6 160.2 reduce-scatter.1

commit v2 on v0

--- a/solution.py
+++ b/solution.py
@@ -2,7 +2,11 @@
 
 import jax
 import jax.numpy as jnp
+import ml_dtypes
+import numpy as np
 from jax import lax
+from jax.experimental import pallas as pl
+from jax.experimental.pallas import tpu as pltpu
 from jax.sharding import PartitionSpec as P
 
 G = 48
@@ -11,6 +15,817 @@
 
 eps = 1e-06
 highest = lax.Precision.HIGHEST
+bf16, f32 = jnp.bfloat16, jnp.float32
+VMEM_BYTES = 56 * 1024 * 1024
+NN = (((1,), (0,)), ((), ()))
+NT = (((1,), (1,)), ((), ()))
+TN = (((0,), (0,)), ((), ()))
+LH, LW = 64, 112
+ANY = pl.BlockSpec(memory_space=pl.ANY)
+PEAK = 1.0e15
+
+
+def mm(a, b, dims=NN):
+    return lax.dot_general(a, b, dims, preferred_element_type=f32)
+
+
+def roll(x, shift, stride=None):
+    extra = {} if stride is None else dict(stride=stride, stride_axis=0)
+    return pltpu.roll(x, shift, 1, **extra)
+
+
+def lane_iota(shape):
+    return lax.broadcasted_iota(jnp.int32, shape, 1)
+
+
+def struct(shape, dtype=bf16):
+    return jax.ShapeDtypeStruct(shape, dtype)
+
+
+def whole(shape):
+    return pl.BlockSpec(shape, lambda *_: (0,) * len(shape))
+
+
+def call(kernel, name, us, grid, prefetch, ins, in_specs, outs, out_specs, scratch=(), aliases=None):
+    return pl.pallas_call(
+        kernel,
+        out_shape=outs,
+        grid_spec=pltpu.PrefetchScalarGridSpec(
+            num_scalar_prefetch=1, grid=grid, in_specs=in_specs, out_specs=out_specs, scratch_shapes=list(scratch)
+        ),
+        input_output_aliases=aliases or {},
+        compiler_params=pltpu.CompilerParams(vmem_limit_bytes=VMEM_BYTES),
+        cost_estimate=pl.CostEstimate(flops=int(us * 1e-6 * PEAK), bytes_accessed=0, transcendentals=0),
+        name=name,
+    )(prefetch, *ins)
+
+
+def columns(w_ref, side):
+    width = w_ref.shape[2] // 2
+    parts = [jnp.where(side == 0, w_ref[j, :, :width], w_ref[j, :, width:]) for j in range(3)]
+    return jnp.concatenate([p[:, :128] for p in parts] + [p[:, 128:] for p in parts], axis=1)
+
+
+def pack_kernel(at_ref, image_ref, w_ref, out_ref):
+    rows = image_ref.shape[1]
+    depth = w_ref.shape[1]
+    out_ref[:rows] = image_ref[0]
+    out_ref[rows:] = jnp.zeros((depth, out_ref.shape[1]), bf16)
+    out_ref[rows:, :576] = columns(w_ref, 1 - at_ref[0])
+
+
+def pack(at, images, w):
+    batch, quarter, d = images.shape
+    rows = quarter // 2
+    out = (rows + w.shape[1], d)
+    return call(
+        pack_kernel, "pack", 2, (1,), at, [images, w],
+        [pl.BlockSpec((1, rows, d), lambda i, o: (o[1], 1 - o[0], 0)), whole(w.shape)], struct(out), whole(out),
+    )
+
+
+def route_kernel(at_ref, image_ref, got_ref, w_ref, ub_ref, qvb_ref, gain_ref, bias_ref, near_ref, normed_ref, far_ref, w_out_ref):
+    rows = image_ref.shape[1]
+    depth = w_ref.shape[1]
+    same = at_ref[0] == at_ref[2]
+    own, got = image_ref[0], got_ref[:rows]
+    near = jnp.where(same, own, got)
+    near_ref[...] = near
+    far_ref[...] = jnp.where(same, got, own)
+    normed_ref[...] = norm(near.astype(f32), gain_ref[...], bias_ref[...])[0].astype(bf16)
+    w_out_ref[...] = jnp.zeros(w_out_ref.shape, bf16)
+    w_out_ref[:depth, :576] = columns(w_ref, at_ref[0])
+    w_out_ref[depth:2 * depth] = got_ref[rows:]
+    d = image_ref.shape[2]
+    w_out_ref[2 * depth:2 * depth + 1] = ub_ref[:, :d]
+    w_out_ref[2 * depth + 1:2 * depth + 2] = ub_ref[:, d:]
+    w_out_ref[2 * depth + 2:2 * depth + 3] = qvb_ref[...]
+
+
+def route(at, images, got, w, up_bias, qv_bias, gain, bias):
+    batch, quarter, d = images.shape
+    rows = quarter // 2
+    half = (rows, d)
+    out = (2 * w.shape[1] + 16, d)
+    return call(
+        route_kernel, "route", 3, (1,), at, [images, got, w, up_bias, qv_bias, gain, bias],
+        [pl.BlockSpec((1, rows, d), lambda i, o: (o[1], o[0], 0))] + [whole(v.shape) for v in (got, w, up_bias, qv_bias, gain, bias)],
+        (struct(half), struct(half), struct(half), struct(out)), [whole(half)] * 3 + [whole(out)],
+    )
+
+
+def norm_kernel(_, x_ref, gain_ref, bias_ref, out_ref):
+    out_ref[...] = norm(x_ref[...].astype(f32), gain_ref[...], bias_ref[...])[0].astype(bf16)
+
+
+def norm_low(at, x, gain, bias):
+    return call(
+        norm_kernel, "norm_low", 1, (1,), at, [x, gain, bias], [whole(v.shape) for v in (x, gain, bias)], struct(x.shape), whole(x.shape)
+    )
+
+
+def arrange_kernel(me_ref, *refs):
+    pieces, out_ref = refs[:-1], refs[-1]
+    depth = pieces[0].shape[0] // 2
+    out_ref[:, 576:] = jnp.zeros((out_ref.shape[0], 64), bf16)
+    for dx in range(2):
+        for dz in range(4):
+            for dc in range(2):
+                ref, lo = (pieces[dz], dc) if dx == 0 else (pieces[4], dz * 2 + dc)
+                at = (dx * 8 + dc * 4 + dz) ^ me_ref[0]
+                out_ref[pl.ds(pl.multiple_of(at * depth, 16), depth), :576] = ref[lo * depth:(lo + 1) * depth]
+
+
+def arrange(me, pieces, rows):
+    return call(
+        arrange_kernel, "arrange", 2, (1,), me, pieces, [whole(p.shape) for p in pieces],
+        struct((rows, 640)), whole((rows, 640)),
+    )
+
+
+def prep_kernel(order_ref, *refs):
+    xs, refs = refs[:4], refs[4:]
+    w_ref, b_ref, tab_ref, hot_ref = refs[:4]
+    q_ref, k_ref, v_ref, n_ref = refs[-4:]
+    step = pl.program_id(0)
+    rows = q_ref.shape[1]
+
+    def work(x):
+        first_row = order_ref[4 + step]
+        n_ref[...] = x
+        qkv = (mm(x, w_ref[...]) + b_ref[...]).astype(bf16).astype(f32)
+        lane = lane_iota((G, 128))
+        lane_all = lane_iota((rows, 128))
+        hot_a = hot_ref[0, :, :128].astype(f32)
+        hot_b = hot_ref[0, :, 128:]
+        cols = [qkv[:, i * 128:(i + 1) * 128] for i in range(5)]
+        back = [roll(v, 64) for v in cols[:4]]
+        for h, (q, k, v) in enumerate(
+            ((cols[0], cols[1], cols[2]), (back[0], back[1], back[2]), (cols[3], back[3], cols[4]))
+        ):
+            k_ref[h, :, :128] = jnp.where(lane_all < 64, k, hot_a).astype(bf16)
+            k_ref[h, :, 128:] = hot_b
+            v_ref[h] = jnp.where(lane_all < 64, v, jnp.where(lane_all < 67, 1.0, 0.0)).astype(bf16)
+            turned = mm(q.astype(bf16), tab_ref[...])
+            qf = q * (HD ** -0.5)
+            for g in range(rows // G):
+                r = first_row + g
+                along_h = turned[g * G:(g + 1) * G, :128]
+                along_w = turned[g * G:(g + 1) * G, 128:]
+                h_a = roll(along_h, (LH - (G - 1) + 128 + r) % 128)
+                h_b = roll(along_h, (32 - (G - 1) + 128 + r) % 128)
+                w_a = roll(along_w, (LW - (G - 1)) % 128, 1)
+                w_b = roll(along_w, (80 - (G - 1)) % 128, 1)
+                h_lo = h_b - h_b.astype(bf16).astype(f32)
+                w_lo = w_b - w_b.astype(bf16).astype(f32)
+                first = jnp.where(lane < LH, qf[g * G:(g + 1) * G], jnp.where(lane < LW, h_a, w_a))
+                second = jnp.where(lane < 32, w_a, jnp.where(lane < 80, h_lo, w_lo))
+                q_ref[h, g * G:(g + 1) * G, :128] = first.astype(bf16)
+                q_ref[h, g * G:(g + 1) * G, 128:] = second.astype(bf16)
+
+    for k in range(4):
+        @pl.when(step == k)
+        def _(k=k):
+            work(xs[k][...])
+
+
+def prep(order, xs, w, b, tab, hot, heads, before, group):
+    rows, d = xs[0].shape
+    tokens = len(xs) * 2 * rows
+    outs = (struct((heads, tokens, 256)), struct((heads, tokens, 256)), struct((heads, tokens, 128)), struct((tokens, d)))
+    return call(
+        prep_kernel, "prep", 7, (len(xs),), order, list(xs) + [w, b, tab, hot] + list(before),
+        [whole(x.shape) for x in xs] + [whole(w.shape), whole(b.shape), whole(tab.shape)]
+        + [pl.BlockSpec((1, rows, 256), lambda i, o: (o[i], 0, 0))] + [ANY] * len(before),
+        outs,
+        [
+            pl.BlockSpec((heads, rows, 256), lambda i, o: (0, 2 * i + group, 0)),
+            pl.BlockSpec((heads, rows, 256), lambda i, o: (0, 2 * i + group, 0)),
+            pl.BlockSpec((heads, rows, 128), lambda i, o: (0, 2 * i + group, 0)),
+            pl.BlockSpec((rows, d), lambda i, o: (2 * i + group, 0)),
+        ],
+        aliases={9 + i: i for i in range(len(before))},
+    )
+
+
+def attend_kernel(order_ref, q_ref, k_ref, v_ref, *refs, tiles):
+    att_ref, q2_ref, mix_ref = refs[-3:]
+    head = pl.program_id(0)
+    start = 0
+    for tile in tiles:
+        at = pl.ds(start, tile)
+        start += tile
+        lane = lane_iota((tile, 128))
+        q = q_ref[0, at, :]
+        s = mm(q, k_ref[0], NT)
+        m = jnp.max(s, axis=1, keepdims=True)
+        p = jnp.exp(s - m)
+        o = mm(p.astype(bf16), v_ref[0])
+        total = o[:, 64:65]
+        att = o / total
+        lse = m + jnp.log(total)
+        att_ref[0, at, :] = att
+        low_att = att[:, :64].astype(bf16)
+        for h in range(3):
+            @pl.when(head == h)
+            def _(h=h):
+                mix_ref[at, h * 64:(h + 1) * 64] = low_att
+        a = q[:, :128].astype(f32)
+        b = q[:, 128:].astype(f32)
+        full = a + roll(b, 32) - lse
+        high = full.astype(bf16)
+        low = roll(full - high.astype(f32), 96)
+        q2_ref[0, at, :128] = jnp.where((lane >= LH) & (lane < LW), high.astype(f32), a).astype(bf16)
+        q2_ref[0, at, 128:] = jnp.where((lane >= 32) & (lane < 80), low, b).astype(bf16)
+
+
+def attend(q, k, v, side):
+    heads, tokens, _ = q.shape
+    rows = tokens // 2
+    tiles = (256,) * (rows // 256) + ((rows % 256,) if rows % 256 else ())
+    return call(
+        partial(attend_kernel, tiles=tiles), "attend", 19, (heads,), jnp.zeros((1,), jnp.int32), [q, k, v],
+        [
+            pl.BlockSpec((1, rows, 256), lambda h, o: (h, side, 0)),
+            pl.BlockSpec((1, tokens, 256), lambda h, o: (h, 0, 0)),
+            pl.BlockSpec((1, tokens, 128), lambda h, o: (h, 0, 0)),
+        ],
+        (struct((heads, rows, 128), f32), struct((heads, rows, 256)), struct((rows, heads * HD))),
+        [pl.BlockSpec((1, rows, 128), lambda h, o: (h, 0, 0)), pl.BlockSpec((1, rows, 256), lambda h, o: (h, 0, 0)), whole((rows, heads * HD))],
+    )
+
+
+def back_kernel(order_ref, qa_ref, qb_ref, k_ref, v_ref, atta_ref, attb_ref, g0, g1, g2, g3, tab_ref, turn_ref,
+                d_ref, table_ref, q_ref, go_ref, kt_ref, acc_ref, hi_ref, lo_ref, *, tile, sets, first, count):
+    head, step = pl.program_id(0), pl.program_id(1)
+    last = pl.num_programs(1) - 1
+    tokens = k_ref.shape[1]
+    rows = tokens // sets
+    wide = count * 64
+
+    @pl.when(step == 0)
+    def _():
+        lane = lane_iota((rows, 128))
+        for n, ref in enumerate((g0, g1, g2, g3)):
+            at = pl.ds(n * rows, rows)
+            for h in range(count):
+                @pl.when(head == h)
+                def _(ref=ref, at=at, h=h):
+                    lo = (first + h) * 64
+                    go_ref[at, :64] = ref[:, lo:lo + 64]
+        go = go_ref[...].astype(f32)
+        lane = lane_iota(go.shape)
+        go = jnp.where(lane < 64, go, 0.0)
+        att = jnp.concatenate([atta_ref[0], attb_ref[0]], axis=0)
+        q_ref[:tokens // 2] = qa_ref[0]
+        q_ref[tokens // 2:] = qb_ref[0]
+        dot = jnp.sum(jnp.where(lane < 64, go * att, 0.0), axis=1, keepdims=True)
+        high = dot.astype(bf16).astype(f32)
+        mid = (dot - high).astype(bf16).astype(f32)
+        low = dot - high - mid
+        go_ref[...] = jnp.where(lane < 64, go, jnp.where(lane == 64, -high, jnp.where(lane == 65, -mid, jnp.where(lane == 66, -low, 0.0)))).astype(bf16)
+        acc_ref[...] = jnp.zeros_like(acc_ref)
+        kt_ref[:LW] = k_ref[0, :, :128].T[:LW]
+        kt_ref[LW:] = turn_ref[...]
+
+    keys = tokens // pl.num_programs(1)
+    for i in range(keys // tile):
+        at = pl.ds(pl.multiple_of(step * keys + i * tile, tile), tile)
+        s = mm(k_ref[0, at, :], q_ref[...], NT)
+        p = jnp.exp(s)
+        pb = p.astype(bf16)
+        d = (p * mm(v_ref[0, at, :], go_ref[...], NT)).astype(bf16)
+        dv = mm(pb, go_ref[...]).astype(bf16)
+        dk = mm(d, q_ref[:, :128]).astype(bf16)
+        for h in range(count):
+            @pl.when(head == h)
+            def _(h=h):
+                d_ref[at, 2 * wide + h * 64:2 * wide + (h + 1) * 64] = dv[:, :64]
+                d_ref[at, wide + h * 64:wide + (h + 1) * 64] = dk[:, :64]
+        acc_ref[...] += mm(kt_ref[:, at], d)
+
+    @pl.when(step == last)
+    def _():
+        small = lane_iota((G, 128))
+        a = acc_ref[:128].T
+        b = jnp.concatenate([acc_ref[128:160], jnp.zeros((96, tokens), f32)], axis=0).T
+        for g in range(tokens // G):
+            block, inner = divmod(g, rows // 2 // G)
+            r = order_ref[block] + inner
+            ag = a[g * G:(g + 1) * G]
+            bg = b[g * G:(g + 1) * G]
+            along_h = jnp.where((small >= LH) & (small < LW), ag, 0.0)
+            along_w = jnp.where(small >= LW, ag, jnp.where(small < 32, bg, 0.0))
+            along_h = roll(along_h, (256 + G - 1 - LH - r) % 128)
+            along_w = roll(along_w, (128 - LW) % 128, 1)
+            h_hi = along_h.astype(bf16)
+            w_hi = along_w.astype(bf16)
+            hi_ref[g * G:(g + 1) * G, :128] = h_hi
+            hi_ref[g * G:(g + 1) * G, 128:] = w_hi
+            lo_ref[g * G:(g + 1) * G, :128] = (along_h - h_hi.astype(f32)).astype(bf16)
+            lo_ref[g * G:(g + 1) * G, 128:] = (along_w - w_hi.astype(f32)).astype(bf16)
+        turned = mm(hi_ref[...], tab_ref[...], NT) + mm(lo_ref[...], tab_ref[...], NT)
+        dq = (a * (HD ** -0.5) + turned).astype(bf16)
+        for h in range(count):
+            @pl.when(head == h)
+            def _(h=h):
+                d_ref[:, h * 64:(h + 1) * 64] = dq[:, :64]
+        tables = mm(hi_ref[...], q_ref[:, :128], TN)
+
+        @pl.when(head == 0)
+        def _():
+            table_ref[...] = tables
+
+        @pl.when(head > 0)
+        def _():
+            table_ref[...] += tables
+
+
+def attend_back(order, q2, k, v, att, grads, tab, turn, first, count, steps, tile, sets):
+    _, tokens, _ = k.shape
+    at = lambda h, i, o: (first + h, 0, 0)
+    wide = 3 * count * HD
+    per_head = lambda a: pl.BlockSpec((1,) + a.shape[1:], at)
+    return call(
+        partial(back_kernel, tile=tile, sets=sets, first=first, count=count), "attend_back", 21 * count,
+        (count, steps), order, list(q2) + [k, v] + list(att) + list(grads) + [tab, turn],
+        [per_head(a) for a in list(q2) + [k, v] + list(att)] + [whole(g.shape) for g in grads] + [whole(tab.shape), whole(turn.shape)],
+        (struct((tokens, wide)), struct((256, 128), f32)),
+        [whole((tokens, wide)), whole((256, 128))],
+        [
+            pltpu.VMEM((tokens, 256), bf16),
+            pltpu.VMEM((tokens, 128), bf16),
+            pltpu.VMEM((160, tokens), bf16),
+            pltpu.VMEM((160, tokens), f32),
+            pltpu.VMEM((tokens, 256), bf16),
+            pltpu.VMEM((tokens, 256), bf16),
+        ],
+    )
+
+
+def norm(v, gain, bias):
+    mean = jnp.mean(v, axis=1, keepdims=True)
+    centered = v - mean
+    inverse = lax.rsqrt(jnp.mean(centered * centered, axis=1, keepdims=True) + eps)
+    unit = centered * inverse
+    return unit * gain + bias, unit, inverse
+
+
+def norm_back(upstream, unit, inverse, gain):
+    scaled = upstream * gain
+    return inverse * (scaled - jnp.mean(scaled, axis=1, keepdims=True) - unit * jnp.mean(scaled * unit, axis=1, keepdims=True))
+
+
+def mlp_kernel(order_ref, m0, m1, m2, m3, src0, src1, top0, top1, up_ref, down_ref, proj_ref, ub_ref, vec_ref,
+               out0, out1, act_ref, hg_ref, n2_ref, mg_ref, br_ref, mix_ref, d0, d1, d2, d3, ubg_ref, vg_ref,
+               mid_ref, unit_ref, inv_ref, acc_ref, ng_ref, quad_ref, top_ref):
+    step = pl.program_id(0)
+    last = pl.num_programs(0) - 1
+    part, d = src0.shape
+    half = proj_ref.shape[3]
+    width = m0.shape[1]
+
+    def proj(i):
+        return proj_ref[:, i].reshape(d, half)
+
+    @pl.when(step == 0)
+    def _():
+        for k, ref in enumerate((m0, m1, m2, m3)):
+            quad_ref[order_ref[k]] = ref[...]
+        for i in range(4):
+            mix_ref[:, i * width:(i + 1) * width] = quad_ref[i]
+        top_ref[:part] = top0[...]
+        top_ref[part:] = top1[...]
+        mid = jnp.concatenate([src0[...], src1[...]], axis=0).astype(f32) + vec_ref[0:1] + mm(mix_ref[:, :half], proj(0), NT) + mm(mix_ref[:, half:], proj(1), NT)
+        normed, unit, inverse = norm(mid, vec_ref[1:2], vec_ref[2:3])
+        mid_ref[...] = mid
+        unit_ref[...] = unit
+        inv_ref[...] = inverse
+        n2_ref[...] = normed.astype(bf16)
+
+    tile = up_ref.shape[3]
+    up = up_ref[:, 0].reshape(d, tile)
+    down = down_ref[:, 0].reshape(d, tile)
+    hidden = mm(n2_ref[...], up) + ub_ref[...]
+    phi_all = 0.5 + 0.5 * lax.erf(hidden * (0.5 ** 0.5))
+    slope = phi_all + hidden * (jnp.exp(-0.5 * hidden * hidden) * 0.3989422804014327)
+    active = (hidden * phi_all).astype(bf16)
+    hg = (mm(top_ref[...], down) * slope).astype(bf16)
+    act_ref[...] = active
+    hg_ref[...] = hg
+    ubg_ref[...] = jnp.sum(hg.astype(f32), axis=0, keepdims=True)
+    out = mm(active, down, NT)
+    ng = mm(hg, up, NT)
+
+    @pl.when(step == 0)
+    def _():
+        acc_ref[...] = out
+        ng_ref[...] = ng
+
+    @pl.when(step > 0)
+    def _():
+        acc_ref[...] += out
+        ng_ref[...] += ng
+
+    @pl.when(step == last)
+    def _():
+        top = top_ref[...].astype(f32)
+        grad = ng_ref[...]
+        unit = unit_ref[...]
+        out = (mid_ref[...] + acc_ref[...] + vec_ref[3:4]).astype(bf16)
+        out0[...] = out[:part]
+        out1[...] = out[part:]
+        middle = top + norm_back(grad, unit, inv_ref[...], vec_ref[1:2])
+        branch = middle.astype(bf16)
+        mg_ref[...] = middle
+        br_ref[...] = branch
+        for i in range(2):
+            piece = mm(branch, proj(i)).astype(bf16)
+            quad_ref[2 * i] = piece[:, :width]
+            quad_ref[2 * i + 1] = piece[:, width:]
+        for k, ref in enumerate((d0, d1, d2, d3)):
+            ref[...] = quad_ref[order_ref[k]]
+        vg_ref[0:1] = jnp.sum(branch.astype(f32), axis=0, keepdims=True)
+        vg_ref[1:2] = jnp.sum(grad * unit, axis=0, keepdims=True)
+        vg_ref[2:3] = jnp.sum(grad, axis=0, keepdims=True)
+        vg_ref[3:4] = jnp.sum(top, axis=0, keepdims=True)
+
+
+def mlp(order, mixed, src, top, packed, up_bias, vecs, half_ff, tile):
+    part, d = src[0].shape
+    rows = 2 * part
+    blocks, halves, depth, _ = packed.shape
+    per = half_ff // tile
+    half = d // halves
+    ff = halves * half_ff
+    by_tile = pl.BlockSpec((rows, tile), lambda i, o: (0, i))
+    row_tile = pl.BlockSpec((1, tile), lambda i, o: (0, i))
+    full = whole((rows, d))
+    piece = whole((part, d))
+    return call(
+        mlp_kernel, "mlp", 24, (halves * per,), order,
+        list(mixed) + list(src) + list(top) + [packed, packed, packed, up_bias, vecs],
+        [whole(m.shape) for m in mixed] + [
+            piece, piece, piece, piece,
+            pl.BlockSpec((blocks, 1, depth, tile), lambda i, o: (0, i // per, 0, i % per)),
+            pl.BlockSpec((blocks, 1, depth, tile), lambda i, o: (0, i // per, 0, per + i % per)),
+            pl.BlockSpec((blocks, halves, depth, half), lambda i, o: (0, 0, 0, 2 * half_ff // half)),
+            row_tile, whole(vecs.shape),
+        ],
+        (struct((part, d)), struct((part, d)), struct((rows, ff)), struct((rows, ff)), struct((rows, d)), struct((rows, d), f32), struct((rows, d)), struct((rows, d)))
+        + (struct(mixed[0].shape),) * 4 + (struct((1, ff), f32), struct((4, d), f32)),
+        [piece, piece, by_tile, by_tile, full, full, full, full] + [whole(mixed[0].shape)] * 4 + [row_tile, whole((4, d))],
+        [
+            pltpu.VMEM((rows, d), f32),
+            pltpu.VMEM((rows, d), f32),
+            pltpu.VMEM((rows, 1), f32),
+            pltpu.VMEM((rows, d), f32),
+            pltpu.VMEM((rows, d), f32),
+            pltpu.VMEM((4,) + mixed[0].shape, bf16),
+            pltpu.VMEM((rows, d), bf16),
+        ],
+    )
+
+
+def wgrad_kernel(_, n2_ref, top0, top1, br_ref, hg_ref, act_ref, mix_ref, out_ref, left_ref, *, per):
+    half, block = pl.program_id(0), pl.program_id(1)
+    blocks, depth = out_ref.shape[0], out_ref.shape[2]
+
+    @pl.when((half == 0) & (block == 0))
+    def _():
+        left_ref[0] = n2_ref[...].T
+        left_ref[1] = jnp.concatenate([top0[...], top1[...]], axis=0).T
+        left_ref[2] = br_ref[...].T
+
+    def put(i, right):
+        out_ref[:, 0] = mm(left_ref[i], right[...]).astype(bf16).reshape(blocks, depth, -1)
+
+    @pl.when(block < per)
+    def _():
+        put(0, hg_ref)
+
+    @pl.when((block >= per) & (block < 2 * per))
+    def _():
+        put(1, act_ref)
+
+    @pl.when(block == 2 * per)
+    def _():
+        put(2, mix_ref)
+
+
+def wgrad(n2, top, branch, hg, active, mixed, blocks, halves):
+    rows, d = n2.shape
+    ff = hg.shape[1]
+    tile = d // halves
+    per = ff // halves // tile
+    depth = d // blocks
+    return call(
+        partial(wgrad_kernel, per=per), "wgrad", 20, (halves, 2 * per + 1), jnp.zeros((1,), jnp.int32),
+        [n2, top[0], top[1], branch, hg, active, mixed],
+        [whole((rows, d)), whole(top[0].shape), whole(top[1].shape), whole((rows, d))] + [
+            pl.BlockSpec((rows, tile), lambda s, j, o: (0, s * per + jnp.minimum(j, per - 1))),
+            pl.BlockSpec((rows, tile), lambda s, j, o: (0, s * per + jnp.clip(j - per, 0, per - 1))),
+            pl.BlockSpec((rows, tile), lambda s, j, o: (0, s)),
+        ],
+        struct((blocks, halves, depth, (2 * per + 1) * tile)),
+        pl.BlockSpec((blocks, 1, depth, tile), lambda s, j, o: (0, s, 0, j)),
+        [pltpu.VMEM((3, d, rows), bf16)],
+    )
+
+
+def down_kernel(_, a_ref, b_ref, w_ref, ng_ref):
+    both = jnp.concatenate([a_ref[...], b_ref[...]], axis=1)
+    ng_ref[0] = mm(both, w_ref[:, :both.shape[1]], NT).astype(bf16)
+
+
+def grad_down(sets, grads, w, rows):
+    d = w.shape[0]
+    return call(
+        down_kernel, "grad_down", 4, (2,), jnp.zeros((1,), jnp.int32), list(grads) + [w],
+        [pl.BlockSpec((rows, g.shape[1]), lambda i, o: (2 * i + sets, 0)) for g in grads] + [whole(w.shape)],
+        struct((2, rows, d)), pl.BlockSpec((1, rows, d), lambda i, o: (i, 0, 0)),
+    )
+
+
+def qkv_grad_kernel(_, x_ref, a_ref, b_ref, w_ref, wg_ref, bg_ref, ng_ref, acc_ref):
+    step = pl.program_id(0)
+    width = wg_ref.shape[-1]
+    both = jnp.concatenate([a_ref[...], b_ref[...]], axis=1)
+    add = mm(x_ref[...].T, both)
+    sums = jnp.sum(both.astype(f32), axis=0, keepdims=True)
+
+    @pl.when(step == 0)
+    def _():
+        acc_ref[...] = add
+        bg_ref[...] = sums
+
+    @pl.when(step > 0)
+    def _():
+        acc_ref[...] += add
+        bg_ref[...] += sums
+
+    @pl.when(step == pl.num_programs(0) - 1)
+    def _():
+        full = acc_ref[...]
+        wg_ref[...] = full.astype(bf16).reshape(wg_ref.shape)
+        w = w_ref[:, :width].astype(f32)
+        lane = lane_iota(ng_ref.shape)
+        a = jnp.sum(full * w, axis=1, keepdims=True)
+        b = jnp.sum(bg_ref[...] * w, axis=1, keepdims=True)
+        ng_ref[...] = jnp.where(lane == 0, a, jnp.where(lane == 1, b, 0.0))
+
+
+def qkv_grad(x, grads, w, steps, blocks):
+    tokens, d = x.shape
+    rows = tokens // steps
+    width = sum(g.shape[1] for g in grads)
+    by_rows = lambda n: pl.BlockSpec((rows, n), lambda i, o: (i, 0))
+    return call(
+        qkv_grad_kernel, "qkv_grad", 5, (steps,), jnp.zeros((1,), jnp.int32), [x] + list(grads) + [w],
+        [by_rows(d)] + [by_rows(g.shape[1]) for g in grads] + [whole(w.shape)],
+        (struct((blocks, d // blocks, width)), struct((1, width), f32), struct((d, 128), f32)),
+        [whole((blocks, d // blocks, width)), whole((1, width)), whole((d, 128))],
+        [pltpu.VMEM((d, width), f32)],
+    )
+
+
+def finish_kernel(_, kept_ref, got_ref, passed_ref, middle_ref, src_ref, gain_ref, out_ref):
+    grad = kept_ref[0].astype(f32) + got_ref[0].astype(f32) + passed_ref[...].astype(f32)
+    _, unit, inverse = norm(src_ref[...].astype(f32), 1.0, 0.0)
+    out_ref[...] = (middle_ref[...] + norm_back(grad, unit, inverse, gain_ref[...])).astype(bf16)
+
+
+def finish(at, kept, got, passed, middle, src, gain, group):
+    part, d = src.shape
+    first = pl.BlockSpec((1, part, d), lambda i, o: (0, group, 0))
+    return call(
+        finish_kernel, "finish", 2, (1,), at, [kept, got, passed, middle, src, gain],
+        [first, first, whole((part, d)), pl.BlockSpec((part, d), lambda i, o: (group, 0)), whole((part, d)), whole(gain.shape)],
+        struct((part, d)), whole((part, d)),
+    )
+
+
+AXES = ("fsdp", "ctx", "tp")
+
+
+def pairs_of(shape, move):
+    nf, nc, nt = shape["fsdp"], shape["ctx"], shape["tp"]
+    flat = lambda f, z, t: (f * nc + z) * nt + t
+    return [(flat(f, z, t), flat(*move(f, z, t))) for f in range(nf) for z in range(nc) for t in range(nt)]
+
+
+def grouped(
+    shape,
+    images,
+    norm1_gain,
+    norm1_bias,
+    qkv_weight,
+    qv_bias,
+    rel_pos_h,
+    rel_pos_w,
+    proj_weight,
+    proj_bias,
+    norm2_gain,
+    norm2_bias,
+    up_weight,
+    up_bias,
+    down_weight,
+    down_bias,
+    out_cotangent,
+):
+    nf, nc, nt = shape["fsdp"], shape["ctx"], shape["tp"]
+    batch, quarter, d = images.shape
+    sets = 4
+    part = quarter // 2
+    rows = 2 * part
+    tokens = sets * rows
+    half = qkv_weight.shape[2]
+    width = half // 2
+    heads = width // HD
+    depth = qkv_weight.shape[1]
+    blocks = nf * nc
+    half_ff = up_weight.shape[1]
+    fi, z, t = lax.axis_index("fsdp"), lax.axis_index("ctx"), lax.axis_index("tp")
+    x, c = fi // 2, fi % 2
+    zi, zp = z // 2, z % 2
+    me = 2 * zp + c
+
+    def send(v, move):
+        return lax.ppermute(v, AXES, pairs_of(shape, move))
+
+    core = lambda v: send(v, lambda f, w, u: (f ^ 1, w, u))
+    tpswap = lambda v: send(v, lambda f, w, u: (f, w, u ^ 1))
+    xswap = lambda v: send(v, lambda f, w, u: (f ^ 2, w, u))
+    zswap = lambda v, k: send(v, lambda f, w, u: (f, w ^ k, u))
+    beside = lambda v: zswap(v, 1)
+    diagonal = lambda v: send(v, lambda f, w, u: (f ^ 1, w ^ 1, u))
+
+    def pick(v, i, axis=0):
+        return lax.dynamic_index_in_dim(v, i, axis, keepdims=False)
+
+    def ordered(bit, mine, other, axis=0):
+        return jnp.where(bit == 0, jnp.concatenate([mine, other], axis), jnp.concatenate([other, mine], axis))
+
+    f = lambda v: v.astype(f32)
+    ints = lambda *v: jnp.stack([jnp.asarray(i, jnp.int32) for i in v])
+    place = ints(c, t, zi, zp)
+    gain1, bias1 = f(norm1_gain)[None], f(norm1_bias)[None]
+
+    got = core(pack(place, images, qkv_weight))
+    near, normed_near, far, w_own = route(place, images, got, qkv_weight, up_bias[None], qv_bias.reshape(1, d), gain1, bias1)
+    w_other = tpswap(w_own)
+    far = zswap(far, 2)
+    mine, yours = w_own[: 2 * depth, :576], w_other[: 2 * depth, :576]
+    keep = jnp.where(t == zp, mine, yours)
+    give = jnp.where(t == zp, yours, mine)
+    w_z = [keep, zswap(give, 1), zswap(keep, 2), zswap(give, 3)]
+    w = arrange(ints(fi * nc + z), w_z + [xswap(jnp.concatenate(w_z, axis=0))], d)
+    near_sets = [normed_near, core(normed_near), beside(normed_near)]
+    near_sets.append(core(near_sets[2]))
+    normed_far = norm_low(place, far, gain1, bias1)
+    far_sets = [normed_far, core(normed_far), beside(normed_far)]
+    far_sets.append(core(far_sets[2]))
+
+    bias = jnp.where(t == zp, qv_bias, w_other[2 * depth + 2].reshape(2, half))
+    bias = pick(bias.reshape(2, 2, width), c, 1)
+    bias = jnp.stack([bias[0], jnp.zeros_like(bias[0]), bias[1]])
+    bias = f(jnp.concatenate([bias[:, :128].reshape(-1), bias[:, 128:].reshape(-1), jnp.zeros((64,), bf16)]))[None]
+    flip = lambda v: jnp.pad(v[::-1].T, ((0, HD), (0, 128 - (2 * G - 1))))
+    plain = lambda v: jnp.pad(v.T, ((0, HD), (0, 128 - (2 * G - 1))))
+    tab = jnp.concatenate([flip(rel_pos_h), flip(rel_pos_w)], axis=1)
+    tab_back = jnp.concatenate([flip(rel_pos_h), plain(rel_pos_w)], axis=1)
+    block_rows = part // G
+    first_of = lambda m, s_: (2 * m + s_ // 2) * (quarter // G) + (s_ % 2) * block_rows
+    spot = np.concatenate([first_of(m, s_) * G + np.arange(part) for m in range(2) for s_ in range(sets)])
+    at = np.arange(tokens)
+    hot = np.zeros((tokens, 256), np.float32)
+    for base, index in ((LH, spot // G), (LW, spot % G), (160, spot // G), (208, spot % G)):
+        hot[at, base + index] = 1
+    turn = np.zeros((G, tokens), np.float32)
+    turn[G - 1 - at % G, at] = 1
+    hot = jnp.asarray(hot.astype(ml_dtypes.bfloat16).reshape(2 * sets, part, 256))
+    turn = jnp.asarray(turn.astype(ml_dtypes.bfloat16))
+
+    order = [me ^ k for k in range(sets)]
+    qkv = ()
+    for g, group in enumerate((near_sets, far_sets)):
+        m = zi ^ g
+        spots = ints(*[m * sets + s for s in order], *[first_of(m, s) for s in order])
+        qkv = prep(spots, group, w, bias, tab, hot, heads, qkv, g)
+    q, k, v, normed = qkv
+
+    packed = lax.all_gather(
+        jnp.concatenate([up_weight, down_weight, proj_weight], axis=1), AXES, axis=0, tiled=False
+    ).reshape(blocks, nt, depth, 2 * half_ff + half)
+
+    att_far, q_far, mix_far = attend(q, k, v, 1)
+    mix2, mix3 = beside(mix_far[:rows]), diagonal(mix_far[rows:])
+    att_near, q_near, mix_near = attend(q, k, v, 0)
+    mix0, mix1 = mix_near[:rows], core(mix_near[rows:])
+    att, q2 = (att_near, att_far), (q_near, q_far)
+
+    out_cotangent, _ = lax.optimization_barrier((out_cotangent, k))
+    top_own = lax.dynamic_index_in_dim(out_cotangent, t, 0, False).reshape(2, part, d)
+    top_got = core(pick(top_own, 1 - c))
+    top_own = pick(top_own, c)
+    top = [jnp.where(c == zi, top_own, top_got), zswap(jnp.where(c == zi, top_got, top_own), 2)]
+    other_up = w_other[2 * depth : 2 * depth + 2].reshape(-1)[:half_ff]
+    full_bias = f(ordered(t, up_bias, other_up))[None]
+    vecs = jnp.stack([f(proj_bias), f(norm2_gain), f(norm2_bias), f(down_bias)])
+    (out0, out1, active, hidden_grad, normed2, middle_grad, branch, mixed, back0, back1, back2, back3, up_bias_grad, vec_grads) = mlp(
+        ints(*order), [mix0, mix1, mix2, mix3], [near, far], top, packed, full_bias, vecs, half_ff, 768
+    )
+    back = [back0, core(back1), beside(back2), diagonal(back3)]
+    big = wgrad(normed2, top, branch, hidden_grad, active, mixed, blocks, nt)
+    big = lax.psum_scatter(big.reshape(blocks * nt, depth, -1), AXES, scatter_dimension=0, tiled=True)
+    big = f(big.reshape(depth, -1))
+
+    def give_back(own, own_other, home, home_other):
+        a = jnp.stack([own, own_other])
+        b = jnp.stack([home, home_other])
+        keep_, pass_ = jnp.where(c == zi, a, b), jnp.where(c == zi, b, a)
+        both = ordered(c, keep_, core(pass_), 1)
+        return jnp.where(t == 0, both, both[::-1])
+
+    out_home, out_own = zswap(out1, 2), tpswap(out0)
+    back, out_home, out_own = lax.optimization_barrier((back, out_home, out_own))
+
+    spots = ints(*[first_of(zi ^ g, s) for s in order for g in range(2)])
+    a_back, a_tables = attend_back(spots, q2, k, v, att, back, tab_back, turn, 0, 2, 3, 256, sets)
+    home_other = tpswap(out_home)
+    q2, home_other, a_back = lax.optimization_barrier((q2, home_other, a_back))
+    result = give_back(out0, out_own, out_home, home_other)
+    b_back, b_tables = attend_back(spots, q2, k, v, att, back, tab_back, turn, 2, 1, 3, 256, sets)
+    tables = (a_tables + b_tables)[:, :HD] * HD ** 0.5
+    grads = [a_back, b_back]
+    result, b_back = lax.optimization_barrier((result, b_back))
+    grads = [a_back, b_back]
+    got = core(grad_down(1, grads, w, rows))
+    kept = grad_down(0, grads, w, rows)
+
+    passed = (f(kept[1]) + f(got[1])).astype(bf16)
+    passed1 = beside(passed[part:])
+    grad1 = finish(place, kept, got, passed1, middle_grad, far, gain1, 1)
+    passed0 = beside(passed[:part])
+    grad0 = finish(place, kept, got, passed0, middle_grad, near, gain1, 0)
+    home = zswap(grad1, 2)
+    input_grad = give_back(grad0, tpswap(grad0), home, tpswap(home))
+
+    wg, sums, ng = qkv_grad(normed, grads, w, 3, blocks)
+    wg = wg.reshape(2, 2, 2, 2, depth, 3 * width)
+    wg = f(pick(wg, x)) + f(xswap(pick(wg, 1 - x)))
+    wg_low = wg.astype(bf16)
+    wg = pick(wg, zi, 1) + f(zswap(pick(wg_low, 1 - zi, 1), 2))
+    wg_low = wg.astype(bf16)
+    wg = pick(wg, t, 1) + f(tpswap(pick(wg_low, 1 - t, 1)))
+    wg = wg.astype(bf16)
+    wg = send(wg, lambda f_, w_, u: (f_, (w_ // 2) * 2 + u, w_ % 2))
+    wg = f(ordered(c, pick(wg, c)[None], core(pick(wg, 1 - c))[None]))
+    wg = jnp.concatenate([wg[..., :384].reshape(2, depth, 3, 128), wg[..., 384:].reshape(2, depth, 3, 64)], axis=-1)
+    wg = wg.transpose(2, 1, 0, 3).reshape(3, depth, half)
+
+    def total(v):
+        for move in (core, beside, tpswap, xswap):
+            v = v + move(v)
+        return v + zswap(v, 2)
+
+    def cut(v, sizes):
+        at, out = 0, []
+        v = v.reshape(-1)
+        for size in sizes:
+            out.append(lax.slice(v, (at,), (at + size,)))
+            at += size
+        return out
+
+    sums = sums[0]
+    qv = jnp.stack([jnp.concatenate([sums[i:i + 128], sums[j:j + 64]]) for i, j in ((0, 384), (256, 512))])
+    qv = jnp.where(jnp.arange(sets)[:, None, None] == me, qv[None], 0.0).transpose(1, 0, 2).reshape(-1)
+    small = total(
+        jnp.concatenate(
+            [vec_grads.reshape(-1), up_bias_grad.reshape(-1), ng[:, 0], ng[:, 1], qv, tables.reshape(-1)]
+        ).reshape(-1, 128)
+    )
+    pb, g2, b2, db, ub, g1, b1, qv, tg = cut(small, (d, d, d, d, nt * half_ff, d, d, 2 * d, 256 * HD))
+    g1 = (g1 - b1 * f(norm1_bias)) / f(norm1_gain)
+    tg = tg.reshape(256, HD)
+    return (
+        result.reshape(batch, quarter, d),
+        input_grad.reshape(batch, quarter, d),
+        g1,
+        b1,
+        wg,
+        pick(qv.reshape(2, nt, half), t, 1),
+        tg[: 2 * G - 1][::-1],
+        tg[128 : 128 + 2 * G - 1],
+        big[:, 2 * half_ff :],
+        pb,
+        g2,
+        b2,
+        big[:, :half_ff],
+        pick(ub.reshape(nt, half_ff), t),
+        big[:, half_ff : 2 * half_ff],
+        db,
+    )
 
 
 def layer_norm(values, gain_vec, shift_vec):
@@ -20,7 +835,7 @@
     return (standard * gain_vec + shift_vec, standard, inverse)
 
 
-def norm_back(upstream, standard, inverse, gain_vec):
+def norm_back_plain(upstream, standard, inverse, gain_vec):
     scaled = upstream * gain_vec
     mean_term = jnp.mean(scaled, axis=-1, keepdims=True)
     proj_term = jnp.mean(scaled * standard, axis=-1, keepdims=True)
@@ -189,7 +1004,7 @@
     normed2_grad = lax.psum(contract_last(hidden_grad, up_full).astype(jnp.bfloat16), "tp").astype(
         jnp.float32
     )
-    middle_grad = top_f + norm_back(normed2_grad, standard_two, inverse_two, gain_two)
+    middle_grad = top_f + norm_back_plain(normed2_grad, standard_two, inverse_two, gain_two)
     gain_two_grad = jnp.sum(normed2_grad * standard_two, axis=0)
     shift_two_grad = jnp.sum(normed2_grad, axis=0)
     branch_grad = middle_grad.astype(jnp.bfloat16)
@@ -266,7 +1081,7 @@
         lax.psum(table_h_part.astype(jnp.bfloat16), "tp").astype(jnp.float32),
         lax.psum(table_w_part.astype(jnp.bfloat16), "tp").astype(jnp.float32),
     )
-    input_grad = (middle_grad + norm_back(normed_grad, standard_one, inverse_one, gain_one)).astype(
+    input_grad = (middle_grad + norm_back_plain(normed_grad, standard_one, inverse_one, gain_one)).astype(
         jnp.bfloat16
     )
     gain_one_grad = jnp.sum(normed_grad * standard_one, axis=0)
@@ -376,6 +1191,8 @@
 
 
 def solution(mesh):
+    shape = dict(mesh.shape)
+    body = partial(grouped, shape) if shape == {"fsdp": 4, "ctx": 4, "tp": 2} else local
     placed = (
         P("fsdp", "ctx", None),
         P(),
@@ -395,7 +1212,7 @@
         P("fsdp", "ctx", None),
     )
     return jax.shard_map(
-        local,
+        body,
         mesh=mesh,
         in_specs=placed,
         out_specs=(

time: 1940 us -> 452 us (0.23)
  waiting for transfers between devices: 1010 us -> 144 us
  matrix products: 365 us -> 0 us
  local copies, waits for them, and re-layouts: 270 us -> 22.3 us
  Pallas kernels: 0 us -> 205 us
  other arithmetic: 174 us -> 17.4 us
  blocking collectives: 94.5 us -> 0 us
  starting transfers between devices: 2.98 us -> 42 us
    dot_general x56 -> x0, matrix products: 365 us -> none  [the longest x2 49.9 us: piece_scores(): jnp.einsum('rhc,nhc->rhn', query, key_h, preferred_element_type=jnp.float32)]
    psum x7 -> x0, waiting for transfers between devices: 348 us -> none  [the longest x2 110 us: micro_step(): lax.psum(normed_part.astype(jnp.bfloat16), 'tp').astype(jnp.float32)]
    reduce_scatter x8 -> x1, waiting for transfers between devices: 274 us -> 0.01 us  [grouped(): lax.psum_scatter(big.reshape(blocks * nt, depth, -1), AXES, scatter_dimen...]
    while x28 -> x0, waiting for transfers between devices: 237 us -> none
    pallas_call x0 -> x17, Pallas kernels: none -> 205 us  [call(): pl.pallas_call(kernel, out_shape=outs, grid_spec=pltpu.PrefetchScalarGrid...]
    all_gather x10 -> x1, waiting for transfers between devices: 145 us -> 0.01 us  [grouped(): lax.all_gather(jnp.concatenate([up_weight, down_weight, proj_weight], axi...]
    ppermute x0 -> x42, waiting for transfers between devices: none -> 144 us  [send(): return lax.ppermute(v, AXES, pairs_of(shape, move))]
    reduce_sum x22 -> x0, other arithmetic: 85.8 us -> none  [the longest x2 30 us: grad_step(): part_h = jnp.sum(grid_grad, axis=-1, dtype=jnp.float32)]
  transfers between devices with their start and end apart: 27 -> 44, of which waited for: 17 -> 19; matrix products, arithmetic and copies ran while one was open for 29% -> 6% of each run, Pallas kernels for 0% -> 40%
where the time goes in v2:
time: 452 us; the launch traced here: 446 us
  Pallas kernels  205 us (45%)
  waiting for transfers between devices  144 us (32%)
  starting transfers between devices  42 us (9%)
  local copies, waits for them, and re-layouts  22.3 us (5%)
  other arithmetic  17.4 us (4%)
  between operations  15.1 us (3%)
    pallas_call x17, Pallas kernels, call(): pl.pallas_call(kernel, out_shape=outs, grid_spec=pltpu.PrefetchScalarGrid...  205 us
    ppermute x42, waiting for transfers between devices, send(): return lax.ppermute(v, AXES, pairs_of(shape, move))  144 us
    ppermute x42, starting transfers between devices, send(): return lax.ppermute(v, AXES, pairs_of(shape, move))  41.9 us
  transfers between devices with their start and end apart: 44, of which 19 were waited for; matrix products, arithmetic and copies ran while one was open for 6% of the time, Pallas kernels for 40%

profile of v2, /device:TPU:8, one launch (start us, length us, event | category | flops | bytes accessed | tf_op | source)
XLA Modules:
  0.0 445.9 jit_solution(3171162510975626015)
XLA Ops:
  7.2 1.9 pad_maximum_fusion.5
  9.9 2.8 pack.1
  19.5 3.3 route.1
  22.8 1.5 collective-permute-start.5
  25.6 2.6 collective-permute-start.1
  30.7 1.6 collective-permute-start.8
  32.4 2.5 collective-permute-start.6
  35.1 25.2 %collective-permute-done.8.refs_3_ = bf16[96,576]{1,0:T(8,128)(2,1)S(1)} collective-permute-done((bf16[96,576]{1,0:T(8,128)(2,1)S(1)}, bf16[96,576]{1,0:T(8,128)(2,1)S(1)}, u32[]{:S(2)}, u32[]{:S(2)}) %collective-permute-start.8) | collective-permute-done | bytes 110624 | tf_op jit(solution)/shard_map/ppermute | solution.py:654
  60.9 10.5 %collective-permute-done.7.refs_2_ = bf16[96,576]{1,0:T(8,128)(2,1)S(1)} collective-permute-done((bf16[96,576]{1,0:T(8,128)(2,1)S(1)}, bf16[96,576]{1,0:T(8,128)(2,1)S(1)}, u32[]{:S(2)}, u32[]{:S(2)}) %collective-permute-start.7) | collective-permute-done | bytes 110624 | tf_op jit(solution)/shard_map/ppermute | solution.py:654
  71.5 1.5 collective-permute-start.9
  73.1 2.8 norm_low.1.refs_0_
  75.9 3.0 collective-permute-start.3
  80.0 5.9 %collective-permute-done.9.refs_4_ = bf16[384,576]{1,0:T(8,128)(2,1)S(1)} collective-permute-done((bf16[384,576]{1,0:T(8,128)(2,1)S(1)}, bf16[384,576]{1,0:T(8,128)(2,1)S(1)}, u32[]{:S(2)}, u32[]{:S(2)}) %collective-permute-start.9) | collective-permute-done | bytes 442400 | tf_op jit(solution)/shard_map/ppermute | solution.py:654
  86.6 2.3 arrange.1.refs_4_.w_ref
  89.0 15.9 %collective-permute-done.3.refs_2_ = bf16[288,768]{1,0:T(8,128)(2,1)S(1)} collective-permute-done((bf16[288,768]{1,0:T(8,128)(2,1)}, bf16[288,768]{1,0:T(8,128)(2,1)S(1)}, u32[]{:S(2)}, u32[]{:S(2)}) %collective-permute-start.3) | collective-permute-done | bytes 442400 | tf_op jit(solution)/shard_map/ppermute | solution.py:654
  105.7 7.9 %prep.2 = (bf16[3,2304,256]{2,1,0:T(8,128)(2,1)}, bf16[3,2304,256]{2,1,0:T(8,128)(2,1)}, bf16[3,2304,128]{2,1,0:T(8,128)(2,1)}, bf16[2304,768]{1,0:T(8,128)(2,1)}) custom-call(s32[8]{0:T(128)} %stack.196.order_ref, bf16[288,768]{1,0:T(8,128)(2,1)} %get-tuple-element.70.refs_0_, bf16[288,768]{1,0:T(8,128)(2,1)} %collective-permute-done.10.refs_1_, ...), custom_call_target="tpu_custom_call" | custom-call | flops 7000000000 | tf_op jit(solution)/shard_map/prep/pallas_call | solution.py:50
  114.5 7.8 %prep.3 = (bf16[3,2304,256]{2,1,0:T(8,128)(2,1)}, bf16[3,2304,256]{2,1,0:T(8,128)(2,1)}, bf16[3,2304,128]{2,1,0:T(8,128)(2,1)}, bf16[2304,768]{1,0:T(8,128)(2,1)}) custom-call(s32[8]{0:T(128)} %stack.180.order_ref, bf16[288,768]{1,0:T(8,128)(2,1)} %norm_low.1.refs_0_, ...), custom_call_target="tpu_custom_call", output_to_operand_aliasing={{0}: (9, {}), {1}: (10, {}), {2}: (11, {}), {3}: (12, {})} | custom-call | flops 7000000000 | tf_op jit(solution)/shard_map/prep/pallas_call | solution.py:50
  122.8 20.3 %attend.3 = (f32[3,1152,128]{2,1,0:T(8,128)}, bf16[3,1152,256]{2,1,0:T(8,128)(2,1)}, bf16[1152,192]{1,0:T(8,128)(2,1)}) custom-call(s32[1]{0:T(128)} %constant.209.clone.1.order_ref._, bf16[3,2304,256]{2,1,0:T(8,128)(2,1)} %get-tuple-element.75.q_ref, bf16[3,2304,256]{2,1,0:T(8,128)(2,1)} %get-tuple-element.76.k_ref, ...), custom_call_target="tpu_custom_call" | custom-call | flops 19000000512 | tf_op jit(solution)/shard_map/attend/pallas_call | solution.py:50
  143.0 20.7 %attend.2 = (f32[3,1152,128]{2,1,0:T(8,128)}, bf16[3,1152,256]{2,1,0:T(8,128)(2,1)}, bf16[1152,192]{1,0:T(8,128)(2,1)}) custom-call(s32[1]{0:T(128)} %constant.209.clone.1.order_ref._, bf16[3,2304,256]{2,1,0:T(8,128)(2,1)} %get-tuple-element.75.q_ref, bf16[3,2304,256]{2,1,0:T(8,128)(2,1)} %get-tuple-element.76.k_ref, ...), custom_call_target="tpu_custom_call" | custom-call | flops 19000000512 | tf_op jit(solution)/shard_map/attend/pallas_call | solution.py:50
  163.8 2.4 collective-permute-start.15
  167.3 2.5 collective-permute-start.17
  171.2 11.9 %collective-permute-done.15.m3 = bf16[576,192]{1,0:T(8,128)(2,1)S(1)} collective-permute-done((bf16[576,192]{1,0:T(8,128)(2,1)S(1)}, bf16[576,192]{1,0:T(8,128)(2,1)S(1)}, u32[]{:S(2)}, u32[]{:S(2)}) %collective-permute-start.15) | collective-permute-done | bytes 221216 | tf_op jit(solution)/shard_map/ppermute | solution.py:654
  183.0 6.0 %collective-permute-done.14.m2 = bf16[576,192]{1,0:T(8,128)(2,1)S(1)} collective-permute-done((bf16[576,192]{1,0:T(8,128)(2,1)S(1)}, bf16[576,192]{1,0:T(8,128)(2,1)S(1)}, u32[]{:S(2)}, u32[]{:S(2)}) %collective-permute-start.14) | collective-permute-done | bytes 221216 | tf_op jit(solution)/shard_map/ppermute | solution.py:654
  191.0 24.8 %mlp.1 = (bf16[288,768]{1,0:T(8,128)(2,1)}, bf16[288,768]{1,0:T(8,128)(2,1)}, bf16[576,3072]{1,0:T(8,128)(2,1)}, bf16[576,3072]{1,0:T(8,128)(2,1)}, bf16[576,768...) custom-call(s32[4]{0:T(128)} %pad_add_fusion.order_ref, ...), custom_call_target="tpu_custom_call" | custom-call | flops 24000000000 | tf_op jit(solution)/shard_map/mlp/pallas_call | solution.py:50
  218.5 2.2 collective-permute-start.21
  220.6 1.9 collective-permute-start.22
  222.6 21.1 %wgrad.1 = bf16[16,2,48,3456]{3,2,1,0:T(8,128)(2,1)} custom-call(s32[1]{0:T(128)} %constant.209.clone.1.order_ref._, bf16[576,768]{1,0:T(8,128)(2,1)} %get-tuple-element.115.n2_ref, bf16[288,768]{1,0:T(8,128)(2,1)} %get-tuple-element.161.top0, bf16[288,768]{1,0:T(8,128)(2,1)} %copy-done.30, bf16[576,768]{1,0:T(8,128)(2,1)} %get-tuple-element.116.br_ref, ...), custom_call_target="tpu_custom_call" | custom-call | flops 20000000000 | tf_op jit(solution)/shard_map/wgrad/pallas_call | solution.py:50
  245.3 45.1 %attend_back.2 = (bf16[2304,384]{1,0:T(8,128)(2,1)}, f32[256,128]{1,0:T(8,128)}) custom-call(s32[8]{0:T(128)} %stack.207.order_ref, bf16[3,1152,256]{2,1,0:T(8,128)(2,1)} %get-tuple-element.100.qa_ref, bf16[3,1152,256]{2,1,0:T(8,128)(2,1)} %get-tuple-element.101.qb_ref, bf16[3,2304,256]{2,1,0:T(8,128)(2,1)} %get-tuple-element.76.k_ref, ...), custom_call_target="tpu_custom_call" | custom-call | flops 41999998976 | tf_op jit(solution)/shard_map/attend_back/pallas_call | solution.py:50
  290.7 21.3 %attend_back.3 = (bf16[2304,192]{1,0:T(8,128)(2,1)}, f32[256,128]{1,0:T(8,128)}) custom-call(s32[8]{0:T(128)} %stack.207.order_ref, bf16[3,1152,256]{2,1,0:T(8,128)(2,1)} %get-tuple-element.100.qa_ref, bf16[3,1152,256]{2,1,0:T(8,128)(2,1)} %get-tuple-element.101.qb_ref, bf16[3,2304,256]{2,1,0:T(8,128)(2,1)} %get-tuple-element.76.k_ref, ...), custom_call_target="tpu_custom_call" | custom-call | flops 20999999488 | tf_op jit(solution)/shard_map/attend_back/pallas_call | solution.py:50
  313.7 1.5 reverse_select_fusion.1
  315.3 4.2 grad_down.3
  320.1 8.0 %qkv_grad.1 = (bf16[16,48,576]{2,1,0:T(8,128)(2,1)}, f32[1,576]{1,0:T(1,128)}, f32[768,128]{1,0:T(8,128)}) custom-call(s32[1]{0:T(128)} %constant.209.clone.1.order_ref._, bf16[2304,768]{1,0:T(8,128)(2,1)} %get-tuple-element.109.x_ref, bf16[2304,384]{1,0:T(8,128)(2,1)} %get-tuple-element.104.a_ref, bf16[2304,192]{1,0:T(8,128)(2,1)} %get-tuple-element.105.b_ref, ...), custom_call_target="tpu_custom_call" | custom-call | flops 5000000000 | tf_op jit(solution)/shard_map/qkv_grad/pallas_call | solution.py:50
  329.6 1.5 slice_reduce_fusion
  331.3 4.7 %grad_down.2.kept_ref = bf16[2,576,768]{2,1,0:T(8,128)(2,1)} custom-call(s32[1]{0:T(128)} %constant.209.clone.1.order_ref._, bf16[2304,384]{1,0:T(8,128)(2,1)} %get-tuple-element.104.a_ref, bf16[2304,192]{1,0:T(8,128)(2,1)} %get-tuple-element.105.b_ref, bf16[768,640]{1,0:T(8,128)(2,1)} %arrange.1.refs_4_.w_ref), custom_call_target="tpu_custom_call" | custom-call | flops 4000000000 | tf_op jit(solution)/shard_map/grad_down/pallas_call | solution.py:50
  336.4 4.9 %collective-permute-done.33 = f32[200,128]{1,0:T(8,128)S(1)} collective-permute-done((f32[200,128]{1,0:T(8,128)S(1)}, f32[200,128]{1,0:T(8,128)S(1)}, u32[]{:S(2)}, u32[]{:S(2)}) %collective-permute-start.33) | collective-permute-done | bytes 102432 | tf_op jit(solution)/shard_map/ppermute | solution.py:654
  344.4 3.7 collective-permute-done.34
  348.1 8.6 %collective-permute-done.35 = f32[200,128]{1,0:T(8,128)S(1)} collective-permute-done((f32[200,128]{1,0:T(8,128)S(1)}, f32[200,128]{1,0:T(8,128)S(1)}, u32[]{:S(2)}, u32[]{:S(2)}) %collective-permute-start.35) | collective-permute-done | bytes 102432 | tf_op jit(solution)/shard_map/ppermute | solution.py:654
  358.9 9.6 %collective-permute-done.28.passed_ref = bf16[288,768]{1,0:T(8,128)(2,1)S(1)} collective-permute-done((bf16[288,768]{1,0:T(8,128)(2,1)S(1)}, bf16[288,768]{1,0:T(8,128)(2,1)S(1)}, u32[]{:S(2)}, u32[]{:S(2)}) %collective-permute-start.28) | collective-permute-done | bytes 442400 | tf_op jit(solution)/shard_map/ppermute | solution.py:654
  369.2 3.8 finish.3
  373.1 3.5 collective-permute-start.29
  376.8 5.1 %collective-permute-done.26.passed_ref = bf16[288,768]{1,0:T(8,128)(2,1)} collective-permute-done((bf16[288,768]{1,0:T(8,128)(2,1)S(1)}, bf16[288,768]{1,0:T(8,128)(2,1)}, u32[]{:S(2)}, u32[]{:S(2)}) %collective-permute-start.26) | collective-permute-done | bytes 442400 | tf_op jit(solution)/shard_map/ppermute | solution.py:654
  381.9 3.8 finish.2
  386.6 22.5 %collective-permute-done.29 = bf16[288,768]{1,0:T(8,128)(2,1)S(1)} collective-permute-done((bf16[288,768]{1,0:T(8,128)(2,1)}, bf16[288,768]{1,0:T(8,128)(2,1)S(1)}, u32[]{:S(2)}, u32[]{:S(2)}) %collective-permute-start.29) | collective-permute-done | bytes 442400 | tf_op jit(solution)/shard_map/ppermute | solution.py:654
  411.2 2.1 collective-permute-done.38
  414.4 6.2 %collective-permute-done.30 = bf16[288,768]{1,0:T(8,128)(2,1)S(1)} collective-permute-done((bf16[288,768]{1,0:T(8,128)(2,1)S(1)}, bf16[288,768]{1,0:T(8,128)(2,1)S(1)}, u32[]{:S(2)}, u32[]{:S(2)}) %collective-permute-start.30) | collective-permute-done | bytes 442400 | tf_op jit(solution)/shard_map/ppermute | solution.py:654
  421.9 4.9 %collective-permute-start.40 = (bf16[2,48,576]{2,1,0:T(8,128)(2,1)S(1)}, bf16[2,48,576]{2,1,0:T(8,128)(2,1)S(1)}, u32[]{:S(2)}, u32[]{:S(2)}) collective-permute-start(bf16[2,48,576]{2,1,0:T(8,128)(2,1)S(1)} %fusion.1), channel_id=1, source_target_pairs={{0,0},{1,2},{2,1},{3,3},{4,4},{5,6},{6,5},{7,7},{8,8},{9,10},{10,9... | collective-permute-start | bytes 331784 | tf_op jit(solution)/shard_map/ppermute | solution.py:654
  427.5 2.3 collective-permute-done.40
  434.8 1.5 reverse_select_fusion
  (249 shorter events, 49.4 us)
Async XLA Ops:
  7.2 115.1 %copy-start = (bf16[2,576,768]{2,1,0:T(8,128)(2,1)S(1)}, bf16[2,576,768]{2,1,0:T(8,128)(2,1)}, u32[]{:S(2)}) copy-start(bf16[2,576,768]{2,1,0:T(8,128)(2,1)} %param.33) | copy-start | bytes 5308420
  7.2 183.1 %all-gather.3.cloned.1.call-start = ((), (), s32[]{:S(2)}) async-start(), calls=%async_computation.2 | async-start | bytes 10948608 | tf_op jit(solution)/shard_map/all_gather | solution.py:717
  9.2 427.1 %reduce-scatter.2.cloned.1.call-start = ((), (), s32[]{:S(2)}) async-start(), calls=%async_computation.1 | async-start | bytes 10948608 | tf_op jit(solution)/shard_map/reduce_scatter | solution.py:740
  12.7 6.0 %collective-permute-start = (bf16[336,768]{1,0:T(8,128)(2,1)}, bf16[336,768]{1,0:T(8,128)(2,1)S(1)}, u32[]{:S(2)}, u32[]{:S(2)}) collective-permute-start(bf16[336,768]{1,0:T(8,128)(2,1)} %pack.1), channel_id=1, source_target_pairs={{0,8},{1,9},{2,10},{3,11},{4,12},{5,13},{6,14},{7,15},{8,0},{9,1},... | collective-permute-start | bytes 1548296 | tf_op jit(solution)/shard_map/ppermute | solution.py:654
  22.8 7.0 %collective-permute-start.5 = (bf16[112,768]{1,0:T(8,128)(2,1)}, bf16[112,768]{1,0:T(8,128)(2,1)S(1)}, u32[]{:S(2)}, u32[]{:S(2)}) collective-permute-start(bf16[112,768]{1,0:T(8,128)(2,1)} %get-tuple-element.69), channel_id=1, source_target_pairs={{0,1},{1,0},{2,3},{3,2},{4,5},{5,4},{6,7},{7,6},{8,9},{9,8},{10,11... | collective-permute-start | bytes 516104 | tf_op jit(solution)/shard_map/ppermute | solution.py:654
  25.6 47.5 %collective-permute-start.1 = (bf16[288,768]{1,0:T(8,128)(2,1)}, bf16[288,768]{1,0:T(8,128)(2,1)}, u32[]{:S(2)}, u32[]{:S(2)}) collective-permute-start(bf16[288,768]{1,0:T(8,128)(2,1)} %get-tuple-element.68), channel_id=1, source_target_pairs={{0,4},{1,5},{2,6},{3,7},{4,0},{5,1},{6,2},{7,3},{8,12},{9,13},{10,... | collective-permute-start | bytes 1327112 | tf_op jit(solution)/shard_map/ppermute | solution.py:654
  28.1 50.7 %collective-permute-start.11 = (bf16[288,768]{1,0:T(8,128)(2,1)}, bf16[288,768]{1,0:T(8,128)(2,1)}, u32[]{:S(2)}, u32[]{:S(2)}) collective-permute-start(bf16[288,768]{1,0:T(8,128)(2,1)} %get-tuple-element.70.refs_0_), channel_id=1, source_target_pairs={{0,2},{1,3},{2,0},{3,1},{4,6},{5,7},{6,4},{7,5},{8,10},{9,11},{10,... | collective-permute-start | bytes 1327112 | tf_op jit(solution)/shard_map/ppermute | solution.py:654
  30.7 45.2 %copy-start.5 = (bf16[96,576]{1,0:T(8,128)(2,1)}, bf16[96,576]{1,0:T(8,128)(2,1)S(1)}, u32[]{:S(2)}) copy-start(bf16[96,576]{1,0:T(8,128)(2,1)S(1)} %get-tuple-element.173.refs_0_) | copy-start | bytes 331780
  30.7 29.6 %collective-permute-start.8 = (bf16[96,576]{1,0:T(8,128)(2,1)S(1)}, bf16[96,576]{1,0:T(8,128)(2,1)S(1)}, u32[]{:S(2)}, u32[]{:S(2)}) collective-permute-start(bf16[96,576]{1,0:T(8,128)(2,1)S(1)} %get-tuple-element.172), channel_id=1, source_target_pairs={{0,6},{1,7},{2,4},{3,5},{4,2},{5,3},{6,0},{7,1},{8,14},{9,15},{10,... | collective-permute-start | bytes 331784 | tf_op jit(solution)/shard_map/ppermute | solution.py:654
  32.4 28.5 %collective-permute-start.6 = (bf16[96,576]{1,0:T(8,128)(2,1)S(1)}, bf16[96,576]{1,0:T(8,128)(2,1)S(1)}, u32[]{:S(2)}, u32[]{:S(2)}) collective-permute-start(bf16[96,576]{1,0:T(8,128)(2,1)S(1)} %get-tuple-element.172), channel_id=1, source_target_pairs={{0,2},{1,3},{2,0},{3,1},{4,6},{5,7},{6,4},{7,5},{8,10},{9,11},{10,... | collective-permute-start | bytes 331784 | tf_op jit(solution)/shard_map/ppermute | solution.py:654
  35.0 36.5 %collective-permute-start.7 = (bf16[96,576]{1,0:T(8,128)(2,1)S(1)}, bf16[96,576]{1,0:T(8,128)(2,1)S(1)}, u32[]{:S(2)}, u32[]{:S(2)}) collective-permute-start(bf16[96,576]{1,0:T(8,128)(2,1)S(1)} %get-tuple-element.173.refs_0_), channel_id=1, source_target_pairs={{0,4},{1,5},{2,6},{3,7},{4,0},{5,1},{6,2},{7,3},{8,12},{9,13},{10,... | collective-permute-start | bytes 331784 | tf_op jit(solution)/shard_map/ppermute | solution.py:654
  60.3 44.6 %collective-permute-start.10 = (bf16[288,768]{1,0:T(8,128)(2,1)}, bf16[288,768]{1,0:T(8,128)(2,1)}, u32[]{:S(2)}, u32[]{:S(2)}) collective-permute-start(bf16[288,768]{1,0:T(8,128)(2,1)} %get-tuple-element.70.refs_0_), channel_id=1, source_target_pairs={{0,8},{1,9},{2,10},{3,11},{4,12},{5,13},{6,14},{7,15},{8,0},{9,1},... | collective-permute-start | bytes 1327112 | tf_op jit(solution)/shard_map/ppermute | solution.py:654
  71.5 14.4 %collective-permute-start.9 = (bf16[384,576]{1,0:T(8,128)(2,1)S(1)}, bf16[384,576]{1,0:T(8,128)(2,1)S(1)}, u32[]{:S(2)}, u32[]{:S(2)}) collective-permute-start(bf16[384,576]{1,0:T(8,128)(2,1)S(1)} %pad_maximum_fusion.4), channel_id=1, source_target_pairs={{0,16},{1,17},{2,18},{3,19},{4,20},{5,21},{6,22},{7,23},{8,24},{9,... | collective-permute-start | bytes 1327112 | tf_op jit(solution)/shard_map/ppermute | solution.py:654
  75.9 28.9 %collective-permute-start.3 = (bf16[288,768]{1,0:T(8,128)(2,1)}, bf16[288,768]{1,0:T(8,128)(2,1)S(1)}, u32[]{:S(2)}, u32[]{:S(2)}) collective-permute-start(bf16[288,768]{1,0:T(8,128)(2,1)} %norm_low.1.refs_0_), channel_id=1, source_target_pairs={{0,2},{1,3},{2,0},{3,1},{4,6},{5,7},{6,4},{7,5},{8,10},{9,11},{10,... | collective-permute-start | bytes 1327112 | tf_op jit(solution)/shard_map/ppermute | solution.py:654
  78.9 26.0 %collective-permute-start.12 = (bf16[288,768]{1,0:T(8,128)(2,1)}, bf16[288,768]{1,0:T(8,128)(2,1)S(1)}, u32[]{:S(2)}, u32[]{:S(2)}) collective-permute-start(bf16[288,768]{1,0:T(8,128)(2,1)} %collective-permute-done.11.refs_2_), channel_id=1, source_target_pairs={{0,8},{1,9},{2,10},{3,11},{4,12},{5,13},{6,14},{7,15},{8,0},{9,1},... | collective-permute-start | bytes 1327112 | tf_op jit(solution)/shard_map/ppermute | solution.py:654
  79.5 34.1 %collective-permute-start.2 = (bf16[288,768]{1,0:T(8,128)(2,1)}, bf16[288,768]{1,0:T(8,128)(2,1)S(1)}, u32[]{:S(2)}, u32[]{:S(2)}) collective-permute-start(bf16[288,768]{1,0:T(8,128)(2,1)} %norm_low.1.refs_0_), channel_id=1, source_target_pairs={{0,8},{1,9},{2,10},{3,11},{4,12},{5,13},{6,14},{7,15},{8,0},{9,1},... | collective-permute-start | bytes 1327112 | tf_op jit(solution)/shard_map/ppermute | solution.py:654
  104.9 8.7 %collective-permute-start.4 = (bf16[288,768]{1,0:T(8,128)(2,1)S(1)}, bf16[288,768]{1,0:T(8,128)(2,1)S(1)}, u32[]{:S(2)}, u32[]{:S(2)}) collective-permute-start(bf16[288,768]{1,0:T(8,128)(2,1)S(1)} %collective-permute-done.3.refs_2_), channel_id=1, source_target_pairs={{0,8},{1,9},{2,10},{3,11},{4,12},{5,13},{6,14},{7,15},{8,0},{9,1},... | collective-permute-start | bytes 1327112 | tf_op jit(solution)/shard_map/ppermute | solution.py:654
  122.4 44.1 %collective-permute-start.16 = (bf16[288,768]{1,0:T(8,128)(2,1)S(1)}, bf16[288,768]{1,0:T(8,128)(2,1)S(1)}, u32[]{:S(2)}, u32[]{:S(2)}) collective-permute-start(bf16[288,768]{1,0:T(8,128)(2,1)S(1)} %dynamic-slice_bitcast_fusion), channel_id=1, source_target_pairs={{0,8},{1,9},{2,10},{3,11},{4,12},{5,13},{6,14},{7,15},{8,0},{9,1},... | collective-permute-start | bytes 1327112 | tf_op jit(solution)/shard_map/ppermute | solution.py:654
  163.8 19.3 %collective-permute-start.15 = (bf16[576,192]{1,0:T(8,128)(2,1)S(1)}, bf16[576,192]{1,0:T(8,128)(2,1)S(1)}, u32[]{:S(2)}, u32[]{:S(2)}) collective-permute-start(bf16[576,192]{1,0:T(8,128)(2,1)S(1)} %get-tuple-element.168), channel_id=1, source_target_pairs={{0,10},{1,11},{2,8},{3,9},{4,14},{5,15},{6,12},{7,13},{8,2},{9,3},... | collective-permute-start | bytes 663560 | tf_op jit(solution)/shard_map/ppermute | solution.py:654
  166.1 22.9 %collective-permute-start.14 = (bf16[576,192]{1,0:T(8,128)(2,1)S(1)}, bf16[576,192]{1,0:T(8,128)(2,1)S(1)}, u32[]{:S(2)}, u32[]{:S(2)}) collective-permute-start(bf16[576,192]{1,0:T(8,128)(2,1)S(1)} %get-tuple-element.169), channel_id=1, source_target_pairs={{0,2},{1,3},{2,0},{3,1},{4,6},{5,7},{6,4},{7,5},{8,10},{9,11},{10,... | collective-permute-start | bytes 663560 | tf_op jit(solution)/shard_map/ppermute | solution.py:654
  167.3 23.0 %collective-permute-start.17 = (bf16[288,768]{1,0:T(8,128)(2,1)S(1)}, bf16[288,768]{1,0:T(8,128)(2,1)S(1)}, u32[]{:S(2)}, u32[]{:S(2)}) collective-permute-start(bf16[288,768]{1,0:T(8,128)(2,1)S(1)} %get-tuple-element.160), channel_id=1, source_target_pairs={{0,4},{1,5},{2,6},{3,7},{4,0},{5,1},{6,2},{7,3},{8,12},{9,13},{10,... | collective-permute-start | bytes 1327112 | tf_op jit(solution)/shard_map/ppermute | solution.py:654
  170.5 18.5 %collective-permute-start.13 = (bf16[576,192]{1,0:T(8,128)(2,1)S(1)}, bf16[576,192]{1,0:T(8,128)(2,1)S(1)}, u32[]{:S(2)}, u32[]{:S(2)}) collective-permute-start(bf16[576,192]{1,0:T(8,128)(2,1)S(1)} %get-tuple-element.170), channel_id=1, source_target_pairs={{0,8},{1,9},{2,10},{3,11},{4,12},{5,13},{6,14},{7,15},{8,0},{9,1},... | collective-permute-start | bytes 663560 | tf_op jit(solution)/shard_map/ppermute | solution.py:654
  216.6 27.8 %collective-permute-start.18 = (bf16[576,192]{1,0:T(8,128)(2,1)}, bf16[576,192]{1,0:T(8,128)(2,1)S(1)}, u32[]{:S(2)}, u32[]{:S(2)}) collective-permute-start(bf16[576,192]{1,0:T(8,128)(2,1)} %get-tuple-element.84), channel_id=1, source_target_pairs={{0,8},{1,9},{2,10},{3,11},{4,12},{5,13},{6,14},{7,15},{8,0},{9,1},... | collective-permute-start | bytes 663560 | tf_op jit(solution)/shard_map/ppermute | solution.py:654
  216.6 27.8 %collective-permute-start.19 = (bf16[576,192]{1,0:T(8,128)(2,1)}, bf16[576,192]{1,0:T(8,128)(2,1)S(1)}, u32[]{:S(2)}, u32[]{:S(2)}) collective-permute-start(bf16[576,192]{1,0:T(8,128)(2,1)} %get-tuple-element.85), channel_id=1, source_target_pairs={{0,2},{1,3},{2,0},{3,1},{4,6},{5,7},{6,4},{7,5},{8,10},{9,11},{10,... | collective-permute-start | bytes 663560 | tf_op jit(solution)/shard_map/ppermute | solution.py:654
  218.1 26.3 %collective-permute-start.20 = (bf16[576,192]{1,0:T(8,128)(2,1)}, bf16[576,192]{1,0:T(8,128)(2,1)S(1)}, u32[]{:S(2)}, u32[]{:S(2)}) collective-permute-start(bf16[576,192]{1,0:T(8,128)(2,1)} %get-tuple-element.86), channel_id=1, source_target_pairs={{0,10},{1,11},{2,8},{3,9},{4,14},{5,15},{6,12},{7,13},{8,2},{9,3},... | collective-permute-start | bytes 663560 | tf_op jit(solution)/shard_map/ppermute | solution.py:654
  218.5 26.0 %collective-permute-start.21 = (bf16[288,768]{1,0:T(8,128)(2,1)}, bf16[288,768]{1,0:T(8,128)(2,1)S(1)}, u32[]{:S(2)}, u32[]{:S(2)}) collective-permute-start(bf16[288,768]{1,0:T(8,128)(2,1)} %get-tuple-element.87), channel_id=1, source_target_pairs={{0,4},{1,5},{2,6},{3,7},{4,0},{5,1},{6,2},{7,3},{8,12},{9,13},{10,... | collective-permute-start | bytes 1327112 | tf_op jit(solution)/shard_map/ppermute | solution.py:654
  220.6 23.8 %collective-permute-start.22 = (bf16[288,768]{1,0:T(8,128)(2,1)}, bf16[288,768]{1,0:T(8,128)(2,1)S(1)}, u32[]{:S(2)}, u32[]{:S(2)}) collective-permute-start(bf16[288,768]{1,0:T(8,128)(2,1)} %get-tuple-element.82), channel_id=1, source_target_pairs={{0,1},{1,0},{2,3},{3,2},{4,5},{5,4},{6,7},{7,6},{8,9},{9,8},{10,11... | collective-permute-start | bytes 1327112 | tf_op jit(solution)/shard_map/ppermute | solution.py:654
  244.5 46.0 %collective-permute-start.23 = (bf16[288,768]{1,0:T(8,128)(2,1)S(1)}, bf16[288,768]{1,0:T(8,128)(2,1)S(1)}, u32[]{:S(2)}, u32[]{:S(2)}) collective-permute-start(bf16[288,768]{1,0:T(8,128)(2,1)S(1)} %collective-permute-done.21), channel_id=1, source_target_pairs={{0,1},{1,0},{2,3},{3,2},{4,5},{5,4},{6,7},{7,6},{8,9},{9,8},{10,11... | collective-permute-start | bytes 1327112 | tf_op jit(solution)/shard_map/ppermute | solution.py:654
  245.3 45.1 %copy-start.7 = (bf16[288,768]{1,0:T(8,128)(2,1)S(1)}, bf16[288,768]{1,0:T(8,128)(2,1)}, u32[]{:S(2)}) copy-start(bf16[288,768]{1,0:T(8,128)(2,1)} %get-tuple-element.82) | copy-start | bytes 1327108
  290.6 22.4 %collective-permute-start.24 = (bf16[2,288,768]{2,1,0:T(8,128)(2,1)S(1)}, bf16[2,288,768]{2,1,0:T(8,128)(2,1)S(1)}, u32[]{:S(2)}, u32[]{:S(2)}) collective-permute-start(bf16[2,288,768]{2,1,0:T(8,128)(2,1)S(1)} %get-tuple-element.159), channel_id=1, source_target_pairs={{0,8},{1,9},{2,10},{3,11},{4,12},{5,13},{6,14},{7,15},{8,0},{9,1},... | collective-permute-start | bytes 2654216 | tf_op jit(solution)/shard_map/ppermute | solution.py:654
  319.5 23.1 %collective-permute-start.25 = (bf16[2,576,768]{2,1,0:T(8,128)(2,1)}, bf16[2,576,768]{2,1,0:T(8,128)(2,1)}, u32[]{:S(2)}, u32[]{:S(2)}) collective-permute-start(bf16[2,576,768]{2,1,0:T(8,128)(2,1)} %grad_down.3), channel_id=1, source_target_pairs={{0,8},{1,9},{2,10},{3,11},{4,12},{5,13},{6,14},{7,15},{8,0},{9,1},... | collective-permute-start | bytes 5308424 | tf_op jit(solution)/shard_map/ppermute | solution.py:654
  331.2 4.8 %collective-permute-start.32 = (f32[200,128]{1,0:T(8,128)S(1)}, f32[200,128]{1,0:T(8,128)S(1)}, u32[]{:S(2)}, u32[]{:S(2)}) collective-permute-start(f32[200,128]{1,0:T(8,128)S(1)} %bitcast.133), channel_id=1, source_target_pairs={{0,8},{1,9},{2,10},{3,11},{4,12},{5,13},{6,14},{7,15},{8,0},{9,1},... | collective-permute-start | bytes 307208 | tf_op jit(solution)/shard_map/ppermute | solution.py:654
  336.0 5.3 %collective-permute-start.33 = (f32[200,128]{1,0:T(8,128)S(1)}, f32[200,128]{1,0:T(8,128)S(1)}, u32[]{:S(2)}, u32[]{:S(2)}) collective-permute-start(f32[200,128]{1,0:T(8,128)S(1)} %bitcast_add_fusion.2), channel_id=1, source_target_pairs={{0,2},{1,3},{2,0},{3,1},{4,6},{5,7},{6,4},{7,5},{8,10},{9,11},{10,... | collective-permute-start | bytes 307208 | tf_op jit(solution)/shard_map/ppermute | solution.py:654
  336.3 21.4 %collective-permute-start.37 = (bf16[2,2,2,48,576]{4,3,2,0,1:T(8,128)(2,1)S(1)}, bf16[2,2,2,48,576]{4,3,2,0,1:T(8,128)(2,1)S(1)}, u32[]{:S(2)}, u32[]{:S(2)}) collective-permute-start(bf16[2,2,2,48,576]{4,3,2,0,1:T(8,128)(2,1)S(1)} %bitcast.132), channel_id=1, source_target_pairs={{0,16},{1,17},{2,18},{3,19},{4,20},{5,21},{6,22},{7,23},{8,24},{9,... | collective-permute-start | bytes 1327112 | tf_op jit(solution)/shard_map/ppermute | solution.py:654
  341.3 6.7 %collective-permute-start.34 = (f32[200,128]{1,0:T(8,128)S(1)}, f32[200,128]{1,0:T(8,128)S(1)}, u32[]{:S(2)}, u32[]{:S(2)}) collective-permute-start(f32[200,128]{1,0:T(8,128)S(1)} %fusion.20), channel_id=1, source_target_pairs={{0,1},{1,0},{2,3},{3,2},{4,5},{5,4},{6,7},{7,6},{8,9},{9,8},{10,11... | collective-permute-start | bytes 307208 | tf_op jit(solution)/shard_map/ppermute | solution.py:654
  344.1 24.4 %collective-permute-start.28 = (bf16[288,768]{1,0:T(8,128)(2,1)S(1)}, bf16[288,768]{1,0:T(8,128)(2,1)S(1)}, u32[]{:S(2)}, u32[]{:S(2)}) collective-permute-start(bf16[288,768]{1,0:T(8,128)(2,1)S(1)} %get-tuple-element.165), channel_id=1, source_target_pairs={{0,2},{1,3},{2,0},{3,1},{4,6},{5,7},{6,4},{7,5},{8,10},{9,11},{10,... | collective-permute-start | bytes 1327112 | tf_op jit(solution)/shard_map/ppermute | solution.py:654
  348.0 8.7 %collective-permute-start.35 = (f32[200,128]{1,0:T(8,128)S(1)}, f32[200,128]{1,0:T(8,128)S(1)}, u32[]{:S(2)}, u32[]{:S(2)}) collective-permute-start(f32[200,128]{1,0:T(8,128)S(1)} %add.254), channel_id=1, source_target_pairs={{0,16},{1,17},{2,18},{3,19},{4,20},{5,21},{6,22},{7,23},{8,24},{9,... | collective-permute-start | bytes 307208 | tf_op jit(solution)/shard_map/ppermute | solution.py:654
  356.8 19.9 %collective-permute-start.36 = (f32[200,128]{1,0:T(8,128)S(1)}, f32[200,128]{1,0:T(8,128)S(1)}, u32[]{:S(2)}, u32[]{:S(2)}) collective-permute-start(f32[200,128]{1,0:T(8,128)S(1)} %add.255), channel_id=1, source_target_pairs={{0,4},{1,5},{2,6},{3,7},{4,0},{5,1},{6,2},{7,3},{8,12},{9,13},{10,... | collective-permute-start | bytes 307208 | tf_op jit(solution)/shard_map/ppermute | solution.py:654
  357.9 24.0 %collective-permute-start.26 = (bf16[288,768]{1,0:T(8,128)(2,1)S(1)}, bf16[288,768]{1,0:T(8,128)(2,1)}, u32[]{:S(2)}, u32[]{:S(2)}) collective-permute-start(bf16[288,768]{1,0:T(8,128)(2,1)S(1)} %get-tuple-element.164), channel_id=1, source_target_pairs={{0,2},{1,3},{2,0},{3,1},{4,6},{5,7},{6,4},{7,5},{8,10},{9,11},{10,... | collective-permute-start | bytes 1327112 | tf_op jit(solution)/shard_map/ppermute | solution.py:654
  373.1 36.1 %collective-permute-start.29 = (bf16[288,768]{1,0:T(8,128)(2,1)}, bf16[288,768]{1,0:T(8,128)(2,1)S(1)}, u32[]{:S(2)}, u32[]{:S(2)}) collective-permute-start(bf16[288,768]{1,0:T(8,128)(2,1)} %finish.3), channel_id=1, source_target_pairs={{0,4},{1,5},{2,6},{3,7},{4,0},{5,1},{6,2},{7,3},{8,12},{9,13},{10,... | collective-permute-start | bytes 1327112 | tf_op jit(solution)/shard_map/ppermute | solution.py:654
  376.6 36.7 %collective-permute-start.38 = (bf16[2,2,48,576]{3,2,1,0:T(8,128)(2,1)S(1)}, bf16[2,2,48,576]{3,2,1,0:T(8,128)(2,1)S(1)}, u32[]{:S(2)}, u32[]{:S(2)}) collective-permute-start(bf16[2,2,48,576]{3,2,1,0:T(8,128)(2,1)S(1)} %fusion), channel_id=1, source_target_pairs={{0,4},{1,5},{2,6},{3,7},{4,0},{5,1},{6,2},{7,3},{8,12},{9,13},{10,... | collective-permute-start | bytes 663560 | tf_op jit(solution)/shard_map/ppermute | solution.py:654
  385.7 34.9 %copy-start.8 = (bf16[288,768]{1,0:T(8,128)(2,1)S(1)}, bf16[288,768]{1,0:T(8,128)(2,1)}, u32[]{:S(2)}) copy-start(bf16[288,768]{1,0:T(8,128)(2,1)} %finish.2) | copy-start | bytes 1327108
  385.7 28.7 %collective-permute-start.27 = (bf16[288,768]{1,0:T(8,128)(2,1)}, bf16[288,768]{1,0:T(8,128)(2,1)S(1)}, u32[]{:S(2)}, u32[]{:S(2)}) collective-permute-start(bf16[288,768]{1,0:T(8,128)(2,1)} %finish.2), channel_id=1, source_target_pairs={{0,1},{1,0},{2,3},{3,2},{4,5},{5,4},{6,7},{7,6},{8,9},{9,8},{10,11... | collective-permute-start | bytes 1327112 | tf_op jit(solution)/shard_map/ppermute | solution.py:654
  409.1 11.4 %collective-permute-start.30 = (bf16[288,768]{1,0:T(8,128)(2,1)S(1)}, bf16[288,768]{1,0:T(8,128)(2,1)S(1)}, u32[]{:S(2)}, u32[]{:S(2)}) collective-permute-start(bf16[288,768]{1,0:T(8,128)(2,1)S(1)} %collective-permute-done.29), channel_id=1, source_target_pairs={{0,1},{1,0},{2,3},{3,2},{4,5},{5,4},{6,7},{7,6},{8,9},{9,8},{10,11... | collective-permute-start | bytes 1327112 | tf_op jit(solution)/shard_map/ppermute | solution.py:654
  413.3 8.5 %collective-permute-start.39 = (bf16[2,48,576]{2,1,0:T(8,128)(2,1)S(1)}, bf16[2,48,576]{2,1,0:T(8,128)(2,1)S(1)}, u32[]{:S(2)}, u32[]{:S(2)}) collective-permute-start(bf16[2,48,576]{2,1,0:T(8,128)(2,1)S(1)} %fusion.6), channel_id=1, source_target_pairs={{0,1},{1,0},{2,3},{3,2},{4,5},{5,4},{6,7},{7,6},{8,9},{9,8},{10,11... | collective-permute-start | bytes 331784 | tf_op jit(solution)/shard_map/ppermute | solution.py:654
  420.7 13.3 %collective-permute-start.31 = (bf16[2,288,768]{2,1,0:T(8,128)(2,1)S(1)}, bf16[2,288,768]{2,1,0:T(8,128)(2,1)S(1)}, u32[]{:S(2)}, u32[]{:S(2)}) collective-permute-start(bf16[2,288,768]{2,1,0:T(8,128)(2,1)S(1)} %get-tuple-element.157), channel_id=1, source_target_pairs={{0,8},{1,9},{2,10},{3,11},{4,12},{5,13},{6,14},{7,15},{8,0},{9,1},... | collective-permute-start | bytes 2654216 | tf_op jit(solution)/shard_map/ppermute | solution.py:654
  421.9 7.9 %collective-permute-start.40 = (bf16[2,48,576]{2,1,0:T(8,128)(2,1)S(1)}, bf16[2,48,576]{2,1,0:T(8,128)(2,1)S(1)}, u32[]{:S(2)}, u32[]{:S(2)}) collective-permute-start(bf16[2,48,576]{2,1,0:T(8,128)(2,1)S(1)} %fusion.1), channel_id=1, source_target_pairs={{0,0},{1,2},{2,1},{3,3},{4,4},{5,6},{6,5},{7,7},{8,8},{9,10},{10,9... | collective-permute-start | bytes 331784 | tf_op jit(solution)/shard_map/ppermute | solution.py:654
  429.7 2.8 collective-permute-start.41
  (38 other events, 198.3 us)
Sparse Core Ops, SparseCore 0:
  10.9 108.5 all-gather.2
  243.8 163.0 reduce-scatter.1

commit v3 on v2

--- a/solution.py
+++ b/solution.py
@@ -84,14 +84,13 @@
     )
 
 
-def route_kernel(at_ref, image_ref, got_ref, w_ref, ub_ref, qvb_ref, gain_ref, bias_ref, near_ref, normed_ref, far_ref, w_out_ref):
+def route_kernel(at_ref, image_ref, got_ref, w_ref, ub_ref, qvb_ref, gain_ref, bias_ref, near_ref, normed_ref, w_out_ref):
     rows = image_ref.shape[1]
     depth = w_ref.shape[1]
     same = at_ref[0] == at_ref[2]
     own, got = image_ref[0], got_ref[:rows]
     near = jnp.where(same, own, got)
     near_ref[...] = near
-    far_ref[...] = jnp.where(same, got, own)
     normed_ref[...] = norm(near.astype(f32), gain_ref[...], bias_ref[...])[0].astype(bf16)
     w_out_ref[...] = jnp.zeros(w_out_ref.shape, bf16)
     w_out_ref[:depth, :576] = columns(w_ref, at_ref[0])
@@ -110,17 +109,21 @@
     return call(
         route_kernel, "route", 3, (1,), at, [images, got, w, up_bias, qv_bias, gain, bias],
         [pl.BlockSpec((1, rows, d), lambda i, o: (o[1], o[0], 0))] + [whole(v.shape) for v in (got, w, up_bias, qv_bias, gain, bias)],
-        (struct(half), struct(half), struct(half), struct(out)), [whole(half)] * 3 + [whole(out)],
-    )
-
-
-def norm_kernel(_, x_ref, gain_ref, bias_ref, out_ref):
-    out_ref[...] = norm(x_ref[...].astype(f32), gain_ref[...], bias_ref[...])[0].astype(bf16)
-
-
-def norm_low(at, x, gain, bias):
+        (struct(half), struct(half), struct(out)), [whole(half)] * 2 + [whole(out)],
+    )
+
+
+def far_kernel(at_ref, a_ref, b_ref, gain_ref, bias_ref, *refs):
+    far_ref, out_ref = refs[-2:]
+    far = jnp.where(at_ref[0] == at_ref[2], a_ref[...], b_ref[...])
+    far_ref[...] = far
+    out_ref[...] = norm(far.astype(f32), gain_ref[...], bias_ref[...])[0].astype(bf16)
+
+
+def take_far(at, a, b, gain, bias, after):
     return call(
-        norm_kernel, "norm_low", 1, (1,), at, [x, gain, bias], [whole(v.shape) for v in (x, gain, bias)], struct(x.shape), whole(x.shape)
+        far_kernel, "take_far", 2, (1,), at, [a, b, gain, bias] + after, [whole(v.shape) for v in (a, b, gain, bias)] + [ANY] * len(after),
+        (struct(a.shape), struct(a.shape)), [whole(a.shape)] * 2,
     )
 
 
@@ -255,7 +258,7 @@
     )
 
 
-def back_kernel(order_ref, qa_ref, qb_ref, k_ref, v_ref, atta_ref, attb_ref, g0, g1, g2, g3, tab_ref, turn_ref,
+def back_kernel(order_ref, qa_ref, qb_ref, k_ref, v_ref, atta_ref, attb_ref, own_ref, beside_ref, core_ref, tab_ref, turn_ref,
                 d_ref, table_ref, q_ref, go_ref, kt_ref, acc_ref, hi_ref, lo_ref, *, tile, sets, first, count):
     head, step = pl.program_id(0), pl.program_id(1)
     last = pl.num_programs(1) - 1
@@ -266,13 +269,13 @@
     @pl.when(step == 0)
     def _():
         lane = lane_iota((rows, 128))
-        for n, ref in enumerate((g0, g1, g2, g3)):
+        for n, (ref, from_row) in enumerate(((own_ref, 0), (core_ref, 0), (beside_ref, 0), (core_ref, rows))):
             at = pl.ds(n * rows, rows)
             for h in range(count):
                 @pl.when(head == h)
-                def _(ref=ref, at=at, h=h):
+                def _(ref=ref, at=at, h=h, from_row=from_row):
                     lo = (first + h) * 64
-                    go_ref[at, :64] = ref[:, lo:lo + 64]
+                    go_ref[at, :64] = ref[from_row:from_row + rows, lo:lo + 64]
         go = go_ref[...].astype(f32)
         lane = lane_iota(go.shape)
         go = jnp.where(lane < 64, go, 0.0)
@@ -376,22 +379,23 @@
     return inverse * (scaled - jnp.mean(scaled, axis=1, keepdims=True) - unit * jnp.mean(scaled * unit, axis=1, keepdims=True))
 
 
-def mlp_kernel(order_ref, m0, m1, m2, m3, src0, src1, top0, top1, up_ref, down_ref, proj_ref, ub_ref, vec_ref,
-               out0, out1, act_ref, hg_ref, n2_ref, mg_ref, br_ref, mix_ref, d0, d1, d2, d3, ubg_ref, vg_ref,
+def mlp_kernel(order_ref, near_ref, beside_ref, core_ref, src0, src1, top0, top1, up_ref, down_ref, proj_ref, ub_ref, vec_ref,
+               out0, out1, act_ref, hg_ref, n2_ref, mg_ref, br_ref, mix_ref, back_ref, ubg_ref, vg_ref,
                mid_ref, unit_ref, inv_ref, acc_ref, ng_ref, quad_ref, top_ref):
     step = pl.program_id(0)
     last = pl.num_programs(0) - 1
     part, d = src0.shape
     half = proj_ref.shape[3]
-    width = m0.shape[1]
+    width = near_ref.shape[1]
 
     def proj(i):
         return proj_ref[:, i].reshape(d, half)
 
     @pl.when(step == 0)
     def _():
-        for k, ref in enumerate((m0, m1, m2, m3)):
-            quad_ref[order_ref[k]] = ref[...]
+        rows = near_ref.shape[0] // 2
+        for k, piece in enumerate((near_ref[:rows], core_ref[:rows], beside_ref[:rows], core_ref[rows:])):
+            quad_ref[order_ref[k]] = piece
         for i in range(4):
             mix_ref[:, i * width:(i + 1) * width] = quad_ref[i]
         top_ref[:part] = top0[...]
@@ -443,8 +447,8 @@
             piece = mm(branch, proj(i)).astype(bf16)
             quad_ref[2 * i] = piece[:, :width]
             quad_ref[2 * i + 1] = piece[:, width:]
-        for k, ref in enumerate((d0, d1, d2, d3)):
-            ref[...] = quad_ref[order_ref[k]]
+        for k in range(4):
+            back_ref[k] = quad_ref[order_ref[k]]
         vg_ref[0:1] = jnp.sum(branch.astype(f32), axis=0, keepdims=True)
         vg_ref[1:2] = jnp.sum(grad * unit, axis=0, keepdims=True)
         vg_ref[2:3] = jnp.sum(grad, axis=0, keepdims=True)
@@ -457,6 +461,7 @@
     blocks, halves, depth, _ = packed.shape
     per = half_ff // tile
     half = d // halves
+    quad = (4, rows, mixed[0].shape[1])
     ff = halves * half_ff
     by_tile = pl.BlockSpec((rows, tile), lambda i, o: (0, i))
     row_tile = pl.BlockSpec((1, tile), lambda i, o: (0, i))
@@ -473,62 +478,55 @@
             row_tile, whole(vecs.shape),
         ],
         (struct((part, d)), struct((part, d)), struct((rows, ff)), struct((rows, ff)), struct((rows, d)), struct((rows, d), f32), struct((rows, d)), struct((rows, d)))
-        + (struct(mixed[0].shape),) * 4 + (struct((1, ff), f32), struct((4, d), f32)),
-        [piece, piece, by_tile, by_tile, full, full, full, full] + [whole(mixed[0].shape)] * 4 + [row_tile, whole((4, d))],
+        + (struct(quad),) + (struct((1, ff), f32), struct((4, d), f32)),
+        [piece, piece, by_tile, by_tile, full, full, full, full] + [whole(quad)] + [row_tile, whole((4, d))],
         [
             pltpu.VMEM((rows, d), f32),
             pltpu.VMEM((rows, d), f32),
             pltpu.VMEM((rows, 1), f32),
             pltpu.VMEM((rows, d), f32),
             pltpu.VMEM((rows, d), f32),
-            pltpu.VMEM((4,) + mixed[0].shape, bf16),
+            pltpu.VMEM(quad, bf16),
             pltpu.VMEM((rows, d), bf16),
         ],
     )
 
 
-def wgrad_kernel(_, n2_ref, top0, top1, br_ref, hg_ref, act_ref, mix_ref, out_ref, left_ref, *, per):
-    half, block = pl.program_id(0), pl.program_id(1)
-    blocks, depth = out_ref.shape[0], out_ref.shape[2]
-
-    @pl.when((half == 0) & (block == 0))
+def wgrad_kernel(_, n2_ref, top0, top1, br_ref, hg_ref, act_ref, mix_ref, out_ref, left_ref):
+    half, third = pl.program_id(0), pl.program_id(1)
+    blocks, depth, tile = out_ref.shape
+
+    @pl.when((half == 0) & (third == 0))
     def _():
         left_ref[0] = n2_ref[...].T
         left_ref[1] = jnp.concatenate([top0[...], top1[...]], axis=0).T
         left_ref[2] = br_ref[...].T
 
-    def put(i, right):
-        out_ref[:, 0] = mm(left_ref[i], right[...]).astype(bf16).reshape(blocks, depth, -1)
-
-    @pl.when(block < per)
-    def _():
-        put(0, hg_ref)
-
-    @pl.when((block >= per) & (block < 2 * per))
-    def _():
-        put(1, act_ref)
-
-    @pl.when(block == 2 * per)
-    def _():
-        put(2, mix_ref)
+    at = 0
+    for i, ref in enumerate((hg_ref, act_ref, mix_ref)):
+        width = ref.shape[1]
+        for k in range(3):
+            lo, hi = max(at, k * tile), min(at + width, (k + 1) * tile)
+            if lo < hi:
+                @pl.when(third == k)
+                def _(i=i, k=k, ref=ref, lo=lo, hi=hi, at=at):
+                    part = mm(left_ref[i], ref[:, lo - at:hi - at]).astype(bf16)
+                    out_ref[:, :, lo - k * tile:hi - k * tile] = part.reshape(blocks, depth, hi - lo)
+        at += width
 
 
 def wgrad(n2, top, branch, hg, active, mixed, blocks, halves):
     rows, d = n2.shape
-    ff = hg.shape[1]
-    tile = d // halves
-    per = ff // halves // tile
+    half_ff, half = hg.shape[1] // halves, d // halves
     depth = d // blocks
+    total = 2 * half_ff + half
+    by_half = lambda n: pl.BlockSpec((rows, n), lambda s, j, o: (0, s))
     return call(
-        partial(wgrad_kernel, per=per), "wgrad", 20, (halves, 2 * per + 1), jnp.zeros((1,), jnp.int32),
+        wgrad_kernel, "wgrad", 18, (halves, 3), jnp.zeros((1,), jnp.int32),
         [n2, top[0], top[1], branch, hg, active, mixed],
-        [whole((rows, d)), whole(top[0].shape), whole(top[1].shape), whole((rows, d))] + [
-            pl.BlockSpec((rows, tile), lambda s, j, o: (0, s * per + jnp.minimum(j, per - 1))),
-            pl.BlockSpec((rows, tile), lambda s, j, o: (0, s * per + jnp.clip(j - per, 0, per - 1))),
-            pl.BlockSpec((rows, tile), lambda s, j, o: (0, s)),
-        ],
-        struct((blocks, halves, depth, (2 * per + 1) * tile)),
-        pl.BlockSpec((blocks, 1, depth, tile), lambda s, j, o: (0, s, 0, j)),
+        [whole((rows, d)), whole(top[0].shape), whole(top[1].shape), whole((rows, d)), by_half(half_ff), by_half(half_ff), by_half(half)],
+        struct((blocks, depth, halves * total)),
+        pl.BlockSpec((blocks, depth, total // 3), lambda s, j, o: (0, 0, 3 * s + j)),
         [pltpu.VMEM((3, d, rows), bf16)],
     )
 
@@ -589,19 +587,40 @@
     )
 
 
-def finish_kernel(_, kept_ref, got_ref, passed_ref, middle_ref, src_ref, gain_ref, out_ref):
+def finish_kernel(_, kept_ref, got_ref, passed_ref, middle_ref, src_ref, gain_ref, *refs):
+    out_ref = refs[-1]
     grad = kept_ref[0].astype(f32) + got_ref[0].astype(f32) + passed_ref[...].astype(f32)
     _, unit, inverse = norm(src_ref[...].astype(f32), 1.0, 0.0)
     out_ref[...] = (middle_ref[...] + norm_back(grad, unit, inverse, gain_ref[...])).astype(bf16)
 
 
-def finish(at, kept, got, passed, middle, src, gain, group):
+def finish(at, kept, got, passed, middle, src, gain, group, after=()):
     part, d = src.shape
     first = pl.BlockSpec((1, part, d), lambda i, o: (0, group, 0))
     return call(
-        finish_kernel, "finish", 2, (1,), at, [kept, got, passed, middle, src, gain],
-        [first, first, whole((part, d)), pl.BlockSpec((part, d), lambda i, o: (group, 0)), whole((part, d)), whole(gain.shape)],
+        finish_kernel, "finish", 2, (1,), at, [kept, got, passed, middle, src, gain, *after],
+        [first, first, whole((part, d)), pl.BlockSpec((part, d), lambda i, o: (group, 0)), whole((part, d)), whole(gain.shape)] + [ANY] * len(after),
         struct((part, d)), whole((part, d)),
+    )
+
+
+def assemble_kernel(at_ref, own_ref, other_ref, home_ref, home_other_ref, got_ref, out_ref):
+    part = own_ref.shape[0]
+    mine = pl.ds(pl.multiple_of(at_ref[0] * part, 16), part)
+    other = pl.ds(pl.multiple_of((1 - at_ref[0]) * part, 16), part)
+    same = at_ref[0] == at_ref[2]
+    out_ref[at_ref[1], mine] = jnp.where(same, own_ref[...], home_ref[...])
+    out_ref[1 - at_ref[1], mine] = jnp.where(same, other_ref[...], home_other_ref[...])
+    out_ref[at_ref[1], other] = got_ref[0]
+    out_ref[1 - at_ref[1], other] = got_ref[1]
+
+
+def assemble(place, own, own_other, home, home_other, got):
+    part, d = own.shape
+    ins = [own, own_other, home, home_other, got]
+    return call(
+        assemble_kernel, "assemble", 3, (1,), place, ins, [whole(v.shape) for v in ins],
+        struct((2, 2 * part, d)), whole((2, 2 * part, d)),
     )
 
 
@@ -667,14 +686,21 @@
         return jnp.where(bit == 0, jnp.concatenate([mine, other], axis), jnp.concatenate([other, mine], axis))
 
     f = lambda v: v.astype(f32)
+    tied = lambda *v: lax.optimization_barrier(v)
     ints = lambda *v: jnp.stack([jnp.asarray(i, jnp.int32) for i in v])
     place = ints(c, t, zi, zp)
     gain1, bias1 = f(norm1_gain)[None], f(norm1_bias)[None]
 
+    image = lax.dynamic_index_in_dim(images, t, 0, False).reshape(2, part, d)
+    is_far = lambda f, w: f % 2 != w // 2
+    some = lambda v, move: lax.ppermute(
+        v, AXES, [p for p in pairs_of(shape, move) if is_far(p[0] // (nc * nt), p[0] // nt % nc)]
+    )
+    far_a = some(pick(image, c), lambda f, w, u: (f, w ^ 2, u))
+    far_b = some(pick(image, 1 - c), lambda f, w, u: (f ^ 1, w ^ 2, u))
     got = core(pack(place, images, qkv_weight))
-    near, normed_near, far, w_own = route(place, images, got, qkv_weight, up_bias[None], qv_bias.reshape(1, d), gain1, bias1)
+    near, normed_near, w_own = route(place, images, got, qkv_weight, up_bias[None], qv_bias.reshape(1, d), gain1, bias1)
     w_other = tpswap(w_own)
-    far = zswap(far, 2)
     mine, yours = w_own[: 2 * depth, :576], w_other[: 2 * depth, :576]
     keep = jnp.where(t == zp, mine, yours)
     give = jnp.where(t == zp, yours, mine)
@@ -682,7 +708,12 @@
     w = arrange(ints(fi * nc + z), w_z + [xswap(jnp.concatenate(w_z, axis=0))], d)
     near_sets = [normed_near, core(normed_near), beside(normed_near)]
     near_sets.append(core(near_sets[2]))
-    normed_far = norm_low(place, far, gain1, bias1)
+    far, normed_far = take_far(place, far_a, far_b, gain1, bias1, w_z[1:])
+
+    own_w = jnp.concatenate([up_weight, down_weight, proj_weight], axis=1)
+    own_w, normed_far = tied(own_w, normed_far)
+    packed = lax.all_gather(own_w, AXES, axis=0, tiled=False).reshape(blocks, nt, depth, 2 * half_ff + half)
+
     far_sets = [normed_far, core(normed_far), beside(normed_far)]
     far_sets.append(core(far_sets[2]))
 
@@ -714,80 +745,67 @@
         qkv = prep(spots, group, w, bias, tab, hot, heads, qkv, g)
     q, k, v, normed = qkv
 
-    packed = lax.all_gather(
-        jnp.concatenate([up_weight, down_weight, proj_weight], axis=1), AXES, axis=0, tiled=False
-    ).reshape(blocks, nt, depth, 2 * half_ff + half)
-
-    att_far, q_far, mix_far = attend(q, k, v, 1)
-    mix2, mix3 = beside(mix_far[:rows]), diagonal(mix_far[rows:])
-    att_near, q_near, mix_near = attend(q, k, v, 0)
-    mix0, mix1 = mix_near[:rows], core(mix_near[rows:])
-    att, q2 = (att_near, att_far), (q_near, q_far)
-
-    out_cotangent, _ = lax.optimization_barrier((out_cotangent, k))
+    normed, out_cotangent = tied(normed, out_cotangent)
     top_own = lax.dynamic_index_in_dim(out_cotangent, t, 0, False).reshape(2, part, d)
     top_got = core(pick(top_own, 1 - c))
     top_own = pick(top_own, c)
-    top = [jnp.where(c == zi, top_own, top_got), zswap(jnp.where(c == zi, top_got, top_own), 2)]
+    top_near, top_far = jnp.where(c == zi, top_own, top_got), jnp.where(c == zi, top_got, top_own)
+    q, top_near, top_far = tied(q, top_near, top_far)
+    top_far = zswap(top_far, 2)
+    att_far, q_far, mix_far = attend(q, k, v, 1)
+    from_beside = beside(mix_far)
+    att_near, q_near, mix_near = attend(q, k, v, 0)
+    mix_near, from_beside, top_far = tied(mix_near, from_beside, top_far)
+    top = [top_near, top_far]
+    from_core = core(jnp.concatenate([mix_near[rows:], from_beside[rows:]], axis=0))
+    att, q2 = (att_near, att_far), (q_near, q_far)
+
     other_up = w_other[2 * depth : 2 * depth + 2].reshape(-1)[:half_ff]
     full_bias = f(ordered(t, up_bias, other_up))[None]
     vecs = jnp.stack([f(proj_bias), f(norm2_gain), f(norm2_bias), f(down_bias)])
-    (out0, out1, active, hidden_grad, normed2, middle_grad, branch, mixed, back0, back1, back2, back3, up_bias_grad, vec_grads) = mlp(
-        ints(*order), [mix0, mix1, mix2, mix3], [near, far], top, packed, full_bias, vecs, half_ff, 768
-    )
-    back = [back0, core(back1), beside(back2), diagonal(back3)]
+    (out0, out1, active, hidden_grad, normed2, middle_grad, branch, mixed, back, up_bias_grad, vec_grads) = mlp(
+        ints(*order), [mix_near, from_beside, from_core], [near, far], top, packed, full_bias, vecs, half_ff, 768
+    )
+    back_beside = beside(back[2:].reshape(2 * rows, width))
     big = wgrad(normed2, top, branch, hidden_grad, active, mixed, blocks, nt)
-    big = lax.psum_scatter(big.reshape(blocks * nt, depth, -1), AXES, scatter_dimension=0, tiled=True)
-    big = f(big.reshape(depth, -1))
+    big, back_beside = tied(big, back_beside)
+    back_core = core(jnp.concatenate([back[1], back_beside[rows:]], axis=0))
+    back = [back[0], back_beside, back_core]
+    big = lax.psum_scatter(big.reshape(d, -1), ("fsdp", "ctx"), scatter_dimension=0, tiled=True)
+    big = big.reshape(depth, nt, -1)
+    big = f(pick(big, t, 1)) + f(tpswap(pick(big, 1 - t, 1)))
 
     def give_back(own, own_other, home, home_other):
         a = jnp.stack([own, own_other])
         b = jnp.stack([home, home_other])
-        keep_, pass_ = jnp.where(c == zi, a, b), jnp.where(c == zi, b, a)
-        both = ordered(c, keep_, core(pass_), 1)
-        return jnp.where(t == 0, both, both[::-1])
+        return own, own_other, home, home_other, core(jnp.where(c == zi, b, a))
 
     out_home, out_own = zswap(out1, 2), tpswap(out0)
-    back, out_home, out_own = lax.optimization_barrier((back, out_home, out_own))
 
     spots = ints(*[first_of(zi ^ g, s) for s in order for g in range(2)])
+    b_back, b_tables = attend_back(spots, q2, k, v, att, back, tab_back, turn, 2, 1, 3, 256, sets)
+    q2, b_back, out_home, out_own = tied(q2, b_back, out_home, out_own)
+    home_other = tpswap(out_home)
     a_back, a_tables = attend_back(spots, q2, k, v, att, back, tab_back, turn, 0, 2, 3, 256, sets)
-    home_other = tpswap(out_home)
-    q2, home_other, a_back = lax.optimization_barrier((q2, home_other, a_back))
-    result = give_back(out0, out_own, out_home, home_other)
-    b_back, b_tables = attend_back(spots, q2, k, v, att, back, tab_back, turn, 2, 1, 3, 256, sets)
+    home_other, a_back = tied(home_other, a_back)
+    result = (out0, out_own, out_home, home_other)
+    grads = [a_back, b_back]
+
+    to_core = grad_down(1, grads, w, rows)
+    w, to_core = tied(w, to_core)
+    got = core(to_core)
+    kept = grad_down(0, grads, w, rows)
+    passed = (f(kept[1]) + f(got[1])).astype(bf16)
+    normed, passed = tied(normed, passed)
+    passed1, passed0 = beside(passed[part:]), beside(passed[:part])
+    wg, sums, ng = qkv_grad(normed, grads, w, 3, blocks)
+    grad1 = finish(place, kept, got, passed1, middle_grad, far, gain1, 1)
+    wg = wg.reshape(2, 2, 2, 2, depth, 3 * width)
+    wg_x = xswap(pick(wg, 1 - x))
     tables = (a_tables + b_tables)[:, :HD] * HD ** 0.5
-    grads = [a_back, b_back]
-    result, b_back = lax.optimization_barrier((result, b_back))
-    grads = [a_back, b_back]
-    got = core(grad_down(1, grads, w, rows))
-    kept = grad_down(0, grads, w, rows)
-
-    passed = (f(kept[1]) + f(got[1])).astype(bf16)
-    passed1 = beside(passed[part:])
-    grad1 = finish(place, kept, got, passed1, middle_grad, far, gain1, 1)
-    passed0 = beside(passed[:part])
-    grad0 = finish(place, kept, got, passed0, middle_grad, near, gain1, 0)
     home = zswap(grad1, 2)
-    input_grad = give_back(grad0, tpswap(grad0), home, tpswap(home))
-
-    wg, sums, ng = qkv_grad(normed, grads, w, 3, blocks)
-    wg = wg.reshape(2, 2, 2, 2, depth, 3 * width)
-    wg = f(pick(wg, x)) + f(xswap(pick(wg, 1 - x)))
-    wg_low = wg.astype(bf16)
-    wg = pick(wg, zi, 1) + f(zswap(pick(wg_low, 1 - zi, 1), 2))
-    wg_low = wg.astype(bf16)
-    wg = pick(wg, t, 1) + f(tpswap(pick(wg_low, 1 - t, 1)))
-    wg = wg.astype(bf16)
-    wg = send(wg, lambda f_, w_, u: (f_, (w_ // 2) * 2 + u, w_ % 2))
-    wg = f(ordered(c, pick(wg, c)[None], core(pick(wg, 1 - c))[None]))
-    wg = jnp.concatenate([wg[..., :384].reshape(2, depth, 3, 128), wg[..., 384:].reshape(2, depth, 3, 64)], axis=-1)
-    wg = wg.transpose(2, 1, 0, 3).reshape(3, depth, half)
-
-    def total(v):
-        for move in (core, beside, tpswap, xswap):
-            v = v + move(v)
-        return v + zswap(v, 2)
+    grad0 = finish(place, kept, got, passed0, middle_grad, near, gain1, 0, [grad1])
+    grad_other = tpswap(grad0)
 
     def cut(v, sizes):
         at, out = 0, []
@@ -797,20 +815,38 @@
             at += size
         return out
 
+    grad1_, wg_x, tables, sums, ng, result = tied(grad1, wg_x, tables, sums, ng, result)
     sums = sums[0]
     qv = jnp.stack([jnp.concatenate([sums[i:i + 128], sums[j:j + 64]]) for i, j in ((0, 384), (256, 512))])
     qv = jnp.where(jnp.arange(sets)[:, None, None] == me, qv[None], 0.0).transpose(1, 0, 2).reshape(-1)
-    small = total(
-        jnp.concatenate(
-            [vec_grads.reshape(-1), up_bias_grad.reshape(-1), ng[:, 0], ng[:, 1], qv, tables.reshape(-1)]
-        ).reshape(-1, 128)
-    )
+    small = jnp.concatenate(
+        [vec_grads.reshape(-1), up_bias_grad.reshape(-1), ng[:, 0], ng[:, 1], qv, tables.reshape(-1)]
+    ).reshape(-1, 128)
+    for move in (core, tpswap, xswap):
+        small = small + move(small)
+
+    wg = f(pick(wg, x)) + f(wg_x)
+    wg_low = wg.astype(bf16)
+    wg = pick(wg, t, 2) + f(tpswap(pick(wg_low, 1 - t, 2)))
+    result = assemble(place, *give_back(*result))
+    grad1_, home, wg, small, result = tied(grad1_, home, wg, small, result)
+    input_grad = assemble(place, *give_back(grad0, grad_other, home, tpswap(home)))
+    wg_low = wg.astype(bf16)
+    wg = pick(wg, zi, 1) + f(zswap(pick(wg_low, 1 - zi, 1), 2))
+    wg = wg.astype(bf16)
+    wg = send(wg, lambda f_, w_, u: (f_, (w_ // 2) * 2 + u, w_ % 2))
+    wg = f(ordered(c, pick(wg, c)[None], core(pick(wg, 1 - c))[None]))
+    wg = jnp.concatenate([wg[..., :384].reshape(2, depth, 3, 128), wg[..., 384:].reshape(2, depth, 3, 64)], axis=-1)
+    wg = wg.transpose(2, 1, 0, 3).reshape(3, depth, half)
+
+    for distance in (1, 2):
+        small = small + zswap(small, distance)
     pb, g2, b2, db, ub, g1, b1, qv, tg = cut(small, (d, d, d, d, nt * half_ff, d, d, 2 * d, 256 * HD))
     g1 = (g1 - b1 * f(norm1_bias)) / f(norm1_gain)
     tg = tg.reshape(256, HD)
     return (
-        result.reshape(batch, quarter, d),
-        input_grad.reshape(batch, quarter, d),
+        result,
+        input_grad,
         g1,
         b1,
         wg,

time: 452 us -> 421 us (0.931)
  waiting for transfers between devices: 144 us -> 99.4 us
  local copies, waits for them, and re-layouts: 22.3 us -> 32.5 us
    ppermute x42 -> x40, waiting for transfers between devices: 144 us -> 91.9 us  [send(): return lax.ppermute(v, AXES, pairs_of(shape, move))]
    ppermute x0 -> x2, waiting for transfers between devices: none -> 7.45 us  [grouped(): lax.ppermute(v, AXES, [p for p in pairs_of(shape, move) if is_far(p[0] //...]
    pallas_call x17 -> x19, Pallas kernels: 205 us -> 209 us  [call(): pl.pallas_call(kernel, out_shape=outs, grid_spec=pltpu.PrefetchScalarGrid...]
    unnamed x97 -> x110, local copies, waits for them, and re-layouts: 8.86 us -> 12.4 us
    ppermute x42 -> x40, starting transfers between devices: 41.9 us -> 40.7 us  [send(): return lax.ppermute(v, AXES, pairs_of(shape, move))]
  transfers between devices with their start and end apart: 44 -> 44, of which waited for: 19 -> 17; matrix products, arithmetic and copies ran while one was open for 6% -> 8% of each run, Pallas kernels for 40% -> 42%
where the time goes in v3:
time: 421 us; the launch traced here: 415 us
  Pallas kernels  209 us (50%)
  waiting for transfers between devices  99.4 us (24%)
  starting transfers between devices  43.5 us (10%)
  local copies, waits for them, and re-layouts  32.5 us (8%)
  between operations  15.4 us (4%)
  other arithmetic  15.2 us (4%)
    pallas_call x19, Pallas kernels, call(): pl.pallas_call(kernel, out_shape=outs, grid_spec=pltpu.PrefetchScalarGrid...  209 us
    ppermute x40, waiting for transfers between devices, send(): return lax.ppermute(v, AXES, pairs_of(shape, move))  91.9 us
    ppermute x40, starting transfers between devices, send(): return lax.ppermute(v, AXES, pairs_of(shape, move))  40.7 us
    unnamed x110, local copies, waits for them, and re-layouts  12.4 us
  transfers between devices with their start and end apart: 44, of which 17 were waited for; matrix products, arithmetic and copies ran while one was open for 8% of the time, Pallas kernels for 42%

profile of v3, /device:TPU:8, one launch (start us, length us, event | category | flops | bytes accessed | tf_op | source)
XLA Modules:
  0.0 415.1 jit_solution(4181527691557091994)
XLA Ops:
  7.9 2.8 pack.1
  13.8 3.2 route.1
  17.0 1.5 collective-permute-start.3
  21.4 2.7 collective-permute-done.3
  25.2 1.6 collective-permute-start.6
  26.8 2.5 collective-permute-start.4
  29.3 1.7 pad_maximum_fusion.3
  31.0 7.5 %collective-permute-done.a_ref = bf16[288,768]{1,0:T(8,128)(2,1)} collective-permute-done((bf16[288,768]{1,0:T(8,128)(2,1)S(1)}, bf16[288,768]{1,0:T(8,128)(2,1)}, u32[]{:S(2)}, u32[]{:S(2)}) %collective-permute-start) | collective-permute-done | bytes 442400 | tf_op jit(solution)/shard_map/ppermute | solution.py:696
  38.5 13.6 %collective-permute-done.6.refs_2_.refs_3_ = bf16[96,576]{1,0:T(8,128)(2,1)S(1)} collective-permute-done((bf16[96,576]{1,0:T(8,128)(2,1)S(1)}, bf16[96,576]{1,0:T(8,128)(2,1)S(1)}, u32[]{:S(2)}, u32[]{:S(2)}) %collective-permute-start.6) | collective-permute-done | bytes 110624 | tf_op jit(solution)/shard_map/ppermute | solution.py:673
  53.4 2.9 take_far.1
  58.9 2.1 collective-permute-start.12
  62.9 1.6 collective-permute-start.10
  64.7 11.5 %collective-permute-done.12.refs_2_ = bf16[288,768]{1,0:T(8,128)(2,1)} collective-permute-done((bf16[288,768]{1,0:T(8,128)(2,1)S(1)}, bf16[288,768]{1,0:T(8,128)(2,1)}, u32[]{:S(2)}, u32[]{:S(2)}) %collective-permute-start.12) | collective-permute-done | bytes 442400 | tf_op jit(solution)/shard_map/ppermute | solution.py:673
  77.3 10.8 %collective-permute-done.8.refs_2_ = bf16[288,768]{1,0:T(8,128)(2,1)} collective-permute-done((bf16[288,768]{1,0:T(8,128)(2,1)}, bf16[288,768]{1,0:T(8,128)(2,1)}, u32[]{:S(2)}, u32[]{:S(2)}) %collective-permute-start.8) | collective-permute-done | bytes 442400 | tf_op jit(solution)/shard_map/ppermute | solution.py:673
  88.9 2.5 arrange.1.refs_4_.w_ref
  92.2 7.9 %prep.2 = (bf16[3,2304,256]{2,1,0:T(8,128)(2,1)}, bf16[3,2304,256]{2,1,0:T(8,128)(2,1)}, bf16[3,2304,128]{2,1,0:T(8,128)(2,1)}, bf16[2304,768]{1,0:T(8,128)(2,1)}) custom-call(s32[8]{0:T(128)} %stack.191.order_ref, bf16[288,768]{1,0:T(8,128)(2,1)} %get-tuple-element.91.refs_0_, bf16[288,768]{1,0:T(8,128)(2,1)} %collective-permute-done.11.refs_1_, ...), custom_call_target="tpu_custom_call" | custom-call | flops 7000000000 | tf_op jit(solution)/shard_map/prep/pallas_call | solution.py:50
  101.0 7.6 %prep.3 = (bf16[3,2304,256]{2,1,0:T(8,128)(2,1)}, bf16[3,2304,256]{2,1,0:T(8,128)(2,1)}, bf16[3,2304,128]{2,1,0:T(8,128)(2,1)}, bf16[2304,768]{1,0:T(8,128)(2,1)}) custom-call(s32[8]{0:T(128)} %stack.180.order_ref, bf16[288,768]{1,0:T(8,128)(2,1)} %get-tuple-element.90.refs_0_, ...), custom_call_target="tpu_custom_call", output_to_operand_aliasing={{0}: (9, {}), {1}: (10, {}), {2}: (11, {}), {3}: (12, {})} | custom-call | flops 7000000000 | tf_op jit(solution)/shard_map/prep/pallas_call | solution.py:50
  111.5 20.4 %attend.3 = (f32[3,1152,128]{2,1,0:T(8,128)}, bf16[3,1152,256]{2,1,0:T(8,128)(2,1)}, bf16[1152,192]{1,0:T(8,128)(2,1)}) custom-call(s32[1]{0:T(128)} %constant.220.clone.1.order_ref._, bf16[3,2304,256]{2,1,0:T(8,128)(2,1)} %get-tuple-element.99.q_ref, bf16[3,2304,256]{2,1,0:T(8,128)(2,1)} %get-tuple-element.100.k_ref, ...), custom_call_target="tpu_custom_call" | custom-call | flops 19000000512 | tf_op jit(solution)/shard_map/attend/pallas_call | solution.py:50
  133.3 2.6 collective-permute-start.15
  135.9 20.3 %attend.2 = (f32[3,1152,128]{2,1,0:T(8,128)}, bf16[3,1152,256]{2,1,0:T(8,128)(2,1)}, bf16[1152,192]{1,0:T(8,128)(2,1)}) custom-call(s32[1]{0:T(128)} %constant.220.clone.1.order_ref._, bf16[3,2304,256]{2,1,0:T(8,128)(2,1)} %get-tuple-element.99.q_ref, bf16[3,2304,256]{2,1,0:T(8,128)(2,1)} %get-tuple-element.100.k_ref, ...), custom_call_target="tpu_custom_call" | custom-call | flops 19000000512 | tf_op jit(solution)/shard_map/attend/pallas_call | solution.py:50
  156.2 10.4 %collective-permute-done.15 = bf16[1152,192]{0,1:T(8,128)(2,1)S(1)} collective-permute-done((bf16[1152,192]{0,1:T(8,128)(2,1)S(1)}, bf16[1152,192]{0,1:T(8,128)(2,1)S(1)}, u32[]{:S(2)}, u32[]{:S(2)}) %collective-permute-start.15) | collective-permute-done | bytes 442400 | tf_op jit(solution)/shard_map/ppermute | solution.py:673
  170.2 25.3 %mlp.1 = (bf16[288,768]{1,0:T(8,128)(2,1)}, bf16[288,768]{1,0:T(8,128)(2,1)}, bf16[576,3072]{1,0:T(8,128)(2,1)}, bf16[576,3072]{1,0:T(8,128)(2,1)}, bf16[576,768...) custom-call(s32[4]{0:T(128)} %pad_add_fusion.1.order_ref, ...), custom_call_target="tpu_custom_call" | custom-call | flops 24000000000 | tf_op jit(solution)/shard_map/mlp/pallas_call | solution.py:50
  196.9 2.5 collective-permute-start.18
  199.4 17.0 %wgrad.1 = bf16[16,48,6912]{2,1,0:T(8,128)(2,1)} custom-call(s32[1]{0:T(128)} %constant.220.clone.1.order_ref._, bf16[576,768]{1,0:T(8,128)(2,1)} %get-tuple-element.117.n2_ref, bf16[288,768]{1,0:T(8,128)(2,1)} %get-tuple-element.113.top0, bf16[288,768]{1,0:T(8,128)(2,1)} %copy-done.42, bf16[576,768]{1,0:T(8,128)(2,1)} %get-tuple-element.118.br_ref, ...), custom_call_target="tpu_custom_call" | custom-call | flops 17999998976 | tf_op jit(solution)/shard_map/wgrad/pallas_call | solution.py:50
  222.7 22.0 %attend_back.2 = (bf16[2304,192]{1,0:T(8,128)(2,1)}, f32[256,128]{1,0:T(8,128)}) custom-call(s32[8]{0:T(128)} %stack.192.order_ref, bf16[3,1152,256]{2,1,0:T(8,128)(2,1)} %get-tuple-element.127.qa_ref, bf16[3,1152,256]{2,1,0:T(8,128)(2,1)} %get-tuple-element.128.qb_ref, bf16[3,2304,256]{2,1,0:T(8,128)(2,1)} %get-tuple-element.100.k_ref, ...), custom_call_target="tpu_custom_call" | custom-call | flops 20999999488 | tf_op jit(solution)/shard_map/attend_back/pallas_call | solution.py:50
  245.7 45.3 %attend_back.3 = (bf16[2304,384]{1,0:T(8,128)(2,1)}, f32[256,128]{1,0:T(8,128)}) custom-call(s32[8]{0:T(128)} %stack.192.order_ref, bf16[3,1152,256]{2,1,0:T(8,128)(2,1)} %get-tuple-element.127.qa_ref, bf16[3,1152,256]{2,1,0:T(8,128)(2,1)} %get-tuple-element.128.qb_ref, bf16[3,2304,256]{2,1,0:T(8,128)(2,1)} %get-tuple-element.100.k_ref, ...), custom_call_target="tpu_custom_call" | custom-call | flops 41999998976 | tf_op jit(solution)/shard_map/attend_back/pallas_call | solution.py:50
  291.1 4.2 %grad_down.2 = bf16[2,576,768]{2,1,0:T(8,128)(2,1)} custom-call(s32[1]{0:T(128)} %constant.220.clone.1.order_ref._, bf16[2304,384]{1,0:T(8,128)(2,1)} %get-tuple-element.130.a_ref, bf16[2304,192]{1,0:T(8,128)(2,1)} %get-tuple-element.131.b_ref, bf16[768,640]{1,0:T(8,128)(2,1)} %arrange.1.refs_4_.w_ref), custom_call_target="tpu_custom_call" | custom-call | flops 4000000000 | tf_op jit(solution)/shard_map/grad_down/pallas_call | solution.py:50
  295.3 4.3 %grad_down.3.kept_ref = bf16[2,576,768]{2,1,0:T(8,128)(2,1)} custom-call(s32[1]{0:T(128)} %constant.220.clone.1.order_ref._, bf16[2304,384]{1,0:T(8,128)(2,1)} %get-tuple-element.130.a_ref, bf16[2304,192]{1,0:T(8,128)(2,1)} %get-tuple-element.131.b_ref, bf16[768,640]{1,0:T(8,128)(2,1)} %arrange.1.refs_4_.w_ref), custom_call_target="tpu_custom_call" | custom-call | flops 4000000000 | tf_op jit(solution)/shard_map/grad_down/pallas_call | solution.py:50
  302.4 2.0 collective-permute-start.24
  304.4 8.0 %qkv_grad.1 = (bf16[16,48,576]{2,1,0:T(8,128)(2,1)}, f32[1,576]{1,0:T(1,128)}, f32[768,128]{1,0:T(8,128)}) custom-call(s32[1]{0:T(128)} %constant.220.clone.1.order_ref._, bf16[2304,768]{1,0:T(8,128)(2,1)} %get-tuple-element.137.x_ref, bf16[2304,384]{1,0:T(8,128)(2,1)} %get-tuple-element.130.a_ref, bf16[2304,192]{1,0:T(8,128)(2,1)} %get-tuple-element.131.b_ref, ...), custom_call_target="tpu_custom_call" | custom-call | flops 5000000000 | tf_op jit(solution)/shard_map/qkv_grad/pallas_call | solution.py:50
  313.8 1.7 collective-permute-start.26
  315.6 8.4 %collective-permute-done.24.passed_ref = bf16[288,768]{1,0:T(8,128)(2,1)S(1)} collective-permute-done((bf16[288,768]{1,0:T(8,128)(2,1)S(1)}, bf16[288,768]{1,0:T(8,128)(2,1)S(1)}, u32[]{:S(2)}, u32[]{:S(2)}) %collective-permute-start.24) | collective-permute-done | bytes 442400 | tf_op jit(solution)/shard_map/ppermute | solution.py:673
  324.7 3.9 finish.2.refs_0_
  328.7 2.2 collective-permute-start.25
  336.0 3.6 collective-permute-done.29
  339.7 1.9 collective-permute-start.30
  341.6 2.4 collective-permute-done.27
  345.4 3.7 assemble.2
  349.1 9.0 %collective-permute-done.25.home_ref = bf16[288,768]{1,0:T(8,128)(2,1)} collective-permute-done((bf16[288,768]{1,0:T(8,128)(2,1)}, bf16[288,768]{1,0:T(8,128)(2,1)}, u32[]{:S(2)}, u32[]{:S(2)}) %collective-permute-start.25) | collective-permute-done | bytes 442400 | tf_op jit(solution)/shard_map/ppermute | solution.py:673
  358.0 3.4 collective-permute-start.36
  361.5 3.8 finish.3.own_ref
  367.4 3.0 collective-permute-start.37
  370.4 2.4 collective-permute-start.39
  375.2 6.1 %collective-permute-done.33.other_ref = bf16[288,768]{1,0:T(8,128)(2,1)S(1)} collective-permute-done((bf16[288,768]{1,0:T(8,128)(2,1)}, bf16[288,768]{1,0:T(8,128)(2,1)S(1)}, u32[]{:S(2)}, u32[]{:S(2)}) %collective-permute-start.33) | collective-permute-done | bytes 442400 | tf_op jit(solution)/shard_map/ppermute | solution.py:673
  381.3 7.1 %collective-permute-done.34.home_other_ref = bf16[288,768]{1,0:T(8,128)(2,1)S(1)} collective-permute-done((bf16[288,768]{1,0:T(8,128)(2,1)}, bf16[288,768]{1,0:T(8,128)(2,1)S(1)}, u32[]{:S(2)}, u32[]{:S(2)}) %collective-permute-start.34) | collective-permute-done | bytes 442400 | tf_op jit(solution)/shard_map/ppermute | solution.py:673
  393.3 2.0 reshape.247
  397.9 3.9 assemble.3
  401.8 4.6 %collective-permute-done.41 = bf16[48,3456]{1,0:T(8,128)(2,1)S(1)} collective-permute-done((bf16[48,3456]{1,0:T(8,128)(2,1)S(1)}, bf16[48,3456]{1,0:T(8,128)(2,1)S(1)}, u32[]{:S(2)}, u32[]{:S(2)}) %collective-permute-start.41) | collective-permute-done | bytes 331808 | tf_op jit(solution)/shard_map/ppermute | solution.py:673
  (277 shorter events, 58.4 us)
Async XLA Ops:
  7.2 101.5 %copy-start = (bf16[2,576,768]{2,1,0:T(8,128)(2,1)S(1)}, bf16[2,576,768]{2,1,0:T(8,128)(2,1)}, u32[]{:S(2)}) copy-start(bf16[2,576,768]{2,1,0:T(8,128)(2,1)} %param.33) | copy-start | bytes 5308420
  7.2 163.0 %all-gather.3.cloned.1.call-start = ((), (), s32[]{:S(2)}) async-start(), calls=%async_computation.2 | async-start | bytes 10948608 | tf_op jit(solution)/shard_map/all_gather | solution.py:715
  10.7 2.4 collective-permute-start.2
  17.0 7.1 %collective-permute-start.3 = (bf16[112,768]{1,0:T(8,128)(2,1)}, bf16[112,768]{1,0:T(8,128)(2,1)}, u32[]{:S(2)}, u32[]{:S(2)}) collective-permute-start(bf16[112,768]{1,0:T(8,128)(2,1)} %get-tuple-element.88), channel_id=1, source_target_pairs={{0,1},{1,0},{2,3},{3,2},{4,5},{5,4},{6,7},{7,6},{8,9},{9,8},{10,11... | collective-permute-start | bytes 516104 | tf_op jit(solution)/shard_map/ppermute | solution.py:673
  18.7 12.3 %collective-permute-start.1 = (bf16[288,768]{1,0:T(8,128)(2,1)S(1)}, bf16[288,768]{1,0:T(8,128)(2,1)}, u32[]{:S(2)}, u32[]{:S(2)}) collective-permute-start(bf16[288,768]{1,0:T(8,128)(2,1)S(1)} %get-tuple-element.220), channel_id=1, source_target_pairs={{4,8},{5,9},{6,10},{7,11},{8,4},{9,5},{10,6},{11,7},{20,24},{21,25... | collective-permute-start | bytes 1327112 | tf_op jit(solution)/shard_map/ppermute | solution.py:696
  20.2 18.3 %collective-permute-start = (bf16[288,768]{1,0:T(8,128)(2,1)S(1)}, bf16[288,768]{1,0:T(8,128)(2,1)}, u32[]{:S(2)}, u32[]{:S(2)}) collective-permute-start(bf16[288,768]{1,0:T(8,128)(2,1)S(1)} %get-tuple-element.221), channel_id=1, source_target_pairs={{4,0},{5,1},{6,2},{7,3},{8,12},{9,13},{10,14},{11,15},{20,16},{21,... | collective-permute-start | bytes 1327112 | tf_op jit(solution)/shard_map/ppermute | solution.py:696
  25.1 36.7 %copy-start.6 = (bf16[96,576]{1,0:T(8,128)(2,1)}, bf16[96,576]{1,0:T(8,128)(2,1)S(1)}, u32[]{:S(2)}) copy-start(bf16[96,576]{1,0:T(8,128)(2,1)S(1)} %get-tuple-element.226.refs_0_) | copy-start | bytes 331780
  25.2 26.9 %collective-permute-start.6 = (bf16[96,576]{1,0:T(8,128)(2,1)S(1)}, bf16[96,576]{1,0:T(8,128)(2,1)S(1)}, u32[]{:S(2)}, u32[]{:S(2)}) collective-permute-start(bf16[96,576]{1,0:T(8,128)(2,1)S(1)} %get-tuple-element.227), channel_id=1, source_target_pairs={{0,6},{1,7},{2,4},{3,5},{4,2},{5,3},{6,0},{7,1},{8,14},{9,15},{10,... | collective-permute-start | bytes 331784 | tf_op jit(solution)/shard_map/ppermute | solution.py:673
  26.8 25.3 %collective-permute-start.4 = (bf16[96,576]{1,0:T(8,128)(2,1)S(1)}, bf16[96,576]{1,0:T(8,128)(2,1)S(1)}, u32[]{:S(2)}, u32[]{:S(2)}) collective-permute-start(bf16[96,576]{1,0:T(8,128)(2,1)S(1)} %get-tuple-element.227), channel_id=1, source_target_pairs={{0,2},{1,3},{2,0},{3,1},{4,6},{5,7},{6,4},{7,5},{8,10},{9,11},{10,... | collective-permute-start | bytes 331784 | tf_op jit(solution)/shard_map/ppermute | solution.py:673
  29.3 22.8 %collective-permute-start.5 = (bf16[96,576]{1,0:T(8,128)(2,1)S(1)}, bf16[96,576]{1,0:T(8,128)(2,1)S(1)}, u32[]{:S(2)}, u32[]{:S(2)}) collective-permute-start(bf16[96,576]{1,0:T(8,128)(2,1)S(1)} %get-tuple-element.226.refs_0_), channel_id=1, source_target_pairs={{0,4},{1,5},{2,6},{3,7},{4,0},{5,1},{6,2},{7,3},{8,12},{9,13},{10,... | collective-permute-start | bytes 331784 | tf_op jit(solution)/shard_map/ppermute | solution.py:673
  56.4 337.0 %reduce-scatter.2.cloned.1.call-start = ((), (), s32[]{:S(2)}) async-start(), calls=%async_computation.1 | async-start | bytes 11280384 | tf_op jit(solution)/shard_map/reduce_scatter | solution.py:774
  58.9 17.3 %collective-permute-start.12 = (bf16[288,768]{1,0:T(8,128)(2,1)S(1)}, bf16[288,768]{1,0:T(8,128)(2,1)}, u32[]{:S(2)}, u32[]{:S(2)}) collective-permute-start(bf16[288,768]{1,0:T(8,128)(2,1)S(1)} %copy-done.41), channel_id=1, source_target_pairs={{0,2},{1,3},{2,0},{3,1},{4,6},{5,7},{6,4},{7,5},{8,10},{9,11},{10,... | collective-permute-start | bytes 1327112 | tf_op jit(solution)/shard_map/ppermute | solution.py:673
  61.0 30.4 %collective-permute-start.11 = (bf16[288,768]{1,0:T(8,128)(2,1)S(1)}, bf16[288,768]{1,0:T(8,128)(2,1)}, u32[]{:S(2)}, u32[]{:S(2)}) collective-permute-start(bf16[288,768]{1,0:T(8,128)(2,1)S(1)} %copy-done.41), channel_id=1, source_target_pairs={{0,8},{1,9},{2,10},{3,11},{4,12},{5,13},{6,14},{7,15},{8,0},{9,1},... | collective-permute-start | bytes 1327112 | tf_op jit(solution)/shard_map/ppermute | solution.py:673
  62.9 25.2 %collective-permute-start.10 = (bf16[384,576]{1,0:T(8,128)(2,1)S(1)}, bf16[384,576]{1,0:T(8,128)(2,1)S(1)}, u32[]{:S(2)}, u32[]{:S(2)}) collective-permute-start(bf16[384,576]{1,0:T(8,128)(2,1)S(1)} %pad_maximum_fusion.2), channel_id=1, source_target_pairs={{0,16},{1,17},{2,18},{3,19},{4,20},{5,21},{6,22},{7,23},{8,24},{9,... | collective-permute-start | bytes 1327112 | tf_op jit(solution)/shard_map/ppermute | solution.py:673
  64.5 23.6 %collective-permute-start.8 = (bf16[288,768]{1,0:T(8,128)(2,1)}, bf16[288,768]{1,0:T(8,128)(2,1)}, u32[]{:S(2)}, u32[]{:S(2)}) collective-permute-start(bf16[288,768]{1,0:T(8,128)(2,1)} %get-tuple-element.90.refs_0_), channel_id=1, source_target_pairs={{0,2},{1,3},{2,0},{3,1},{4,6},{5,7},{6,4},{7,5},{8,10},{9,11},{10,... | collective-permute-start | bytes 1327112 | tf_op jit(solution)/shard_map/ppermute | solution.py:673
  76.2 15.2 %collective-permute-start.13 = (bf16[288,768]{1,0:T(8,128)(2,1)}, bf16[288,768]{1,0:T(8,128)(2,1)S(1)}, u32[]{:S(2)}, u32[]{:S(2)}) collective-permute-start(bf16[288,768]{1,0:T(8,128)(2,1)} %collective-permute-done.12.refs_2_), channel_id=1, source_target_pairs={{0,8},{1,9},{2,10},{3,11},{4,12},{5,13},{6,14},{7,15},{8,0},{9,1},... | collective-permute-start | bytes 1327112 | tf_op jit(solution)/shard_map/ppermute | solution.py:673
  76.8 23.3 %collective-permute-start.7 = (bf16[288,768]{1,0:T(8,128)(2,1)}, bf16[288,768]{1,0:T(8,128)(2,1)S(1)}, u32[]{:S(2)}, u32[]{:S(2)}) collective-permute-start(bf16[288,768]{1,0:T(8,128)(2,1)} %get-tuple-element.90.refs_0_), channel_id=1, source_target_pairs={{0,8},{1,9},{2,10},{3,11},{4,12},{5,13},{6,14},{7,15},{8,0},{9,1},... | collective-permute-start | bytes 1327112 | tf_op jit(solution)/shard_map/ppermute | solution.py:673
  88.1 12.0 %collective-permute-start.9 = (bf16[288,768]{1,0:T(8,128)(2,1)}, bf16[288,768]{1,0:T(8,128)(2,1)S(1)}, u32[]{:S(2)}, u32[]{:S(2)}) collective-permute-start(bf16[288,768]{1,0:T(8,128)(2,1)} %collective-permute-done.8.refs_2_), channel_id=1, source_target_pairs={{0,8},{1,9},{2,10},{3,11},{4,12},{5,13},{6,14},{7,15},{8,0},{9,1},... | collective-permute-start | bytes 1327112 | tf_op jit(solution)/shard_map/ppermute | solution.py:673
  108.8 1.9 collective-permute-start.14
  111.5 44.7 %collective-permute-start.16 = (bf16[288,768]{1,0:T(8,128)(2,1)S(1)}, bf16[288,768]{1,0:T(8,128)(2,1)S(1)}, u32[]{:S(2)}, u32[]{:S(2)}) collective-permute-start(bf16[288,768]{1,0:T(8,128)(2,1)S(1)} %get-tuple-element.108), channel_id=1, source_target_pairs={{0,4},{1,5},{2,6},{3,7},{4,0},{5,1},{6,2},{7,3},{8,12},{9,13},{10,... | collective-permute-start | bytes 1327112 | tf_op jit(solution)/shard_map/ppermute | solution.py:673
  133.3 33.3 %collective-permute-start.15 = (bf16[1152,192]{0,1:T(8,128)(2,1)S(1)}, bf16[1152,192]{0,1:T(8,128)(2,1)S(1)}, u32[]{:S(2)}, u32[]{:S(2)}) collective-permute-start(bf16[1152,192]{0,1:T(8,128)(2,1)S(1)} %copy.45), channel_id=1, source_target_pairs={{0,2},{1,3},{2,0},{3,1},{4,6},{5,7},{6,4},{7,5},{8,10},{9,11},{10,... | collective-permute-start | bytes 1327112 | tf_op jit(solution)/shard_map/ppermute | solution.py:673
  167.3 1.9 collective-permute-start.17
  196.9 19.5 %collective-permute-start.18 = (bf16[1152,192]{0,1:T(8,128)(2,1)S(1)}, bf16[1152,192]{0,1:T(8,128)(2,1)S(1)}, u32[]{:S(2)}, u32[]{:S(2)}) collective-permute-start(bf16[1152,192]{0,1:T(8,128)(2,1)S(1)} %copy.50), channel_id=1, source_target_pairs={{0,2},{1,3},{2,0},{3,1},{4,6},{5,7},{6,4},{7,5},{8,10},{9,11},{10,... | collective-permute-start | bytes 1327112 | tf_op jit(solution)/shard_map/ppermute | solution.py:673
  219.1 2.5 collective-permute-start.19
  219.8 24.9 %collective-permute-start.20 = (bf16[288,768]{1,0:T(8,128)(2,1)S(1)}, bf16[288,768]{1,0:T(8,128)(2,1)S(1)}, u32[]{:S(2)}, u32[]{:S(2)}) collective-permute-start(bf16[288,768]{1,0:T(8,128)(2,1)S(1)} %copy-done.43), channel_id=1, source_target_pairs={{0,4},{1,5},{2,6},{3,7},{4,0},{5,1},{6,2},{7,3},{8,12},{9,13},{10,... | collective-permute-start | bytes 1327112 | tf_op jit(solution)/shard_map/ppermute | solution.py:673
  220.5 24.2 %collective-permute-start.21 = (bf16[288,768]{1,0:T(8,128)(2,1)S(1)}, bf16[288,768]{1,0:T(8,128)(2,1)S(1)}, u32[]{:S(2)}, u32[]{:S(2)}) collective-permute-start(bf16[288,768]{1,0:T(8,128)(2,1)S(1)} %copy-done.9), channel_id=1, source_target_pairs={{0,1},{1,0},{2,3},{3,2},{4,5},{5,4},{6,7},{7,6},{8,9},{9,8},{10,11... | collective-permute-start | bytes 1327112 | tf_op jit(solution)/shard_map/ppermute | solution.py:673
  244.7 46.3 %copy-start.11 = (bf16[288,768]{1,0:T(8,128)(2,1)}, bf16[288,768]{1,0:T(8,128)(2,1)S(1)}, u32[]{:S(2)}) copy-start(bf16[288,768]{1,0:T(8,128)(2,1)S(1)} %collective-permute-done.20.home_ref) | copy-start | bytes 1327108
  244.7 46.3 %copy-start.12 = (bf16[288,768]{1,0:T(8,128)(2,1)}, bf16[288,768]{1,0:T(8,128)(2,1)S(1)}, u32[]{:S(2)}) copy-start(bf16[288,768]{1,0:T(8,128)(2,1)S(1)} %collective-permute-done.21.other_ref) | copy-start | bytes 1327108
  244.7 46.3 %collective-permute-start.22 = (bf16[288,768]{1,0:T(8,128)(2,1)S(1)}, bf16[288,768]{1,0:T(8,128)(2,1)}, u32[]{:S(2)}, u32[]{:S(2)}) collective-permute-start(bf16[288,768]{1,0:T(8,128)(2,1)S(1)} %collective-permute-done.20.home_ref), channel_id=1, source_target_pairs={{0,1},{1,0},{2,3},{3,2},{4,5},{5,4},{6,7},{7,6},{8,9},{9,8},{10,11... | collective-permute-start | bytes 1327112 | tf_op jit(solution)/shard_map/ppermute | solution.py:673
  295.2 4.4 %collective-permute-start.23 = (bf16[2,576,768]{2,1,0:T(8,128)(2,1)}, bf16[2,576,768]{2,1,0:T(8,128)(2,1)S(1)}, u32[]{:S(2)}, u32[]{:S(2)}) collective-permute-start(bf16[2,576,768]{2,1,0:T(8,128)(2,1)} %grad_down.2), channel_id=1, source_target_pairs={{0,8},{1,9},{2,10},{3,11},{4,12},{5,13},{6,14},{7,15},{8,0},{9,1},... | collective-permute-start | bytes 5308424 | tf_op jit(solution)/shard_map/ppermute | solution.py:673
  302.4 21.6 %collective-permute-start.24 = (bf16[288,768]{1,0:T(8,128)(2,1)S(1)}, bf16[288,768]{1,0:T(8,128)(2,1)S(1)}, u32[]{:S(2)}, u32[]{:S(2)}) collective-permute-start(bf16[288,768]{1,0:T(8,128)(2,1)S(1)} %get-tuple-element.219), channel_id=1, source_target_pairs={{0,2},{1,3},{2,0},{3,1},{4,6},{5,7},{6,4},{7,5},{8,10},{9,11},{10,... | collective-permute-start | bytes 1327112 | tf_op jit(solution)/shard_map/ppermute | solution.py:673
  313.8 17.1 %collective-permute-start.26 = (bf16[2,2,2,48,576]{4,3,1,0,2:T(8,128)(2,1)S(1)}, bf16[2,2,2,48,576]{4,3,1,0,2:T(8,128)(2,1)S(1)}, u32[]{:S(2)}, u32[]{:S(2)}) collective-permute-start(bf16[2,2,2,48,576]{4,3,1,0,2:T(8,128)(2,1)S(1)} %bitcast.144), channel_id=1, source_target_pairs={{0,16},{1,17},{2,18},{3,19},{4,20},{5,21},{6,22},{7,23},{8,24},{9,... | collective-permute-start | bytes 1327112 | tf_op jit(solution)/shard_map/ppermute | solution.py:673
  315.5 46.0 %collective-permute-start.32 = (bf16[288,768]{1,0:T(8,128)(2,1)S(1)}, bf16[288,768]{1,0:T(8,128)(2,1)}, u32[]{:S(2)}, u32[]{:S(2)}) collective-permute-start(bf16[288,768]{1,0:T(8,128)(2,1)S(1)} %get-tuple-element.218), channel_id=1, source_target_pairs={{0,2},{1,3},{2,0},{3,1},{4,6},{5,7},{6,4},{7,5},{8,10},{9,11},{10,... | collective-permute-start | bytes 1327112 | tf_op jit(solution)/shard_map/ppermute | solution.py:673
  328.7 29.3 %collective-permute-start.25 = (bf16[288,768]{1,0:T(8,128)(2,1)}, bf16[288,768]{1,0:T(8,128)(2,1)}, u32[]{:S(2)}, u32[]{:S(2)}) collective-permute-start(bf16[288,768]{1,0:T(8,128)(2,1)} %finish.2.refs_0_), channel_id=1, source_target_pairs={{0,4},{1,5},{2,6},{3,7},{4,0},{5,1},{6,2},{7,3},{8,12},{9,13},{10,... | collective-permute-start | bytes 1327112 | tf_op jit(solution)/shard_map/ppermute | solution.py:673
  331.6 2.2 collective-permute-start.28
  333.1 11.3 %collective-permute-start.31 = (bf16[2,288,768]{2,1,0:T(8,128)(2,1)S(1)}, bf16[2,288,768]{2,1,0:T(8,128)(2,1)S(1)}, u32[]{:S(2)}, u32[]{:S(2)}) collective-permute-start(bf16[2,288,768]{2,1,0:T(8,128)(2,1)S(1)} %maximum_select_fusion), channel_id=1, source_target_pairs={{0,8},{1,9},{2,10},{3,11},{4,12},{5,13},{6,14},{7,15},{8,0},{9,1},... | collective-permute-start | bytes 2654216 | tf_op jit(solution)/shard_map/ppermute | solution.py:673
  333.8 5.8 %collective-permute-start.29 = (f32[200,128]{1,0:T(8,128)S(1)}, f32[200,128]{1,0:T(8,128)S(1)}, u32[]{:S(2)}, u32[]{:S(2)}) collective-permute-start(f32[200,128]{1,0:T(8,128)S(1)} %bitcast_add_fusion.3), channel_id=1, source_target_pairs={{0,1},{1,0},{2,3},{3,2},{4,5},{5,4},{6,7},{7,6},{8,9},{9,8},{10,11... | collective-permute-start | bytes 307208 | tf_op jit(solution)/shard_map/ppermute | solution.py:673
  334.7 9.3 %collective-permute-start.27 = (bf16[2,2,48,576]{3,2,1,0:T(8,128)(2,1)S(1)}, bf16[2,2,48,576]{3,2,1,0:T(8,128)(2,1)S(1)}, u32[]{:S(2)}, u32[]{:S(2)}) collective-permute-start(bf16[2,2,48,576]{3,2,1,0:T(8,128)(2,1)S(1)} %fusion.1), channel_id=1, source_target_pairs={{0,1},{1,0},{2,3},{3,2},{4,5},{5,4},{6,7},{7,6},{8,9},{9,8},{10,11... | collective-permute-start | bytes 663560 | tf_op jit(solution)/shard_map/ppermute | solution.py:673
  339.7 4.7 %collective-permute-start.30 = (f32[200,128]{1,0:T(8,128)S(1)}, f32[200,128]{1,0:T(8,128)S(1)}, u32[]{:S(2)}, u32[]{:S(2)}) collective-permute-start(f32[200,128]{1,0:T(8,128)S(1)} %fusion.20), channel_id=1, source_target_pairs={{0,16},{1,17},{2,18},{3,19},{4,20},{5,21},{6,22},{7,23},{8,24},{9,... | collective-permute-start | bytes 307208 | tf_op jit(solution)/shard_map/ppermute | solution.py:673
  358.0 9.3 %collective-permute-start.36 = (f32[200,128]{1,0:T(8,128)S(1)}, f32[200,128]{1,0:T(8,128)S(1)}, u32[]{:S(2)}, u32[]{:S(2)}) collective-permute-start(f32[200,128]{1,0:T(8,128)S(1)} %add.268), channel_id=1, source_target_pairs={{0,2},{1,3},{2,0},{3,1},{4,6},{5,7},{6,4},{7,5},{8,10},{9,11},{10,... | collective-permute-start | bytes 307208 | tf_op jit(solution)/shard_map/ppermute | solution.py:673
  361.5 8.9 %collective-permute-start.38 = (bf16[2,48,576]{2,1,0:T(8,128)(2,1)S(1)}, bf16[2,48,576]{2,1,0:T(8,128)(2,1)S(1)}, u32[]{:S(2)}, u32[]{:S(2)}) collective-permute-start(bf16[2,48,576]{2,1,0:T(8,128)(2,1)S(1)} %fusion.7), channel_id=1, source_target_pairs={{0,4},{1,5},{2,6},{3,7},{4,0},{5,1},{6,2},{7,3},{8,12},{9,13},{10,... | collective-permute-start | bytes 331784 | tf_op jit(solution)/shard_map/ppermute | solution.py:673
  365.3 15.9 %collective-permute-start.33 = (bf16[288,768]{1,0:T(8,128)(2,1)}, bf16[288,768]{1,0:T(8,128)(2,1)S(1)}, u32[]{:S(2)}, u32[]{:S(2)}) collective-permute-start(bf16[288,768]{1,0:T(8,128)(2,1)} %finish.3.own_ref), channel_id=1, source_target_pairs={{0,1},{1,0},{2,3},{3,2},{4,5},{5,4},{6,7},{7,6},{8,9},{9,8},{10,11... | collective-permute-start | bytes 1327112 | tf_op jit(solution)/shard_map/ppermute | solution.py:673
  366.4 21.9 %collective-permute-start.34 = (bf16[288,768]{1,0:T(8,128)(2,1)}, bf16[288,768]{1,0:T(8,128)(2,1)S(1)}, u32[]{:S(2)}, u32[]{:S(2)}) collective-permute-start(bf16[288,768]{1,0:T(8,128)(2,1)} %collective-permute-done.25.home_ref), channel_id=1, source_target_pairs={{0,1},{1,0},{2,3},{3,2},{4,5},{5,4},{6,7},{7,6},{8,9},{9,8},{10,11... | collective-permute-start | bytes 1327112 | tf_op jit(solution)/shard_map/ppermute | solution.py:673
  367.4 6.4 %collective-permute-start.37 = (f32[200,128]{1,0:T(8,128)S(1)}, f32[200,128]{1,0:T(8,128)S(1)}, u32[]{:S(2)}, u32[]{:S(2)}) collective-permute-start(f32[200,128]{1,0:T(8,128)S(1)} %add.269), channel_id=1, source_target_pairs={{0,4},{1,5},{2,6},{3,7},{4,0},{5,1},{6,2},{7,3},{8,12},{9,13},{10,... | collective-permute-start | bytes 307208 | tf_op jit(solution)/shard_map/ppermute | solution.py:673
  370.4 19.4 %collective-permute-start.39 = (bf16[2,48,576]{2,1,0:T(8,128)(2,1)S(1)}, bf16[2,48,576]{2,1,0:T(8,128)(2,1)S(1)}, u32[]{:S(2)}, u32[]{:S(2)}) collective-permute-start(bf16[2,48,576]{2,1,0:T(8,128)(2,1)S(1)} %fusion.2), channel_id=1, source_target_pairs={{0,0},{1,2},{2,1},{3,3},{4,4},{5,6},{6,5},{7,7},{8,8},{9,10},{10,9... | collective-permute-start | bytes 331784 | tf_op jit(solution)/shard_map/ppermute | solution.py:673
  389.7 8.2 %collective-permute-start.35 = (bf16[2,288,768]{2,1,0:T(8,128)(2,1)S(1)}, bf16[2,288,768]{2,1,0:T(8,128)(2,1)}, u32[]{:S(2)}, u32[]{:S(2)}) collective-permute-start(bf16[2,288,768]{2,1,0:T(8,128)(2,1)S(1)} %maximum_select_fusion.1), channel_id=1, source_target_pairs={{0,8},{1,9},{2,10},{3,11},{4,12},{5,13},{6,14},{7,15},{8,0},{9,1},... | collective-permute-start | bytes 2654216 | tf_op jit(solution)/shard_map/ppermute | solution.py:673
  389.8 3.2 collective-permute-start.40
  396.6 9.8 %collective-permute-start.41 = (bf16[48,3456]{1,0:T(8,128)(2,1)S(1)}, bf16[48,3456]{1,0:T(8,128)(2,1)S(1)}, u32[]{:S(2)}, u32[]{:S(2)}) collective-permute-start(bf16[48,3456]{1,0:T(8,128)(2,1)S(1)} %bitcast.152), channel_id=1, source_target_pairs={{0,1},{1,0},{2,3},{3,2},{4,5},{5,4},{6,7},{7,6},{8,9},{9,8},{10,11... | collective-permute-start | bytes 995336 | tf_op jit(solution)/shard_map/ppermute | solution.py:673
  (44 other events, 254.4 us)
Sparse Core Ops, SparseCore 0:
  56.5 107.4 all-gather.2
  216.5 139.0 reduce-scatter.1

commit v4 on v3

--- a/solution.py
+++ b/solution.py
@@ -22,7 +22,7 @@
 TN = (((0,), (0,)), ((), ()))
 LH, LW = 64, 112
 ANY = pl.BlockSpec(memory_space=pl.ANY)
-PEAK = 1.0e15
+PEAK = 5.0e15
 
 
 def mm(a, b, dims=NN):
@@ -598,7 +598,7 @@
     part, d = src.shape
     first = pl.BlockSpec((1, part, d), lambda i, o: (0, group, 0))
     return call(
-        finish_kernel, "finish", 2, (1,), at, [kept, got, passed, middle, src, gain, *after],
+        finish_kernel, "finish", 0.1, (1,), at, [kept, got, passed, middle, src, gain, *after],
         [first, first, whole((part, d)), pl.BlockSpec((part, d), lambda i, o: (group, 0)), whole((part, d)), whole(gain.shape)] + [ANY] * len(after),
         struct((part, d)), whole((part, d)),
     )
@@ -619,7 +619,7 @@
     part, d = own.shape
     ins = [own, own_other, home, home_other, got]
     return call(
-        assemble_kernel, "assemble", 3, (1,), place, ins, [whole(v.shape) for v in ins],
+        assemble_kernel, "assemble", 0.1, (1,), place, ins, [whole(v.shape) for v in ins],
         struct((2, 2 * part, d)), whole((2, 2 * part, d)),
     )
 
@@ -772,8 +772,6 @@
     back_core = core(jnp.concatenate([back[1], back_beside[rows:]], axis=0))
     back = [back[0], back_beside, back_core]
     big = lax.psum_scatter(big.reshape(d, -1), ("fsdp", "ctx"), scatter_dimension=0, tiled=True)
-    big = big.reshape(depth, nt, -1)
-    big = f(pick(big, t, 1)) + f(tpswap(pick(big, 1 - t, 1)))
 
     def give_back(own, own_other, home, home_other):
         a = jnp.stack([own, own_other])
@@ -804,8 +802,7 @@
     wg_x = xswap(pick(wg, 1 - x))
     tables = (a_tables + b_tables)[:, :HD] * HD ** 0.5
     home = zswap(grad1, 2)
-    grad0 = finish(place, kept, got, passed0, middle_grad, near, gain1, 0, [grad1])
-    grad_other = tpswap(grad0)
+
 
     def cut(v, sizes):
         at, out = 0, []
@@ -820,8 +817,8 @@
     qv = jnp.stack([jnp.concatenate([sums[i:i + 128], sums[j:j + 64]]) for i, j in ((0, 384), (256, 512))])
     qv = jnp.where(jnp.arange(sets)[:, None, None] == me, qv[None], 0.0).transpose(1, 0, 2).reshape(-1)
     small = jnp.concatenate(
-        [vec_grads.reshape(-1), up_bias_grad.reshape(-1), ng[:, 0], ng[:, 1], qv, tables.reshape(-1)]
-    ).reshape(-1, 128)
+        [v.reshape(-1, 128) for v in (vec_grads, up_bias_grad, ng[:, 0], ng[:, 1], qv, tables)], axis=0
+    )
     for move in (core, tpswap, xswap):
         small = small + move(small)
 
@@ -829,8 +826,12 @@
     wg_low = wg.astype(bf16)
     wg = pick(wg, t, 2) + f(tpswap(pick(wg_low, 1 - t, 2)))
     result = assemble(place, *give_back(*result))
-    grad1_, home, wg, small, result = tied(grad1_, home, wg, small, result)
-    input_grad = assemble(place, *give_back(grad0, grad_other, home, tpswap(home)))
+    grad0 = finish(place, kept, got, passed0, middle_grad, near, gain1, 0, [grad1, small, result])
+    near_other = tpswap(grad0)
+    grad1_, home, wg, small, result, grad0_, big = tied(grad1_, home, wg, small, result, grad0, big)
+    big = big.reshape(depth, nt, -1)
+    big = f(pick(big, t, 1)) + f(tpswap(pick(big, 1 - t, 1)))
+    input_grad = assemble(place, *give_back(grad0_, near_other, home, tpswap(home)))
     wg_low = wg.astype(bf16)
     wg = pick(wg, zi, 1) + f(zswap(pick(wg_low, 1 - zi, 1), 2))
     wg = wg.astype(bf16)

time: 421 us -> 404 us (0.960)
  waiting for transfers between devices: 99.4 us -> 84.9 us
    ppermute x40, waiting for transfers between devices: 91.9 us -> 80.3 us  [send(): return lax.ppermute(v, AXES, pairs_of(shape, move))]
    ppermute x2, waiting for transfers between devices: 7.45 us -> 0.01 us  [grouped(): lax.ppermute(v, AXES, [p for p in pairs_of(shape, move) if is_far(p[0] //...]
    all_gather x1, waiting for transfers between devices: 0.01 us -> 4.61 us  [grouped(): lax.all_gather(own_w, AXES, axis=0, tiled=False)]
    unnamed x110 -> x119, local copies, waits for them, and re-layouts: 12.4 us -> 9.46 us
  transfers between devices with their start and end apart: 44 -> 44, of which waited for: 17 -> 16; matrix products, arithmetic and copies ran while one was open for 8% -> 10% of each run, Pallas kernels for 42% -> 44%
where the time goes in v4:
time: 404 us; the launch traced here: 398 us
  Pallas kernels  208 us (51%)
  waiting for transfers between devices  84.9 us (21%)
  starting transfers between devices  40.8 us (10%)
  local copies, waits for them, and re-layouts  31.6 us (8%)
  other arithmetic  17 us (4%)
  between operations  15.3 us (4%)
    pallas_call x19, Pallas kernels, call(): pl.pallas_call(kernel, out_shape=outs, grid_spec=pltpu.PrefetchScalarGrid...  208 us
    ppermute x40, waiting for transfers between devices, send(): return lax.ppermute(v, AXES, pairs_of(shape, move))  80.3 us
    ppermute x40, starting transfers between devices, send(): return lax.ppermute(v, AXES, pairs_of(shape, move))  38 us
    unnamed x119, local copies, waits for them, and re-layouts  9.46 us
  transfers between devices with their start and end apart: 44, of which 16 were waited for; matrix products, arithmetic and copies ran while one was open for 10% of the time, Pallas kernels for 44%

profile of v4, /device:TPU:8, one launch (start us, length us, event | category | flops | bytes accessed | tf_op | source)
XLA Modules:
  0.0 397.8 jit_solution(14125301170224782329)
XLA Ops:
  7.9 2.8 pack.1
  10.9 1.4 collective-permute-start.1
  16.0 3.2 route.1
  19.2 1.5 collective-permute-start.3
  25.9 3.0 collective-permute-start.6
  28.9 2.8 collective-permute-start.4
  31.9 12.2 %collective-permute-done.6.refs_2_.refs_3_ = bf16[96,576]{1,0:T(8,128)(2,1)S(1)} collective-permute-done((bf16[96,576]{1,0:T(8,128)(2,1)S(1)}, bf16[96,576]{1,0:T(8,128)(2,1)S(1)}, u32[]{:S(2)}, u32[]{:S(2)}) %collective-permute-start.6) | collective-permute-done | bytes 110624 | tf_op jit(solution)/shard_map/ppermute | solution.py:673
  44.3 2.0 collective-permute-start.10
  46.3 2.9 take_far.1
  49.2 2.7 collective-permute-start.8
  52.7 4.7 %collective-permute-done.12.refs_2_ = bf16[288,768]{1,0:T(8,128)(2,1)} collective-permute-done((bf16[288,768]{1,0:T(8,128)(2,1)}, bf16[288,768]{1,0:T(8,128)(2,1)}, u32[]{:S(2)}, u32[]{:S(2)}) %collective-permute-start.12) | collective-permute-done | bytes 442400 | tf_op jit(solution)/shard_map/ppermute | solution.py:673
  57.4 12.7 %collective-permute-done.8.refs_2_ = bf16[288,768]{1,0:T(8,128)(2,1)S(1)} collective-permute-done((bf16[288,768]{1,0:T(8,128)(2,1)}, bf16[288,768]{1,0:T(8,128)(2,1)S(1)}, u32[]{:S(2)}, u32[]{:S(2)}) %collective-permute-start.8) | collective-permute-done | bytes 442400 | tf_op jit(solution)/shard_map/ppermute | solution.py:673
  70.2 2.5 arrange.1.refs_4_.w_ref
  73.5 7.8 %prep.2 = (bf16[3,2304,256]{2,1,0:T(8,128)(2,1)}, bf16[3,2304,256]{2,1,0:T(8,128)(2,1)}, bf16[3,2304,128]{2,1,0:T(8,128)(2,1)}, bf16[2304,768]{1,0:T(8,128)(2,1)}) custom-call(s32[8]{0:T(128)} %stack.191.order_ref, bf16[288,768]{1,0:T(8,128)(2,1)} %get-tuple-element.93.refs_0_, bf16[288,768]{1,0:T(8,128)(2,1)} %collective-permute-done.11.refs_1_, ...), custom_call_target="tpu_custom_call" | custom-call | flops 35000000512 | tf_op jit(solution)/shard_map/prep/pallas_call | solution.py:50
  82.2 7.6 %prep.3 = (bf16[3,2304,256]{2,1,0:T(8,128)(2,1)}, bf16[3,2304,256]{2,1,0:T(8,128)(2,1)}, bf16[3,2304,128]{2,1,0:T(8,128)(2,1)}, bf16[2304,768]{1,0:T(8,128)(2,1)}) custom-call(s32[8]{0:T(128)} %stack.180.order_ref, bf16[288,768]{1,0:T(8,128)(2,1)} %get-tuple-element.92.refs_0_, ...), custom_call_target="tpu_custom_call", output_to_operand_aliasing={{0}: (9, {}), {1}: (10, {}), {2}: (11, {}), {3}: (12, {})} | custom-call | flops 35000000512 | tf_op jit(solution)/shard_map/prep/pallas_call | solution.py:50
  94.1 20.5 %attend.3 = (f32[3,1152,128]{2,1,0:T(8,128)}, bf16[3,1152,256]{2,1,0:T(8,128)(2,1)}, bf16[1152,192]{1,0:T(8,128)(2,1)}) custom-call(s32[1]{0:T(128)} %constant.220.clone.1.order_ref._, bf16[3,2304,256]{2,1,0:T(8,128)(2,1)} %get-tuple-element.101.q_ref, bf16[3,2304,256]{2,1,0:T(8,128)(2,1)} %get-tuple-element.102.k_ref, ...), custom_call_target="tpu_custom_call" | custom-call | flops 95000002560 | tf_op jit(solution)/shard_map/attend/pallas_call | solution.py:50
  116.0 20.5 %attend.2 = (f32[3,1152,128]{2,1,0:T(8,128)}, bf16[3,1152,256]{2,1,0:T(8,128)(2,1)}, bf16[1152,192]{1,0:T(8,128)(2,1)}) custom-call(s32[1]{0:T(128)} %constant.220.clone.1.order_ref._, bf16[3,2304,256]{2,1,0:T(8,128)(2,1)} %get-tuple-element.101.q_ref, bf16[3,2304,256]{2,1,0:T(8,128)(2,1)} %get-tuple-element.102.k_ref, ...), custom_call_target="tpu_custom_call" | custom-call | flops 95000002560 | tf_op jit(solution)/shard_map/attend/pallas_call | solution.py:50
  136.5 13.7 %collective-permute-done.15 = bf16[1152,192]{0,1:T(8,128)(2,1)S(1)} collective-permute-done((bf16[1152,192]{0,1:T(8,128)(2,1)S(1)}, bf16[1152,192]{0,1:T(8,128)(2,1)S(1)}, u32[]{:S(2)}, u32[]{:S(2)}) %collective-permute-start.15) | collective-permute-done | bytes 442400 | tf_op jit(solution)/shard_map/ppermute | solution.py:673
  154.1 4.6 %all-gather.3.cloned.1.call-done = bf16[1536,3456]{1,0:T(8,128)(2,1)} async-done(((bf16[48,3456]{1,0:T(8,128)(2,1)}), bf16[1536,3456]{1,0:T(8,128)(2,1)}) %all-gather.3.cloned.1.call-update) | async-done | bytes 10616848 | tf_op jit(solution)/shard_map/all_gather | solution.py:715
  158.7 25.2 %mlp.1 = (bf16[288,768]{1,0:T(8,128)(2,1)}, bf16[288,768]{1,0:T(8,128)(2,1)}, bf16[576,3072]{1,0:T(8,128)(2,1)}, bf16[576,3072]{1,0:T(8,128)(2,1)}, bf16[576,768...) custom-call(s32[4]{0:T(128)} %pad_add_fusion.1.order_ref, ...), custom_call_target="tpu_custom_call" | custom-call | flops 120000004096 | tf_op jit(solution)/shard_map/mlp/pallas_call | solution.py:50
  186.5 17.0 %wgrad.1 = bf16[16,48,6912]{2,1,0:T(8,128)(2,1)} custom-call(s32[1]{0:T(128)} %constant.220.clone.1.order_ref._, bf16[576,768]{1,0:T(8,128)(2,1)} %get-tuple-element.119.n2_ref, bf16[288,768]{1,0:T(8,128)(2,1)} %get-tuple-element.115.top0, bf16[288,768]{1,0:T(8,128)(2,1)} %collective-permute-done.16.top1, bf16[576,768]{1,0:T(8,128)(2,1)} %get-tuple-element.120.br_ref, ...), custom_call_target="tpu_custom_call" | custom-call | flops 89999998976 | tf_op jit(solution)/shard_map/wgrad/pallas_call | solution.py:50
  209.0 21.3 %attend_back.2 = (bf16[2304,192]{1,0:T(8,128)(2,1)}, f32[256,128]{1,0:T(8,128)}) custom-call(s32[8]{0:T(128)} %stack.192.order_ref, bf16[3,1152,256]{2,1,0:T(8,128)(2,1)} %get-tuple-element.129.qa_ref, bf16[3,1152,256]{2,1,0:T(8,128)(2,1)} %get-tuple-element.130.qb_ref, bf16[3,2304,256]{2,1,0:T(8,128)(2,1)} %get-tuple-element.102.k_ref, ...), custom_call_target="tpu_custom_call" | custom-call | flops 105000001536 | tf_op jit(solution)/shard_map/attend_back/pallas_call | solution.py:50
  231.2 44.8 %attend_back.3 = (bf16[2304,384]{1,0:T(8,128)(2,1)}, f32[256,128]{1,0:T(8,128)}) custom-call(s32[8]{0:T(128)} %stack.192.order_ref, bf16[3,1152,256]{2,1,0:T(8,128)(2,1)} %get-tuple-element.129.qa_ref, bf16[3,1152,256]{2,1,0:T(8,128)(2,1)} %get-tuple-element.130.qb_ref, bf16[3,2304,256]{2,1,0:T(8,128)(2,1)} %get-tuple-element.102.k_ref, ...), custom_call_target="tpu_custom_call" | custom-call | flops 210000003072 | tf_op jit(solution)/shard_map/attend_back/pallas_call | solution.py:50
  276.0 4.2 %grad_down.2 = bf16[2,576,768]{2,1,0:T(8,128)(2,1)} custom-call(s32[1]{0:T(128)} %constant.220.clone.1.order_ref._, bf16[2304,384]{1,0:T(8,128)(2,1)} %get-tuple-element.132.a_ref, bf16[2304,192]{1,0:T(8,128)(2,1)} %get-tuple-element.133.b_ref, bf16[768,640]{1,0:T(8,128)(2,1)} %arrange.1.refs_4_.w_ref), custom_call_target="tpu_custom_call" | custom-call | flops 20000000000 | tf_op jit(solution)/shard_map/grad_down/pallas_call | solution.py:50
  280.2 4.3 %grad_down.3.kept_ref = bf16[2,576,768]{2,1,0:T(8,128)(2,1)} custom-call(s32[1]{0:T(128)} %constant.220.clone.1.order_ref._, bf16[2304,384]{1,0:T(8,128)(2,1)} %get-tuple-element.132.a_ref, bf16[2304,192]{1,0:T(8,128)(2,1)} %get-tuple-element.133.b_ref, bf16[768,640]{1,0:T(8,128)(2,1)} %arrange.1.refs_4_.w_ref), custom_call_target="tpu_custom_call" | custom-call | flops 20000000000 | tf_op jit(solution)/shard_map/grad_down/pallas_call | solution.py:50
  284.5 2.0 fusion
  288.6 8.1 %qkv_grad.1 = (bf16[16,48,576]{2,1,0:T(8,128)(2,1)}, f32[1,576]{1,0:T(1,128)}, f32[768,128]{1,0:T(8,128)}) custom-call(s32[1]{0:T(128)} %constant.220.clone.1.order_ref._, bf16[2304,768]{1,0:T(8,128)(2,1)} %get-tuple-element.139.x_ref, bf16[2304,384]{1,0:T(8,128)(2,1)} %get-tuple-element.132.a_ref, bf16[2304,192]{1,0:T(8,128)(2,1)} %get-tuple-element.133.b_ref, ...), custom_call_target="tpu_custom_call" | custom-call | flops 24999999488 | tf_op jit(solution)/shard_map/qkv_grad/pallas_call | solution.py:50
  300.7 4.3 %finish.2.refs_0_ = bf16[288,768]{1,0:T(8,128)(2,1)} custom-call(s32[4]{0:T(128)} %pad_add_fusion.at_ref._, bf16[2,576,768]{2,1,0:T(8,128)(2,1)} %grad_down.3.kept_ref, bf16[2,576,768]{2,1,0:T(8,128)(2,1)} %copy-done.2, bf16[288,768]{1,0:T(8,128)(2,1)} %copy-done.23, f32[576,768]{1,0:T(8,128)} %get-tuple-element.138.middle_ref, ...), custom_call_target="tpu_custom_call" | custom-call | flops 500000000 | tf_op jit(solution)/shard_map/finish/pallas_call | solution.py:50
  305.0 13.6 %collective-permute-done.26 = bf16[2,2,2,48,576]{4,3,1,0,2:T(8,128)(2,1)S(1)} collective-permute-done((bf16[2,2,2,48,576]{4,3,1,0,2:T(8,128)(2,1)S(1)}, bf16[2,2,2,48,576]{4,3,1,0,2:T(8,128)(2,1)S(1)}, u32[]{:S(2)}, u32[]{:S(2)}) %collective-permute-start.26) | collective-permute-done | bytes 442400 | tf_op jit(solution)/shard_map/ppermute | solution.py:673
  319.4 1.7 collective-permute-start.27
  321.1 2.3 maximum_select_fusion
  325.2 2.2 collective-permute-start.25
  328.1 4.1 %collective-permute-done.29 = f32[200,128]{1,0:T(8,128)S(1)} collective-permute-done((f32[200,128]{1,0:T(8,128)S(1)}, f32[200,128]{1,0:T(8,128)S(1)}, u32[]{:S(2)}, u32[]{:S(2)}) %collective-permute-start.29) | collective-permute-done | bytes 102432 | tf_op jit(solution)/shard_map/ppermute | solution.py:673
  333.0 1.8 bitcast_add_fusion.1
  334.7 2.2 collective-permute-done.30
  338.5 3.7 assemble.2.refs_2_
  342.2 5.0 %collective-permute-done.32.passed_ref = bf16[288,768]{1,0:T(8,128)(2,1)S(1)} collective-permute-done((bf16[288,768]{1,0:T(8,128)(2,1)}, bf16[288,768]{1,0:T(8,128)(2,1)S(1)}, u32[]{:S(2)}, u32[]{:S(2)}) %collective-permute-start.32) | collective-permute-done | bytes 442400 | tf_op jit(solution)/shard_map/ppermute | solution.py:673
  348.0 3.8 finish.3.own_ref
  351.8 1.6 collective-permute-start.33
  353.4 2.4 collective-permute-start.36
  358.2 2.0 reshape.242
  362.2 1.5 collective-permute-start.41
  363.8 2.2 collective-permute-start.37
  366.0 1.9 collective-permute-start.39
  367.9 1.6 collective-permute-done.37
  370.9 2.9 collective-permute-done.39
  378.8 4.7 %collective-permute-done.41 = bf16[48,3456]{1,0:T(8,128)(2,1)} collective-permute-done((bf16[48,3456]{1,0:T(8,128)(2,1)}, bf16[48,3456]{1,0:T(8,128)(2,1)}, u32[]{:S(2)}, u32[]{:S(2)}) %collective-permute-start.41) | collective-permute-done | bytes 331808 | tf_op jit(solution)/shard_map/ppermute | solution.py:673
  386.9 3.7 assemble.3
  (286 shorter events, 57.3 us)
Async XLA Ops:
  7.2 82.7 %copy-start = (bf16[2,576,768]{2,1,0:T(8,128)(2,1)S(1)}, bf16[2,576,768]{2,1,0:T(8,128)(2,1)}, u32[]{:S(2)}) copy-start(bf16[2,576,768]{2,1,0:T(8,128)(2,1)} %param.33) | copy-start | bytes 5308420
  7.2 151.5 %all-gather.3.cloned.1.call-start = ((), (), s32[]{:S(2)}) async-start(), calls=%async_computation.2 | async-start | bytes 10948608 | tf_op jit(solution)/shard_map/all_gather | solution.py:715
  10.7 5.3 %collective-permute-start.2 = (bf16[336,768]{1,0:T(8,128)(2,1)}, bf16[336,768]{1,0:T(8,128)(2,1)}, u32[]{:S(2)}, u32[]{:S(2)}) collective-permute-start(bf16[336,768]{1,0:T(8,128)(2,1)} %pack.1), channel_id=1, source_target_pairs={{0,8},{1,9},{2,10},{3,11},{4,12},{5,13},{6,14},{7,15},{8,0},{9,1},... | collective-permute-start | bytes 1548296 | tf_op jit(solution)/shard_map/ppermute | solution.py:673
  10.9 35.4 %collective-permute-start.1 = (bf16[288,768]{1,0:T(8,128)(2,1)S(1)}, bf16[288,768]{1,0:T(8,128)(2,1)}, u32[]{:S(2)}, u32[]{:S(2)}) collective-permute-start(bf16[288,768]{1,0:T(8,128)(2,1)S(1)} %get-tuple-element.224), channel_id=1, source_target_pairs={{4,8},{5,9},{6,10},{7,11},{8,4},{9,5},{10,6},{11,7},{20,24},{21,25... | collective-permute-start | bytes 1327112 | tf_op jit(solution)/shard_map/ppermute | solution.py:696
  12.3 33.9 %collective-permute-start = (bf16[288,768]{1,0:T(8,128)(2,1)S(1)}, bf16[288,768]{1,0:T(8,128)(2,1)}, u32[]{:S(2)}, u32[]{:S(2)}) collective-permute-start(bf16[288,768]{1,0:T(8,128)(2,1)S(1)} %get-tuple-element.225), channel_id=1, source_target_pairs={{4,0},{5,1},{6,2},{7,3},{8,12},{9,13},{10,14},{11,15},{20,16},{21,... | collective-permute-start | bytes 1327112 | tf_op jit(solution)/shard_map/ppermute | solution.py:696
  19.2 5.6 %collective-permute-start.3 = (bf16[112,768]{1,0:T(8,128)(2,1)}, bf16[112,768]{1,0:T(8,128)(2,1)S(1)}, u32[]{:S(2)}, u32[]{:S(2)}) collective-permute-start(bf16[112,768]{1,0:T(8,128)(2,1)} %get-tuple-element.90), channel_id=1, source_target_pairs={{0,1},{1,0},{2,3},{3,2},{4,5},{5,4},{6,7},{7,6},{8,9},{9,8},{10,11... | collective-permute-start | bytes 516104 | tf_op jit(solution)/shard_map/ppermute | solution.py:673
  25.9 23.4 %copy-start.20 = (bf16[96,576]{1,0:T(8,128)(2,1)}, bf16[96,576]{1,0:T(8,128)(2,1)S(1)}, u32[]{:S(2)}) copy-start(bf16[96,576]{1,0:T(8,128)(2,1)S(1)} %get-tuple-element.230.refs_0_) | copy-start | bytes 331780
  25.9 18.2 %collective-permute-start.6 = (bf16[96,576]{1,0:T(8,128)(2,1)S(1)}, bf16[96,576]{1,0:T(8,128)(2,1)S(1)}, u32[]{:S(2)}, u32[]{:S(2)}) collective-permute-start(bf16[96,576]{1,0:T(8,128)(2,1)S(1)} %get-tuple-element.231), channel_id=1, source_target_pairs={{0,6},{1,7},{2,4},{3,5},{4,2},{5,3},{6,0},{7,1},{8,14},{9,15},{10,... | collective-permute-start | bytes 331784 | tf_op jit(solution)/shard_map/ppermute | solution.py:673
  28.9 15.2 %collective-permute-start.4 = (bf16[96,576]{1,0:T(8,128)(2,1)S(1)}, bf16[96,576]{1,0:T(8,128)(2,1)S(1)}, u32[]{:S(2)}, u32[]{:S(2)}) collective-permute-start(bf16[96,576]{1,0:T(8,128)(2,1)S(1)} %get-tuple-element.231), channel_id=1, source_target_pairs={{0,2},{1,3},{2,0},{3,1},{4,6},{5,7},{6,4},{7,5},{8,10},{9,11},{10,... | collective-permute-start | bytes 331784 | tf_op jit(solution)/shard_map/ppermute | solution.py:673
  31.8 12.4 %collective-permute-start.5 = (bf16[96,576]{1,0:T(8,128)(2,1)S(1)}, bf16[96,576]{1,0:T(8,128)(2,1)S(1)}, u32[]{:S(2)}, u32[]{:S(2)}) collective-permute-start(bf16[96,576]{1,0:T(8,128)(2,1)S(1)} %get-tuple-element.230.refs_0_), channel_id=1, source_target_pairs={{0,4},{1,5},{2,6},{3,7},{4,0},{5,1},{6,2},{7,3},{8,12},{9,13},{10,... | collective-permute-start | bytes 331784 | tf_op jit(solution)/shard_map/ppermute | solution.py:673
  44.1 13.4 %collective-permute-start.12 = (bf16[288,768]{1,0:T(8,128)(2,1)}, bf16[288,768]{1,0:T(8,128)(2,1)}, u32[]{:S(2)}, u32[]{:S(2)}) collective-permute-start(bf16[288,768]{1,0:T(8,128)(2,1)} %get-tuple-element.93.refs_0_), channel_id=1, source_target_pairs={{0,2},{1,3},{2,0},{3,1},{4,6},{5,7},{6,4},{7,5},{8,10},{9,11},{10,... | collective-permute-start | bytes 1327112 | tf_op jit(solution)/shard_map/ppermute | solution.py:673
  44.1 28.6 %collective-permute-start.11 = (bf16[288,768]{1,0:T(8,128)(2,1)}, bf16[288,768]{1,0:T(8,128)(2,1)}, u32[]{:S(2)}, u32[]{:S(2)}) collective-permute-start(bf16[288,768]{1,0:T(8,128)(2,1)} %get-tuple-element.93.refs_0_), channel_id=1, source_target_pairs={{0,8},{1,9},{2,10},{3,11},{4,12},{5,13},{6,14},{7,15},{8,0},{9,1},... | collective-permute-start | bytes 1327112 | tf_op jit(solution)/shard_map/ppermute | solution.py:673
  44.3 25.9 %collective-permute-start.10 = (bf16[384,576]{1,0:T(8,128)(2,1)S(1)}, bf16[384,576]{1,0:T(8,128)(2,1)}, u32[]{:S(2)}, u32[]{:S(2)}) collective-permute-start(bf16[384,576]{1,0:T(8,128)(2,1)S(1)} %pad_maximum_fusion.2), channel_id=1, source_target_pairs={{0,16},{1,17},{2,18},{3,19},{4,20},{5,21},{6,22},{7,23},{8,24},{9,... | collective-permute-start | bytes 1327112 | tf_op jit(solution)/shard_map/ppermute | solution.py:673
  49.2 21.0 %collective-permute-start.8 = (bf16[288,768]{1,0:T(8,128)(2,1)}, bf16[288,768]{1,0:T(8,128)(2,1)S(1)}, u32[]{:S(2)}, u32[]{:S(2)}) collective-permute-start(bf16[288,768]{1,0:T(8,128)(2,1)} %get-tuple-element.92.refs_0_), channel_id=1, source_target_pairs={{0,2},{1,3},{2,0},{3,1},{4,6},{5,7},{6,4},{7,5},{8,10},{9,11},{10,... | collective-permute-start | bytes 1327112 | tf_op jit(solution)/shard_map/ppermute | solution.py:673
  52.6 28.7 %collective-permute-start.7 = (bf16[288,768]{1,0:T(8,128)(2,1)}, bf16[288,768]{1,0:T(8,128)(2,1)S(1)}, u32[]{:S(2)}, u32[]{:S(2)}) collective-permute-start(bf16[288,768]{1,0:T(8,128)(2,1)} %get-tuple-element.92.refs_0_), channel_id=1, source_target_pairs={{0,8},{1,9},{2,10},{3,11},{4,12},{5,13},{6,14},{7,15},{8,0},{9,1},... | collective-permute-start | bytes 1327112 | tf_op jit(solution)/shard_map/ppermute | solution.py:673
  52.7 300.8 %reduce-scatter.2.cloned.1.call-start = ((), (), s32[]{:S(2)}) async-start(), calls=%async_computation.1 | async-start | bytes 11280384 | tf_op jit(solution)/shard_map/reduce_scatter | solution.py:774
  57.4 15.2 %collective-permute-start.13 = (bf16[288,768]{1,0:T(8,128)(2,1)}, bf16[288,768]{1,0:T(8,128)(2,1)S(1)}, u32[]{:S(2)}, u32[]{:S(2)}) collective-permute-start(bf16[288,768]{1,0:T(8,128)(2,1)} %collective-permute-done.12.refs_2_), channel_id=1, source_target_pairs={{0,8},{1,9},{2,10},{3,11},{4,12},{5,13},{6,14},{7,15},{8,0},{9,1},... | collective-permute-start | bytes 1327112 | tf_op jit(solution)/shard_map/ppermute | solution.py:673
  70.2 11.2 %collective-permute-start.9 = (bf16[288,768]{1,0:T(8,128)(2,1)S(1)}, bf16[288,768]{1,0:T(8,128)(2,1)S(1)}, u32[]{:S(2)}, u32[]{:S(2)}) collective-permute-start(bf16[288,768]{1,0:T(8,128)(2,1)S(1)} %collective-permute-done.8.refs_2_), channel_id=1, source_target_pairs={{0,8},{1,9},{2,10},{3,11},{4,12},{5,13},{6,14},{7,15},{8,0},{9,1},... | collective-permute-start | bytes 1327112 | tf_op jit(solution)/shard_map/ppermute | solution.py:673
  90.0 1.9 collective-permute-start.14
  92.9 43.6 %collective-permute-start.16 = (bf16[288,768]{1,0:T(8,128)(2,1)}, bf16[288,768]{1,0:T(8,128)(2,1)}, u32[]{:S(2)}, u32[]{:S(2)}) collective-permute-start(bf16[288,768]{1,0:T(8,128)(2,1)} %get-tuple-element.110), channel_id=1, source_target_pairs={{0,4},{1,5},{2,6},{3,7},{4,0},{5,1},{6,2},{7,3},{8,12},{9,13},{10,... | collective-permute-start | bytes 1327112 | tf_op jit(solution)/shard_map/ppermute | solution.py:673
  115.9 34.3 %collective-permute-start.15 = (bf16[1152,192]{0,1:T(8,128)(2,1)S(1)}, bf16[1152,192]{0,1:T(8,128)(2,1)S(1)}, u32[]{:S(2)}, u32[]{:S(2)}) collective-permute-start(bf16[1152,192]{0,1:T(8,128)(2,1)S(1)} %copy.47), channel_id=1, source_target_pairs={{0,2},{1,3},{2,0},{3,1},{4,6},{5,7},{6,4},{7,5},{8,10},{9,11},{10,... | collective-permute-start | bytes 1327112 | tf_op jit(solution)/shard_map/ppermute | solution.py:673
  150.9 2.1 collective-permute-start.17
  185.3 19.0 %collective-permute-start.18 = (bf16[1152,192]{0,1:T(8,128)(2,1)S(1)}, bf16[1152,192]{0,1:T(8,128)(2,1)S(1)}, u32[]{:S(2)}, u32[]{:S(2)}) collective-permute-start(bf16[1152,192]{0,1:T(8,128)(2,1)S(1)} %copy.52), channel_id=1, source_target_pairs={{0,2},{1,3},{2,0},{3,1},{4,6},{5,7},{6,4},{7,5},{8,10},{9,11},{10,... | collective-permute-start | bytes 1327112 | tf_op jit(solution)/shard_map/ppermute | solution.py:673
  204.9 3.0 collective-permute-start.19
  205.6 24.6 %collective-permute-start.20 = (bf16[288,768]{1,0:T(8,128)(2,1)S(1)}, bf16[288,768]{1,0:T(8,128)(2,1)}, u32[]{:S(2)}, u32[]{:S(2)}) collective-permute-start(bf16[288,768]{1,0:T(8,128)(2,1)S(1)} %copy-done.50), channel_id=1, source_target_pairs={{0,4},{1,5},{2,6},{3,7},{4,0},{5,1},{6,2},{7,3},{8,12},{9,13},{10,... | collective-permute-start | bytes 1327112 | tf_op jit(solution)/shard_map/ppermute | solution.py:673
  206.6 23.6 %collective-permute-start.21 = (bf16[288,768]{1,0:T(8,128)(2,1)S(1)}, bf16[288,768]{1,0:T(8,128)(2,1)S(1)}, u32[]{:S(2)}, u32[]{:S(2)}) collective-permute-start(bf16[288,768]{1,0:T(8,128)(2,1)S(1)} %copy-done.4), channel_id=1, source_target_pairs={{0,1},{1,0},{2,3},{3,2},{4,5},{5,4},{6,7},{7,6},{8,9},{9,8},{10,11... | collective-permute-start | bytes 1327112 | tf_op jit(solution)/shard_map/ppermute | solution.py:673
  230.3 45.7 %copy-start.6 = (bf16[288,768]{1,0:T(8,128)(2,1)}, bf16[288,768]{1,0:T(8,128)(2,1)S(1)}, u32[]{:S(2)}) copy-start(bf16[288,768]{1,0:T(8,128)(2,1)S(1)} %collective-permute-done.21.other_ref) | copy-start | bytes 1327108
  230.3 45.7 %collective-permute-start.22 = (bf16[288,768]{1,0:T(8,128)(2,1)}, bf16[288,768]{1,0:T(8,128)(2,1)}, u32[]{:S(2)}, u32[]{:S(2)}) collective-permute-start(bf16[288,768]{1,0:T(8,128)(2,1)} %collective-permute-done.20.home_ref), channel_id=1, source_target_pairs={{0,1},{1,0},{2,3},{3,2},{4,5},{5,4},{6,7},{7,6},{8,9},{9,8},{10,11... | collective-permute-start | bytes 1327112 | tf_op jit(solution)/shard_map/ppermute | solution.py:673
  280.2 4.3 %collective-permute-start.23 = (bf16[2,576,768]{2,1,0:T(8,128)(2,1)}, bf16[2,576,768]{2,1,0:T(8,128)(2,1)S(1)}, u32[]{:S(2)}, u32[]{:S(2)}) collective-permute-start(bf16[2,576,768]{2,1,0:T(8,128)(2,1)} %grad_down.2), channel_id=1, source_target_pairs={{0,8},{1,9},{2,10},{3,11},{4,12},{5,13},{6,14},{7,15},{8,0},{9,1},... | collective-permute-start | bytes 5308424 | tf_op jit(solution)/shard_map/ppermute | solution.py:673
  287.3 12.6 %collective-permute-start.24 = (bf16[288,768]{1,0:T(8,128)(2,1)S(1)}, bf16[288,768]{1,0:T(8,128)(2,1)S(1)}, u32[]{:S(2)}, u32[]{:S(2)}) collective-permute-start(bf16[288,768]{1,0:T(8,128)(2,1)S(1)} %get-tuple-element.223), channel_id=1, source_target_pairs={{0,2},{1,3},{2,0},{3,1},{4,6},{5,7},{6,4},{7,5},{8,10},{9,11},{10,... | collective-permute-start | bytes 1327112 | tf_op jit(solution)/shard_map/ppermute | solution.py:673
  298.0 20.5 %collective-permute-start.26 = (bf16[2,2,2,48,576]{4,3,1,0,2:T(8,128)(2,1)S(1)}, bf16[2,2,2,48,576]{4,3,1,0,2:T(8,128)(2,1)S(1)}, u32[]{:S(2)}, u32[]{:S(2)}) collective-permute-start(bf16[2,2,2,48,576]{4,3,1,0,2:T(8,128)(2,1)S(1)} %bitcast.148), channel_id=1, source_target_pairs={{0,16},{1,17},{2,18},{3,19},{4,20},{5,21},{6,22},{7,23},{8,24},{9,... | collective-permute-start | bytes 1327112 | tf_op jit(solution)/shard_map/ppermute | solution.py:673
  319.4 13.6 %collective-permute-start.27 = (bf16[2,2,48,576]{3,2,1,0:T(8,128)(2,1)}, bf16[2,2,48,576]{3,2,1,0:T(8,128)(2,1)}, u32[]{:S(2)}, u32[]{:S(2)}) collective-permute-start(bf16[2,2,48,576]{3,2,1,0:T(8,128)(2,1)} %fusion.1), channel_id=1, source_target_pairs={{0,1},{1,0},{2,3},{3,2},{4,5},{5,4},{6,7},{7,6},{8,9},{9,8},{10,11... | collective-permute-start | bytes 663560 | tf_op jit(solution)/shard_map/ppermute | solution.py:673
  323.4 14.1 %collective-permute-start.31 = (bf16[2,288,768]{2,1,0:T(8,128)(2,1)}, bf16[2,288,768]{2,1,0:T(8,128)(2,1)S(1)}, u32[]{:S(2)}, u32[]{:S(2)}) collective-permute-start(bf16[2,288,768]{2,1,0:T(8,128)(2,1)} %maximum_select_fusion), channel_id=1, source_target_pairs={{0,8},{1,9},{2,10},{3,11},{4,12},{5,13},{6,14},{7,15},{8,0},{9,1},... | collective-permute-start | bytes 2654216 | tf_op jit(solution)/shard_map/ppermute | solution.py:673
  324.3 3.1 collective-permute-start.28
  324.9 22.3 %collective-permute-start.32 = (bf16[288,768]{1,0:T(8,128)(2,1)}, bf16[288,768]{1,0:T(8,128)(2,1)S(1)}, u32[]{:S(2)}, u32[]{:S(2)}) collective-permute-start(bf16[288,768]{1,0:T(8,128)(2,1)} %get-tuple-element.222), channel_id=1, source_target_pairs={{0,2},{1,3},{2,0},{3,1},{4,6},{5,7},{6,4},{7,5},{8,10},{9,11},{10,... | collective-permute-start | bytes 1327112 | tf_op jit(solution)/shard_map/ppermute | solution.py:673
  325.2 28.2 %collective-permute-start.25 = (bf16[288,768]{1,0:T(8,128)(2,1)S(1)}, bf16[288,768]{1,0:T(8,128)(2,1)S(1)}, u32[]{:S(2)}, u32[]{:S(2)}) collective-permute-start(bf16[288,768]{1,0:T(8,128)(2,1)S(1)} %copy-done.11), channel_id=1, source_target_pairs={{0,4},{1,5},{2,6},{3,7},{4,0},{5,1},{6,2},{7,3},{8,12},{9,13},{10,... | collective-permute-start | bytes 1327112 | tf_op jit(solution)/shard_map/ppermute | solution.py:673
  327.4 4.7 %collective-permute-start.29 = (f32[200,128]{1,0:T(8,128)S(1)}, f32[200,128]{1,0:T(8,128)S(1)}, u32[]{:S(2)}, u32[]{:S(2)}) collective-permute-start(f32[200,128]{1,0:T(8,128)S(1)} %add.266), channel_id=1, source_target_pairs={{0,1},{1,0},{2,3},{3,2},{4,5},{5,4},{6,7},{7,6},{8,9},{9,8},{10,11... | collective-permute-start | bytes 307208 | tf_op jit(solution)/shard_map/ppermute | solution.py:673
  332.2 4.7 %collective-permute-start.30 = (f32[200,128]{1,0:T(8,128)S(1)}, f32[200,128]{1,0:T(8,128)S(1)}, u32[]{:S(2)}, u32[]{:S(2)}) collective-permute-start(f32[200,128]{1,0:T(8,128)S(1)} %add.267), channel_id=1, source_target_pairs={{0,16},{1,17},{2,18},{3,19},{4,20},{5,21},{6,22},{7,23},{8,24},{9,... | collective-permute-start | bytes 307208 | tf_op jit(solution)/shard_map/ppermute | solution.py:673
  351.8 26.3 %collective-permute-start.33 = (bf16[288,768]{1,0:T(8,128)(2,1)}, bf16[288,768]{1,0:T(8,128)(2,1)S(1)}, u32[]{:S(2)}, u32[]{:S(2)}) collective-permute-start(bf16[288,768]{1,0:T(8,128)(2,1)} %finish.3.own_ref), channel_id=1, source_target_pairs={{0,1},{1,0},{2,3},{3,2},{4,5},{5,4},{6,7},{7,6},{8,9},{9,8},{10,11... | collective-permute-start | bytes 1327112 | tf_op jit(solution)/shard_map/ppermute | solution.py:673
  353.4 24.7 %copy-start.8 = (bf16[288,768]{1,0:T(8,128)(2,1)}, bf16[288,768]{1,0:T(8,128)(2,1)S(1)}, u32[]{:S(2)}) copy-start(bf16[288,768]{1,0:T(8,128)(2,1)S(1)} %collective-permute-done.25.home_ref) | copy-start | bytes 1327108
  353.4 10.3 %collective-permute-start.36 = (f32[200,128]{1,0:T(8,128)S(1)}, f32[200,128]{1,0:T(8,128)S(1)}, u32[]{:S(2)}, u32[]{:S(2)}) collective-permute-start(f32[200,128]{1,0:T(8,128)S(1)} %copy-done.17), channel_id=1, source_target_pairs={{0,2},{1,3},{2,0},{3,1},{4,6},{5,7},{6,4},{7,5},{8,10},{9,11},{10,... | collective-permute-start | bytes 307208 | tf_op jit(solution)/shard_map/ppermute | solution.py:673
  356.8 9.1 %collective-permute-start.38 = (bf16[2,48,576]{2,1,0:T(8,128)(2,1)S(1)}, bf16[2,48,576]{2,1,0:T(8,128)(2,1)S(1)}, u32[]{:S(2)}, u32[]{:S(2)}) collective-permute-start(bf16[2,48,576]{2,1,0:T(8,128)(2,1)S(1)} %fusion.7), channel_id=1, source_target_pairs={{0,4},{1,5},{2,6},{3,7},{4,0},{5,1},{6,2},{7,3},{8,12},{9,13},{10,... | collective-permute-start | bytes 331784 | tf_op jit(solution)/shard_map/ppermute | solution.py:673
  357.7 20.4 %collective-permute-start.34 = (bf16[288,768]{1,0:T(8,128)(2,1)S(1)}, bf16[288,768]{1,0:T(8,128)(2,1)S(1)}, u32[]{:S(2)}, u32[]{:S(2)}) collective-permute-start(bf16[288,768]{1,0:T(8,128)(2,1)S(1)} %collective-permute-done.25.home_ref), channel_id=1, source_target_pairs={{0,1},{1,0},{2,3},{3,2},{4,5},{5,4},{6,7},{7,6},{8,9},{9,8},{10,11... | collective-permute-start | bytes 1327112 | tf_op jit(solution)/shard_map/ppermute | solution.py:673
  362.2 21.2 %collective-permute-start.41 = (bf16[48,3456]{1,0:T(8,128)(2,1)}, bf16[48,3456]{1,0:T(8,128)(2,1)}, u32[]{:S(2)}, u32[]{:S(2)}) collective-permute-start(bf16[48,3456]{1,0:T(8,128)(2,1)} %bitcast.133), channel_id=1, source_target_pairs={{0,1},{1,0},{2,3},{3,2},{4,5},{5,4},{6,7},{7,6},{8,9},{9,8},{10,11... | collective-permute-start | bytes 995336 | tf_op jit(solution)/shard_map/ppermute | solution.py:673
  363.8 5.7 %collective-permute-start.37 = (f32[200,128]{1,0:T(8,128)S(1)}, f32[200,128]{1,0:T(8,128)S(1)}, u32[]{:S(2)}, u32[]{:S(2)}) collective-permute-start(f32[200,128]{1,0:T(8,128)S(1)} %add.269), channel_id=1, source_target_pairs={{0,4},{1,5},{2,6},{3,7},{4,0},{5,1},{6,2},{7,3},{8,12},{9,13},{10,... | collective-permute-start | bytes 307208 | tf_op jit(solution)/shard_map/ppermute | solution.py:673
  366.0 7.8 %collective-permute-start.39 = (bf16[2,48,576]{2,1,0:T(8,128)(2,1)S(1)}, bf16[2,48,576]{2,1,0:T(8,128)(2,1)S(1)}, u32[]{:S(2)}, u32[]{:S(2)}) collective-permute-start(bf16[2,48,576]{2,1,0:T(8,128)(2,1)S(1)} %fusion.2), channel_id=1, source_target_pairs={{0,0},{1,2},{2,1},{3,3},{4,4},{5,6},{6,5},{7,7},{8,8},{9,10},{10,9... | collective-permute-start | bytes 331784 | tf_op jit(solution)/shard_map/ppermute | solution.py:673
  373.8 2.8 collective-permute-start.40
  378.3 7.8 %collective-permute-start.35 = (bf16[2,288,768]{2,1,0:T(8,128)(2,1)S(1)}, bf16[2,288,768]{2,1,0:T(8,128)(2,1)S(1)}, u32[]{:S(2)}, u32[]{:S(2)}) collective-permute-start(bf16[2,288,768]{2,1,0:T(8,128)(2,1)S(1)} %maximum_select_fusion.1), channel_id=1, source_target_pairs={{0,8},{1,9},{2,10},{3,11},{4,12},{5,13},{6,14},{7,15},{8,0},{9,1},... | collective-permute-start | bytes 2654216 | tf_op jit(solution)/shard_map/ppermute | solution.py:673
  (51 other events, 236.8 us)
Sparse Core Ops, SparseCore 0:
  52.8 105.8 all-gather.2
  208.0 124.6 reduce-scatter.1

commit v5 on v4

--- a/solution.py
+++ b/solution.py
@@ -812,7 +812,7 @@
             at += size
         return out
 
-    grad1_, wg_x, tables, sums, ng, result = tied(grad1, wg_x, tables, sums, ng, result)
+    grad1_, tables, sums, ng, result = tied(grad1, tables, sums, ng, result)
     sums = sums[0]
     qv = jnp.stack([jnp.concatenate([sums[i:i + 128], sums[j:j + 64]]) for i, j in ((0, 384), (256, 512))])
     qv = jnp.where(jnp.arange(sets)[:, None, None] == me, qv[None], 0.0).transpose(1, 0, 2).reshape(-1)
@@ -822,10 +822,12 @@
     for move in (core, tpswap, xswap):
         small = small + move(small)
 
+    result = assemble(place, *give_back(*result))
+    wg_x, small, result = tied(wg_x, small, result)
+
     wg = f(pick(wg, x)) + f(wg_x)
     wg_low = wg.astype(bf16)
     wg = pick(wg, t, 2) + f(tpswap(pick(wg_low, 1 - t, 2)))
-    result = assemble(place, *give_back(*result))
     grad0 = finish(place, kept, got, passed0, middle_grad, near, gain1, 0, [grad1, small, result])
     near_other = tpswap(grad0)
     grad1_, home, wg, small, result, grad0_, big = tied(grad1_, home, wg, small, result, grad0, big)

time: 404 us -> 399 us (0.988)
  waiting for transfers between devices: 84.9 us -> 77.1 us
    ppermute x40, waiting for transfers between devices: 80.3 us -> 72.5 us  [send(): return lax.ppermute(v, AXES, pairs_of(shape, move))]
    unnamed x119 -> x123, local copies, waits for them, and re-layouts: 9.46 us -> 9.51 us
  transfers between devices with their start and end apart: 44 -> 44, of which waited for: 16 -> 16; matrix products, arithmetic and copies ran while one was open for 10% -> 10% of each run, Pallas kernels for 44% -> 45%
where the time goes in v5:
time: 399 us; the launch traced here: 392 us
  Pallas kernels  208 us (52%)
  waiting for transfers between devices  77.1 us (19%)
  starting transfers between devices  42.8 us (11%)
  local copies, waits for them, and re-layouts  31.4 us (8%)
  other arithmetic  17.8 us (4%)
  between operations  15.3 us (4%)
    pallas_call x19, Pallas kernels, call(): pl.pallas_call(kernel, out_shape=outs, grid_spec=pltpu.PrefetchScalarGrid...  208 us
    ppermute x40, waiting for transfers between devices, send(): return lax.ppermute(v, AXES, pairs_of(shape, move))  72.5 us
    ppermute x40, starting transfers between devices, send(): return lax.ppermute(v, AXES, pairs_of(shape, move))  40 us
    unnamed x123, local copies, waits for them, and re-layouts  9.51 us
  transfers between devices with their start and end apart: 44, of which 16 were waited for; matrix products, arithmetic and copies ran while one was open for 10% of the time, Pallas kernels for 45%

profile of v5, /device:TPU:8, one launch (start us, length us, event | category | flops | bytes accessed | tf_op | source)
XLA Modules:
  0.0 392.5 jit_solution(7977783127374079513)
XLA Ops:
  7.9 2.8 pack.1
  10.9 1.5 collective-permute-start.1
  12.4 1.3 collective-permute-start
  16.0 3.2 route.1
  19.3 1.5 collective-permute-start.3
  25.9 3.0 collective-permute-start.6
  28.9 2.8 collective-permute-start.4
  31.9 12.2 %collective-permute-done.6.refs_2_.refs_3_ = bf16[96,576]{1,0:T(8,128)(2,1)S(1)} collective-permute-done((bf16[96,576]{1,0:T(8,128)(2,1)S(1)}, bf16[96,576]{1,0:T(8,128)(2,1)S(1)}, u32[]{:S(2)}, u32[]{:S(2)}) %collective-permute-start.6) | collective-permute-done | bytes 110624 | tf_op jit(solution)/shard_map/ppermute | solution.py:673
  44.3 2.0 collective-permute-start.10
  46.3 2.9 take_far.1
  49.2 2.7 collective-permute-start.8
  52.7 4.7 %collective-permute-done.12.refs_2_ = bf16[288,768]{1,0:T(8,128)(2,1)} collective-permute-done((bf16[288,768]{1,0:T(8,128)(2,1)}, bf16[288,768]{1,0:T(8,128)(2,1)}, u32[]{:S(2)}, u32[]{:S(2)}) %collective-permute-start.12) | collective-permute-done | bytes 442400 | tf_op jit(solution)/shard_map/ppermute | solution.py:673
  57.5 12.7 %collective-permute-done.8.refs_2_ = bf16[288,768]{1,0:T(8,128)(2,1)S(1)} collective-permute-done((bf16[288,768]{1,0:T(8,128)(2,1)}, bf16[288,768]{1,0:T(8,128)(2,1)S(1)}, u32[]{:S(2)}, u32[]{:S(2)}) %collective-permute-start.8) | collective-permute-done | bytes 442400 | tf_op jit(solution)/shard_map/ppermute | solution.py:673
  70.2 2.5 arrange.1.refs_4_.w_ref
  73.5 7.9 %prep.2 = (bf16[3,2304,256]{2,1,0:T(8,128)(2,1)}, bf16[3,2304,256]{2,1,0:T(8,128)(2,1)}, bf16[3,2304,128]{2,1,0:T(8,128)(2,1)}, bf16[2304,768]{1,0:T(8,128)(2,1)}) custom-call(s32[8]{0:T(128)} %stack.191.order_ref, bf16[288,768]{1,0:T(8,128)(2,1)} %get-tuple-element.95.refs_0_, bf16[288,768]{1,0:T(8,128)(2,1)} %collective-permute-done.11.refs_1_, ...), custom_call_target="tpu_custom_call" | custom-call | flops 35000000512 | tf_op jit(solution)/shard_map/prep/pallas_call | solution.py:50
  82.2 7.6 %prep.3 = (bf16[3,2304,256]{2,1,0:T(8,128)(2,1)}, bf16[3,2304,256]{2,1,0:T(8,128)(2,1)}, bf16[3,2304,128]{2,1,0:T(8,128)(2,1)}, bf16[2304,768]{1,0:T(8,128)(2,1)}) custom-call(s32[8]{0:T(128)} %stack.180.order_ref, bf16[288,768]{1,0:T(8,128)(2,1)} %get-tuple-element.94.refs_0_, ...), custom_call_target="tpu_custom_call", output_to_operand_aliasing={{0}: (9, {}), {1}: (10, {}), {2}: (11, {}), {3}: (12, {})} | custom-call | flops 35000000512 | tf_op jit(solution)/shard_map/prep/pallas_call | solution.py:50
  94.1 20.5 %attend.3 = (f32[3,1152,128]{2,1,0:T(8,128)}, bf16[3,1152,256]{2,1,0:T(8,128)(2,1)}, bf16[1152,192]{1,0:T(8,128)(2,1)}) custom-call(s32[1]{0:T(128)} %constant.220.clone.1.order_ref._, bf16[3,2304,256]{2,1,0:T(8,128)(2,1)} %get-tuple-element.103.q_ref, bf16[3,2304,256]{2,1,0:T(8,128)(2,1)} %get-tuple-element.104.k_ref, ...), custom_call_target="tpu_custom_call" | custom-call | flops 95000002560 | tf_op jit(solution)/shard_map/attend/pallas_call | solution.py:50
  114.6 1.3 copy.47
  116.0 20.5 %attend.2 = (f32[3,1152,128]{2,1,0:T(8,128)}, bf16[3,1152,256]{2,1,0:T(8,128)(2,1)}, bf16[1152,192]{1,0:T(8,128)(2,1)}) custom-call(s32[1]{0:T(128)} %constant.220.clone.1.order_ref._, bf16[3,2304,256]{2,1,0:T(8,128)(2,1)} %get-tuple-element.103.q_ref, bf16[3,2304,256]{2,1,0:T(8,128)(2,1)} %get-tuple-element.104.k_ref, ...), custom_call_target="tpu_custom_call" | custom-call | flops 95000002560 | tf_op jit(solution)/shard_map/attend/pallas_call | solution.py:50
  136.5 13.7 %collective-permute-done.15 = bf16[1152,192]{0,1:T(8,128)(2,1)S(1)} collective-permute-done((bf16[1152,192]{0,1:T(8,128)(2,1)S(1)}, bf16[1152,192]{0,1:T(8,128)(2,1)S(1)}, u32[]{:S(2)}, u32[]{:S(2)}) %collective-permute-start.15) | collective-permute-done | bytes 442400 | tf_op jit(solution)/shard_map/ppermute | solution.py:673
  154.1 4.6 %all-gather.3.cloned.1.call-done = bf16[1536,3456]{1,0:T(8,128)(2,1)} async-done(((bf16[48,3456]{1,0:T(8,128)(2,1)}), bf16[1536,3456]{1,0:T(8,128)(2,1)}) %all-gather.3.cloned.1.call-update) | async-done | bytes 10616848 | tf_op jit(solution)/shard_map/all_gather | solution.py:715
  158.7 25.2 %mlp.1 = (bf16[288,768]{1,0:T(8,128)(2,1)}, bf16[288,768]{1,0:T(8,128)(2,1)}, bf16[576,3072]{1,0:T(8,128)(2,1)}, bf16[576,3072]{1,0:T(8,128)(2,1)}, bf16[576,768...) custom-call(s32[4]{0:T(128)} %pad_add_fusion.1.order_ref, ...), custom_call_target="tpu_custom_call" | custom-call | flops 120000004096 | tf_op jit(solution)/shard_map/mlp/pallas_call | solution.py:50
  185.3 1.2 collective-permute-start.18
  186.5 16.9 %wgrad.1 = bf16[16,48,6912]{2,1,0:T(8,128)(2,1)} custom-call(s32[1]{0:T(128)} %constant.220.clone.1.order_ref._, bf16[576,768]{1,0:T(8,128)(2,1)} %get-tuple-element.121.n2_ref, bf16[288,768]{1,0:T(8,128)(2,1)} %get-tuple-element.117.top0, bf16[288,768]{1,0:T(8,128)(2,1)} %collective-permute-done.16.top1, bf16[576,768]{1,0:T(8,128)(2,1)} %get-tuple-element.122.br_ref, ...), custom_call_target="tpu_custom_call" | custom-call | flops 89999998976 | tf_op jit(solution)/shard_map/wgrad/pallas_call | solution.py:50
  210.0 21.3 %attend_back.2 = (bf16[2304,192]{1,0:T(8,128)(2,1)}, f32[256,128]{1,0:T(8,128)}) custom-call(s32[8]{0:T(128)} %stack.192.order_ref, bf16[3,1152,256]{2,1,0:T(8,128)(2,1)} %get-tuple-element.131.qa_ref, bf16[3,1152,256]{2,1,0:T(8,128)(2,1)} %get-tuple-element.132.qb_ref, bf16[3,2304,256]{2,1,0:T(8,128)(2,1)} %get-tuple-element.104.k_ref, ...), custom_call_target="tpu_custom_call" | custom-call | flops 105000001536 | tf_op jit(solution)/shard_map/attend_back/pallas_call | solution.py:50
  232.2 44.9 %attend_back.3 = (bf16[2304,384]{1,0:T(8,128)(2,1)}, f32[256,128]{1,0:T(8,128)}) custom-call(s32[8]{0:T(128)} %stack.192.order_ref, bf16[3,1152,256]{2,1,0:T(8,128)(2,1)} %get-tuple-element.131.qa_ref, bf16[3,1152,256]{2,1,0:T(8,128)(2,1)} %get-tuple-element.132.qb_ref, bf16[3,2304,256]{2,1,0:T(8,128)(2,1)} %get-tuple-element.104.k_ref, ...), custom_call_target="tpu_custom_call" | custom-call | flops 210000003072 | tf_op jit(solution)/shard_map/attend_back/pallas_call | solution.py:50
  278.1 4.2 %grad_down.2 = bf16[2,576,768]{2,1,0:T(8,128)(2,1)} custom-call(s32[1]{0:T(128)} %constant.220.clone.1.order_ref._, bf16[2304,384]{1,0:T(8,128)(2,1)} %get-tuple-element.134.a_ref, bf16[2304,192]{1,0:T(8,128)(2,1)} %get-tuple-element.135.b_ref, bf16[768,640]{1,0:T(8,128)(2,1)} %arrange.1.refs_4_.w_ref), custom_call_target="tpu_custom_call" | custom-call | flops 20000000000 | tf_op jit(solution)/shard_map/grad_down/pallas_call | solution.py:50
  282.3 4.3 %grad_down.3.kept_ref = bf16[2,576,768]{2,1,0:T(8,128)(2,1)} custom-call(s32[1]{0:T(128)} %constant.220.clone.1.order_ref._, bf16[2304,384]{1,0:T(8,128)(2,1)} %get-tuple-element.134.a_ref, bf16[2304,192]{1,0:T(8,128)(2,1)} %get-tuple-element.135.b_ref, bf16[768,640]{1,0:T(8,128)(2,1)} %arrange.1.refs_4_.w_ref), custom_call_target="tpu_custom_call" | custom-call | flops 20000000000 | tf_op jit(solution)/shard_map/grad_down/pallas_call | solution.py:50
  286.6 2.1 fusion
  290.6 8.1 %qkv_grad.1 = (bf16[16,48,576]{2,1,0:T(8,128)(2,1)}, f32[1,576]{1,0:T(1,128)}, f32[768,128]{1,0:T(8,128)}) custom-call(s32[1]{0:T(128)} %constant.220.clone.1.order_ref._, bf16[2304,768]{1,0:T(8,128)(2,1)} %get-tuple-element.141.x_ref, bf16[2304,384]{1,0:T(8,128)(2,1)} %get-tuple-element.134.a_ref, bf16[2304,192]{1,0:T(8,128)(2,1)} %get-tuple-element.135.b_ref, ...), custom_call_target="tpu_custom_call" | custom-call | flops 24999999488 | tf_op jit(solution)/shard_map/qkv_grad/pallas_call | solution.py:50
  298.7 1.3 constant_dynamic-slice_fusion.5
  302.9 4.0 %finish.2.refs_0_ = bf16[288,768]{1,0:T(8,128)(2,1)} custom-call(s32[4]{0:T(128)} %pad_add_fusion.at_ref._, bf16[2,576,768]{2,1,0:T(8,128)(2,1)} %grad_down.3.kept_ref, bf16[2,576,768]{2,1,0:T(8,128)(2,1)} %copy-done.2, bf16[288,768]{1,0:T(8,128)(2,1)} %copy-done.24, f32[576,768]{1,0:T(8,128)} %get-tuple-element.140.middle_ref, ...), custom_call_target="tpu_custom_call" | custom-call | flops 500000000 | tf_op jit(solution)/shard_map/finish/pallas_call | solution.py:50
  306.9 1.4 maximum_select_fusion
  310.9 1.3 collective-permute-start.28
  312.3 3.8 collective-permute-done.28
  317.8 5.8 %collective-permute-done.29 = f32[200,128]{1,0:T(8,128)S(1)} collective-permute-done((f32[200,128]{1,0:T(8,128)S(1)}, f32[200,128]{1,0:T(8,128)S(1)}, u32[]{:S(2)}, u32[]{:S(2)}) %collective-permute-start.29) | collective-permute-done | bytes 102432 | tf_op jit(solution)/shard_map/ppermute | solution.py:673
  325.2 3.8 assemble.2.refs_2_
  330.2 1.8 collective-permute-start.31
  333.3 8.5 %collective-permute-done.32.passed_ref = bf16[288,768]{1,0:T(8,128)(2,1)S(1)} collective-permute-done((bf16[288,768]{1,0:T(8,128)(2,1)}, bf16[288,768]{1,0:T(8,128)(2,1)S(1)}, u32[]{:S(2)}, u32[]{:S(2)}) %collective-permute-start.32) | collective-permute-done | bytes 442400 | tf_op jit(solution)/shard_map/ppermute | solution.py:673
  342.5 3.8 finish.3.own_ref
  346.3 2.1 collective-permute-start.33
  349.4 3.3 collective-permute-done.25.home_ref
  352.8 3.4 collective-permute-start.36
  357.3 2.0 reshape.242
  362.4 2.9 collective-permute-start.37
  365.3 2.2 collective-permute-start.39
  369.5 3.7 collective-permute-done.39
  381.7 3.7 assemble.3
  (290 shorter events, 58.5 us)
Async XLA Ops:
  7.2 82.7 %copy-start = (bf16[2,576,768]{2,1,0:T(8,128)(2,1)S(1)}, bf16[2,576,768]{2,1,0:T(8,128)(2,1)}, u32[]{:S(2)}) copy-start(bf16[2,576,768]{2,1,0:T(8,128)(2,1)} %param.33) | copy-start | bytes 5308420
  7.2 151.5 %all-gather.3.cloned.1.call-start = ((), (), s32[]{:S(2)}) async-start(), calls=%async_computation.2 | async-start | bytes 10948608 | tf_op jit(solution)/shard_map/all_gather | solution.py:715
  10.7 5.3 %collective-permute-start.2 = (bf16[336,768]{1,0:T(8,128)(2,1)}, bf16[336,768]{1,0:T(8,128)(2,1)}, u32[]{:S(2)}, u32[]{:S(2)}) collective-permute-start(bf16[336,768]{1,0:T(8,128)(2,1)} %pack.1), channel_id=1, source_target_pairs={{0,8},{1,9},{2,10},{3,11},{4,12},{5,13},{6,14},{7,15},{8,0},{9,1},... | collective-permute-start | bytes 1548296 | tf_op jit(solution)/shard_map/ppermute | solution.py:673
  10.9 35.4 %collective-permute-start.1 = (bf16[288,768]{1,0:T(8,128)(2,1)S(1)}, bf16[288,768]{1,0:T(8,128)(2,1)}, u32[]{:S(2)}, u32[]{:S(2)}) collective-permute-start(bf16[288,768]{1,0:T(8,128)(2,1)S(1)} %get-tuple-element.228), channel_id=1, source_target_pairs={{4,8},{5,9},{6,10},{7,11},{8,4},{9,5},{10,6},{11,7},{20,24},{21,25... | collective-permute-start | bytes 1327112 | tf_op jit(solution)/shard_map/ppermute | solution.py:696
  12.4 33.9 %collective-permute-start = (bf16[288,768]{1,0:T(8,128)(2,1)S(1)}, bf16[288,768]{1,0:T(8,128)(2,1)}, u32[]{:S(2)}, u32[]{:S(2)}) collective-permute-start(bf16[288,768]{1,0:T(8,128)(2,1)S(1)} %get-tuple-element.229), channel_id=1, source_target_pairs={{4,0},{5,1},{6,2},{7,3},{8,12},{9,13},{10,14},{11,15},{20,16},{21,... | collective-permute-start | bytes 1327112 | tf_op jit(solution)/shard_map/ppermute | solution.py:696
  19.3 5.6 %collective-permute-start.3 = (bf16[112,768]{1,0:T(8,128)(2,1)}, bf16[112,768]{1,0:T(8,128)(2,1)S(1)}, u32[]{:S(2)}, u32[]{:S(2)}) collective-permute-start(bf16[112,768]{1,0:T(8,128)(2,1)} %get-tuple-element.92), channel_id=1, source_target_pairs={{0,1},{1,0},{2,3},{3,2},{4,5},{5,4},{6,7},{7,6},{8,9},{9,8},{10,11... | collective-permute-start | bytes 516104 | tf_op jit(solution)/shard_map/ppermute | solution.py:673
  25.9 18.2 %collective-permute-start.6 = (bf16[96,576]{1,0:T(8,128)(2,1)S(1)}, bf16[96,576]{1,0:T(8,128)(2,1)S(1)}, u32[]{:S(2)}, u32[]{:S(2)}) collective-permute-start(bf16[96,576]{1,0:T(8,128)(2,1)S(1)} %get-tuple-element.235), channel_id=1, source_target_pairs={{0,6},{1,7},{2,4},{3,5},{4,2},{5,3},{6,0},{7,1},{8,14},{9,15},{10,... | collective-permute-start | bytes 331784 | tf_op jit(solution)/shard_map/ppermute | solution.py:673
  28.9 15.2 %collective-permute-start.4 = (bf16[96,576]{1,0:T(8,128)(2,1)S(1)}, bf16[96,576]{1,0:T(8,128)(2,1)S(1)}, u32[]{:S(2)}, u32[]{:S(2)}) collective-permute-start(bf16[96,576]{1,0:T(8,128)(2,1)S(1)} %get-tuple-element.235), channel_id=1, source_target_pairs={{0,2},{1,3},{2,0},{3,1},{4,6},{5,7},{6,4},{7,5},{8,10},{9,11},{10,... | collective-permute-start | bytes 331784 | tf_op jit(solution)/shard_map/ppermute | solution.py:673
  31.9 12.3 %collective-permute-start.5 = (bf16[96,576]{1,0:T(8,128)(2,1)S(1)}, bf16[96,576]{1,0:T(8,128)(2,1)S(1)}, u32[]{:S(2)}, u32[]{:S(2)}) collective-permute-start(bf16[96,576]{1,0:T(8,128)(2,1)S(1)} %get-tuple-element.234.refs_0_), channel_id=1, source_target_pairs={{0,4},{1,5},{2,6},{3,7},{4,0},{5,1},{6,2},{7,3},{8,12},{9,13},{10,... | collective-permute-start | bytes 331784 | tf_op jit(solution)/shard_map/ppermute | solution.py:673
  44.1 13.4 %collective-permute-start.12 = (bf16[288,768]{1,0:T(8,128)(2,1)}, bf16[288,768]{1,0:T(8,128)(2,1)}, u32[]{:S(2)}, u32[]{:S(2)}) collective-permute-start(bf16[288,768]{1,0:T(8,128)(2,1)} %get-tuple-element.95.refs_0_), channel_id=1, source_target_pairs={{0,2},{1,3},{2,0},{3,1},{4,6},{5,7},{6,4},{7,5},{8,10},{9,11},{10,... | collective-permute-start | bytes 1327112 | tf_op jit(solution)/shard_map/ppermute | solution.py:673
  44.1 28.6 %collective-permute-start.11 = (bf16[288,768]{1,0:T(8,128)(2,1)}, bf16[288,768]{1,0:T(8,128)(2,1)}, u32[]{:S(2)}, u32[]{:S(2)}) collective-permute-start(bf16[288,768]{1,0:T(8,128)(2,1)} %get-tuple-element.95.refs_0_), channel_id=1, source_target_pairs={{0,8},{1,9},{2,10},{3,11},{4,12},{5,13},{6,14},{7,15},{8,0},{9,1},... | collective-permute-start | bytes 1327112 | tf_op jit(solution)/shard_map/ppermute | solution.py:673
  44.3 25.9 %collective-permute-start.10 = (bf16[384,576]{1,0:T(8,128)(2,1)S(1)}, bf16[384,576]{1,0:T(8,128)(2,1)}, u32[]{:S(2)}, u32[]{:S(2)}) collective-permute-start(bf16[384,576]{1,0:T(8,128)(2,1)S(1)} %pad_maximum_fusion.2), channel_id=1, source_target_pairs={{0,16},{1,17},{2,18},{3,19},{4,20},{5,21},{6,22},{7,23},{8,24},{9,... | collective-permute-start | bytes 1327112 | tf_op jit(solution)/shard_map/ppermute | solution.py:673
  49.2 20.9 %collective-permute-start.8 = (bf16[288,768]{1,0:T(8,128)(2,1)}, bf16[288,768]{1,0:T(8,128)(2,1)S(1)}, u32[]{:S(2)}, u32[]{:S(2)}) collective-permute-start(bf16[288,768]{1,0:T(8,128)(2,1)} %get-tuple-element.94.refs_0_), channel_id=1, source_target_pairs={{0,2},{1,3},{2,0},{3,1},{4,6},{5,7},{6,4},{7,5},{8,10},{9,11},{10,... | collective-permute-start | bytes 1327112 | tf_op jit(solution)/shard_map/ppermute | solution.py:673
  52.7 28.7 %collective-permute-start.7 = (bf16[288,768]{1,0:T(8,128)(2,1)}, bf16[288,768]{1,0:T(8,128)(2,1)S(1)}, u32[]{:S(2)}, u32[]{:S(2)}) collective-permute-start(bf16[288,768]{1,0:T(8,128)(2,1)} %get-tuple-element.94.refs_0_), channel_id=1, source_target_pairs={{0,8},{1,9},{2,10},{3,11},{4,12},{5,13},{6,14},{7,15},{8,0},{9,1},... | collective-permute-start | bytes 1327112 | tf_op jit(solution)/shard_map/ppermute | solution.py:673
  52.7 300.1 %reduce-scatter.2.cloned.1.call-start = ((), (), s32[]{:S(2)}) async-start(), calls=%async_computation.1 | async-start | bytes 11280384 | tf_op jit(solution)/shard_map/reduce_scatter | solution.py:774
  57.5 15.2 %collective-permute-start.13 = (bf16[288,768]{1,0:T(8,128)(2,1)}, bf16[288,768]{1,0:T(8,128)(2,1)S(1)}, u32[]{:S(2)}, u32[]{:S(2)}) collective-permute-start(bf16[288,768]{1,0:T(8,128)(2,1)} %collective-permute-done.12.refs_2_), channel_id=1, source_target_pairs={{0,8},{1,9},{2,10},{3,11},{4,12},{5,13},{6,14},{7,15},{8,0},{9,1},... | collective-permute-start | bytes 1327112 | tf_op jit(solution)/shard_map/ppermute | solution.py:673
  70.2 11.2 %collective-permute-start.9 = (bf16[288,768]{1,0:T(8,128)(2,1)S(1)}, bf16[288,768]{1,0:T(8,128)(2,1)S(1)}, u32[]{:S(2)}, u32[]{:S(2)}) collective-permute-start(bf16[288,768]{1,0:T(8,128)(2,1)S(1)} %collective-permute-done.8.refs_2_), channel_id=1, source_target_pairs={{0,8},{1,9},{2,10},{3,11},{4,12},{5,13},{6,14},{7,15},{8,0},{9,1},... | collective-permute-start | bytes 1327112 | tf_op jit(solution)/shard_map/ppermute | solution.py:673
  90.1 1.9 collective-permute-start.14
  92.9 43.6 %collective-permute-start.16 = (bf16[288,768]{1,0:T(8,128)(2,1)}, bf16[288,768]{1,0:T(8,128)(2,1)}, u32[]{:S(2)}, u32[]{:S(2)}) collective-permute-start(bf16[288,768]{1,0:T(8,128)(2,1)} %get-tuple-element.112), channel_id=1, source_target_pairs={{0,4},{1,5},{2,6},{3,7},{4,0},{5,1},{6,2},{7,3},{8,12},{9,13},{10,... | collective-permute-start | bytes 1327112 | tf_op jit(solution)/shard_map/ppermute | solution.py:673
  115.9 34.3 %collective-permute-start.15 = (bf16[1152,192]{0,1:T(8,128)(2,1)S(1)}, bf16[1152,192]{0,1:T(8,128)(2,1)S(1)}, u32[]{:S(2)}, u32[]{:S(2)}) collective-permute-start(bf16[1152,192]{0,1:T(8,128)(2,1)S(1)} %copy.47), channel_id=1, source_target_pairs={{0,2},{1,3},{2,0},{3,1},{4,6},{5,7},{6,4},{7,5},{8,10},{9,11},{10,... | collective-permute-start | bytes 1327112 | tf_op jit(solution)/shard_map/ppermute | solution.py:673
  150.9 2.1 collective-permute-start.17
  185.3 18.9 %collective-permute-start.18 = (bf16[1152,192]{0,1:T(8,128)(2,1)S(1)}, bf16[1152,192]{0,1:T(8,128)(2,1)S(1)}, u32[]{:S(2)}, u32[]{:S(2)}) collective-permute-start(bf16[1152,192]{0,1:T(8,128)(2,1)S(1)} %copy.52), channel_id=1, source_target_pairs={{0,2},{1,3},{2,0},{3,1},{4,6},{5,7},{6,4},{7,5},{8,10},{9,11},{10,... | collective-permute-start | bytes 1327112 | tf_op jit(solution)/shard_map/ppermute | solution.py:673
  204.8 4.1 %collective-permute-start.19 = (bf16[1152,192]{0,1:T(8,128)(2,1)S(1)}, bf16[1152,192]{0,1:T(8,128)(2,1)S(1)}, u32[]{:S(2)}, u32[]{:S(2)}) collective-permute-start(bf16[1152,192]{0,1:T(8,128)(2,1)S(1)} %copy.54), channel_id=1, source_target_pairs={{0,8},{1,9},{2,10},{3,11},{4,12},{5,13},{6,14},{7,15},{8,0},{9,1},... | collective-permute-start | bytes 1327112 | tf_op jit(solution)/shard_map/ppermute | solution.py:673
  206.7 24.6 %collective-permute-start.20 = (bf16[288,768]{1,0:T(8,128)(2,1)S(1)}, bf16[288,768]{1,0:T(8,128)(2,1)}, u32[]{:S(2)}, u32[]{:S(2)}) collective-permute-start(bf16[288,768]{1,0:T(8,128)(2,1)S(1)} %copy-done.52), channel_id=1, source_target_pairs={{0,4},{1,5},{2,6},{3,7},{4,0},{5,1},{6,2},{7,3},{8,12},{9,13},{10,... | collective-permute-start | bytes 1327112 | tf_op jit(solution)/shard_map/ppermute | solution.py:673
  207.7 23.6 %collective-permute-start.21 = (bf16[288,768]{1,0:T(8,128)(2,1)S(1)}, bf16[288,768]{1,0:T(8,128)(2,1)S(1)}, u32[]{:S(2)}, u32[]{:S(2)}) collective-permute-start(bf16[288,768]{1,0:T(8,128)(2,1)S(1)} %copy-done.4), channel_id=1, source_target_pairs={{0,1},{1,0},{2,3},{3,2},{4,5},{5,4},{6,7},{7,6},{8,9},{9,8},{10,11... | collective-permute-start | bytes 1327112 | tf_op jit(solution)/shard_map/ppermute | solution.py:673
  231.3 45.8 %copy-start.7 = (bf16[288,768]{1,0:T(8,128)(2,1)}, bf16[288,768]{1,0:T(8,128)(2,1)S(1)}, u32[]{:S(2)}) copy-start(bf16[288,768]{1,0:T(8,128)(2,1)S(1)} %collective-permute-done.21.other_ref) | copy-start | bytes 1327108
  231.3 46.8 %collective-permute-start.22 = (bf16[288,768]{1,0:T(8,128)(2,1)}, bf16[288,768]{1,0:T(8,128)(2,1)}, u32[]{:S(2)}, u32[]{:S(2)}) collective-permute-start(bf16[288,768]{1,0:T(8,128)(2,1)} %collective-permute-done.20.home_ref), channel_id=1, source_target_pairs={{0,1},{1,0},{2,3},{3,2},{4,5},{5,4},{6,7},{7,6},{8,9},{9,8},{10,11... | collective-permute-start | bytes 1327112 | tf_op jit(solution)/shard_map/ppermute | solution.py:673
  232.2 44.9 %copy-start.28 = (f32[256,128]{1,0:T(8,128)S(1)}, f32[256,128]{1,0:T(8,128)}, u32[]{:S(2)}) copy-start(f32[256,128]{1,0:T(8,128)} %get-tuple-element.146) | copy-start | bytes 393220
  282.3 4.3 %collective-permute-start.23 = (bf16[2,576,768]{2,1,0:T(8,128)(2,1)}, bf16[2,576,768]{2,1,0:T(8,128)(2,1)S(1)}, u32[]{:S(2)}, u32[]{:S(2)}) collective-permute-start(bf16[2,576,768]{2,1,0:T(8,128)(2,1)} %grad_down.2), channel_id=1, source_target_pairs={{0,8},{1,9},{2,10},{3,11},{4,12},{5,13},{6,14},{7,15},{8,0},{9,1},... | collective-permute-start | bytes 5308424 | tf_op jit(solution)/shard_map/ppermute | solution.py:673
  289.5 12.6 %collective-permute-start.24 = (bf16[288,768]{1,0:T(8,128)(2,1)S(1)}, bf16[288,768]{1,0:T(8,128)(2,1)S(1)}, u32[]{:S(2)}, u32[]{:S(2)}) collective-permute-start(bf16[288,768]{1,0:T(8,128)(2,1)S(1)} %get-tuple-element.227), channel_id=1, source_target_pairs={{0,2},{1,3},{2,0},{3,1},{4,6},{5,7},{6,4},{7,5},{8,10},{9,11},{10,... | collective-permute-start | bytes 1327112 | tf_op jit(solution)/shard_map/ppermute | solution.py:673
  300.8 28.2 %collective-permute-start.26 = (bf16[2,2,2,48,576]{4,3,1,0,2:T(8,128)(2,1)}, bf16[2,2,2,48,576]{4,3,1,0,2:T(8,128)(2,1)}, u32[]{:S(2)}, u32[]{:S(2)}) collective-permute-start(bf16[2,2,2,48,576]{4,3,1,0,2:T(8,128)(2,1)} %bitcast.132), channel_id=1, source_target_pairs={{0,16},{1,17},{2,18},{3,19},{4,20},{5,21},{6,22},{7,23},{8,24},{9,... | collective-permute-start | bytes 1327112 | tf_op jit(solution)/shard_map/ppermute | solution.py:673
  308.3 16.0 %collective-permute-start.30 = (bf16[2,288,768]{2,1,0:T(8,128)(2,1)S(1)}, bf16[2,288,768]{2,1,0:T(8,128)(2,1)S(1)}, u32[]{:S(2)}, u32[]{:S(2)}) collective-permute-start(bf16[2,288,768]{2,1,0:T(8,128)(2,1)S(1)} %maximum_select_fusion), channel_id=1, source_target_pairs={{0,8},{1,9},{2,10},{3,11},{4,12},{5,13},{6,14},{7,15},{8,0},{9,1},... | collective-permute-start | bytes 2654216 | tf_op jit(solution)/shard_map/ppermute | solution.py:673
  309.3 1.6 collective-permute-start.27
  310.9 5.1 %collective-permute-start.28 = (f32[200,128]{1,0:T(8,128)S(1)}, f32[200,128]{1,0:T(8,128)S(1)}, u32[]{:S(2)}, u32[]{:S(2)}) collective-permute-start(f32[200,128]{1,0:T(8,128)S(1)} %add.263), channel_id=1, source_target_pairs={{0,1},{1,0},{2,3},{3,2},{4,5},{5,4},{6,7},{7,6},{8,9},{9,8},{10,11... | collective-permute-start | bytes 307208 | tf_op jit(solution)/shard_map/ppermute | solution.py:673
  316.0 7.6 %collective-permute-start.29 = (f32[200,128]{1,0:T(8,128)S(1)}, f32[200,128]{1,0:T(8,128)S(1)}, u32[]{:S(2)}, u32[]{:S(2)}) collective-permute-start(f32[200,128]{1,0:T(8,128)S(1)} %add.264), channel_id=1, source_target_pairs={{0,16},{1,17},{2,18},{3,19},{4,20},{5,21},{6,22},{7,23},{8,24},{9,... | collective-permute-start | bytes 307208 | tf_op jit(solution)/shard_map/ppermute | solution.py:673
  317.2 24.5 %collective-permute-start.32 = (bf16[288,768]{1,0:T(8,128)(2,1)}, bf16[288,768]{1,0:T(8,128)(2,1)S(1)}, u32[]{:S(2)}, u32[]{:S(2)}) collective-permute-start(bf16[288,768]{1,0:T(8,128)(2,1)} %get-tuple-element.226), channel_id=1, source_target_pairs={{0,2},{1,3},{2,0},{3,1},{4,6},{5,7},{6,4},{7,5},{8,10},{9,11},{10,... | collective-permute-start | bytes 1327112 | tf_op jit(solution)/shard_map/ppermute | solution.py:673
  330.2 18.2 %collective-permute-start.31 = (bf16[2,2,48,576]{3,2,1,0:T(8,128)(2,1)S(1)}, bf16[2,2,48,576]{3,2,1,0:T(8,128)(2,1)}, u32[]{:S(2)}, u32[]{:S(2)}) collective-permute-start(bf16[2,2,48,576]{3,2,1,0:T(8,128)(2,1)S(1)} %fusion.1), channel_id=1, source_target_pairs={{0,1},{1,0},{2,3},{3,2},{4,5},{5,4},{6,7},{7,6},{8,9},{9,8},{10,11... | collective-permute-start | bytes 663560 | tf_op jit(solution)/shard_map/ppermute | solution.py:673
  332.0 20.7 %collective-permute-start.25 = (bf16[288,768]{1,0:T(8,128)(2,1)S(1)}, bf16[288,768]{1,0:T(8,128)(2,1)S(1)}, u32[]{:S(2)}, u32[]{:S(2)}) collective-permute-start(bf16[288,768]{1,0:T(8,128)(2,1)S(1)} %copy-done.11), channel_id=1, source_target_pairs={{0,4},{1,5},{2,6},{3,7},{4,0},{5,1},{6,2},{7,3},{8,12},{9,13},{10,... | collective-permute-start | bytes 1327112 | tf_op jit(solution)/shard_map/ppermute | solution.py:673
  346.3 31.1 %collective-permute-start.33 = (bf16[288,768]{1,0:T(8,128)(2,1)}, bf16[288,768]{1,0:T(8,128)(2,1)S(1)}, u32[]{:S(2)}, u32[]{:S(2)}) collective-permute-start(bf16[288,768]{1,0:T(8,128)(2,1)} %finish.3.own_ref), channel_id=1, source_target_pairs={{0,1},{1,0},{2,3},{3,2},{4,5},{5,4},{6,7},{7,6},{8,9},{9,8},{10,11... | collective-permute-start | bytes 1327112 | tf_op jit(solution)/shard_map/ppermute | solution.py:673
  352.8 24.7 %copy-start.6 = (bf16[288,768]{1,0:T(8,128)(2,1)}, bf16[288,768]{1,0:T(8,128)(2,1)S(1)}, u32[]{:S(2)}) copy-start(bf16[288,768]{1,0:T(8,128)(2,1)S(1)} %collective-permute-done.25.home_ref) | copy-start | bytes 1327108
  352.8 9.6 %collective-permute-start.36 = (f32[200,128]{1,0:T(8,128)S(1)}, f32[200,128]{1,0:T(8,128)S(1)}, u32[]{:S(2)}, u32[]{:S(2)}) collective-permute-start(f32[200,128]{1,0:T(8,128)S(1)} %copy-done.18), channel_id=1, source_target_pairs={{0,2},{1,3},{2,0},{3,1},{4,6},{5,7},{6,4},{7,5},{8,10},{9,11},{10,... | collective-permute-start | bytes 307208 | tf_op jit(solution)/shard_map/ppermute | solution.py:673
  356.2 9.1 %collective-permute-start.38 = (bf16[2,48,576]{2,1,0:T(8,128)(2,1)S(1)}, bf16[2,48,576]{2,1,0:T(8,128)(2,1)S(1)}, u32[]{:S(2)}, u32[]{:S(2)}) collective-permute-start(bf16[2,48,576]{2,1,0:T(8,128)(2,1)S(1)} %fusion.7), channel_id=1, source_target_pairs={{0,4},{1,5},{2,6},{3,7},{4,0},{5,1},{6,2},{7,3},{8,12},{9,13},{10,... | collective-permute-start | bytes 331784 | tf_op jit(solution)/shard_map/ppermute | solution.py:673
  356.3 21.2 %collective-permute-start.34 = (bf16[288,768]{1,0:T(8,128)(2,1)S(1)}, bf16[288,768]{1,0:T(8,128)(2,1)S(1)}, u32[]{:S(2)}, u32[]{:S(2)}) collective-permute-start(bf16[288,768]{1,0:T(8,128)(2,1)S(1)} %collective-permute-done.25.home_ref), channel_id=1, source_target_pairs={{0,1},{1,0},{2,3},{3,2},{4,5},{5,4},{6,7},{7,6},{8,9},{9,8},{10,11... | collective-permute-start | bytes 1327112 | tf_op jit(solution)/shard_map/ppermute | solution.py:673
  361.4 16.8 %collective-permute-start.41 = (bf16[48,3456]{1,0:T(8,128)(2,1)}, bf16[48,3456]{1,0:T(8,128)(2,1)}, u32[]{:S(2)}, u32[]{:S(2)}) collective-permute-start(bf16[48,3456]{1,0:T(8,128)(2,1)} %bitcast.133), channel_id=1, source_target_pairs={{0,1},{1,0},{2,3},{3,2},{4,5},{5,4},{6,7},{7,6},{8,9},{9,8},{10,11... | collective-permute-start | bytes 995336 | tf_op jit(solution)/shard_map/ppermute | solution.py:673
  362.4 5.7 %collective-permute-start.37 = (f32[200,128]{1,0:T(8,128)S(1)}, f32[200,128]{1,0:T(8,128)S(1)}, u32[]{:S(2)}, u32[]{:S(2)}) collective-permute-start(f32[200,128]{1,0:T(8,128)S(1)} %add.269), channel_id=1, source_target_pairs={{0,4},{1,5},{2,6},{3,7},{4,0},{5,1},{6,2},{7,3},{8,12},{9,13},{10,... | collective-permute-start | bytes 307208 | tf_op jit(solution)/shard_map/ppermute | solution.py:673
  365.3 7.8 %collective-permute-start.39 = (bf16[2,48,576]{2,1,0:T(8,128)(2,1)S(1)}, bf16[2,48,576]{2,1,0:T(8,128)(2,1)S(1)}, u32[]{:S(2)}, u32[]{:S(2)}) collective-permute-start(bf16[2,48,576]{2,1,0:T(8,128)(2,1)S(1)} %fusion.2), channel_id=1, source_target_pairs={{0,0},{1,2},{2,1},{3,3},{4,4},{5,6},{6,5},{7,7},{8,8},{9,10},{10,9... | collective-permute-start | bytes 331784 | tf_op jit(solution)/shard_map/ppermute | solution.py:673
  373.1 2.8 collective-permute-start.40
  377.6 3.1 collective-permute-start.35
  (53 other events, 236.6 us)
Sparse Core Ops, SparseCore 0:
  52.8 105.8 all-gather.2
  209.0 132.1 reduce-scatter.1
